TPU v7x, 32 devices: a whole 2x2x4 slice. The times are simulated.
32 devices in a mesh: fsdp: 8 (over y, x, core), tp: 4 (over z).
Axes of the slice: x: 2, y: 2, z: 4, core: 2. Of those that a mesh axis runs over, the one named last changes fastest.
Arguments:
- tokens: bfloat16 [8192, 2048], P(('fsdp', 'tp')), may hold values from -6 to 6
- segment_ids: int32 [8, 1024], P('fsdp'), may hold values from 0 to 3, never falling along the last dimension, each value on 1 to 800 neighbouring positions
- attn_gain: float32 [2, 2048], replicated, may hold values from 0.25 to 1.75
- query_gain: float32 [2, 128], replicated, may hold values from 0.25 to 1.75
- key_gain: float32 [2, 128], replicated, may hold values from 0.25 to 1.75
- query_weight: bfloat16 [2, 2048, 2048], P(None, 'fsdp', 'tp'), may hold values from -0.125 to 0.125
- key_matrix: bfloat16 [2, 2048, 1024], P(None, 'fsdp', 'tp'), may hold values from -0.125 to 0.125
- value_matrix: bfloat16 [2, 2048, 1024], P(None, 'fsdp', 'tp'), may hold values from -0.125 to 0.125
- out_weight: bfloat16 [2, 2048, 2048], P(None, 'tp', 'fsdp'), may hold values from -1 to 1
- mlp_gain: float32 [2, 2048], replicated, may hold values from 0.25 to 1.75
- gate_weight: bfloat16 [2, 2048, 6144], P(None, 'fsdp', 'tp'), may hold values from -0.125 to 0.125
- up_weight: bfloat16 [2, 2048, 6144], P(None, 'fsdp', 'tp'), may hold values from -0.125 to 0.125
- down_weight: bfloat16 [2, 6144, 2048], P(None, 'tp', 'fsdp'), may hold values from -0.078125 to 0.078125
- cotangent: bfloat16 [8192, 2048], P(('fsdp', 'tp')), may hold values from -6 to 6
Outputs:
- result: bfloat16 [8192, 2048], P(('fsdp', 'tp'))
- grad_tokens: float32 [8192, 2048], P(('fsdp', 'tp'))
- grad_attn_gain: float32 [2, 2048], replicated
- grad_query_gain: float32 [2, 128], replicated
- grad_key_gain: float32 [2, 128], replicated
- grad_query_weight: float32 [2, 2048, 2048], P(None, 'fsdp', 'tp')
- grad_key_weight: float32 [2, 2048, 1024], P(None, 'fsdp', 'tp')
- grad_value_weight: float32 [2, 2048, 1024], P(None, 'fsdp', 'tp')
- grad_out_weight: float32 [2, 2048, 2048], P(None, 'tp', 'fsdp')
- grad_mlp_gain: float32 [2, 2048], replicated
- grad_gate_weight: float32 [2, 2048, 6144], P(None, 'fsdp', 'tp')
- grad_up_weight: float32 [2, 2048, 6144], P(None, 'fsdp', 'tp')
- grad_down_weight: float32 [2, 6144, 2048], P(None, 'tp', 'fsdp')
Inputs may be any that keep to these rules, and one draw needn't show every extreme that they name: `segment_ids`: along each sequence the ids never fall; a document (a run of equal ids) has at most 800 tokens, and in each sequence one document has exactly 800.
All inputs are finite; a program needn't handle non-finite values.
Results may differ from a plain program's by a relative error of at most 0.03.
Values may be sent and summed in bfloat16 or wider, within the bound.
No kernel may reach another device: no remote copies, remote signals or barrier semaphores. Data moves between devices by JAX's collectives and lax.ppermute only.
A program may use at most 320 MiB of HBM per device.

v0:
```python
import math

import jax
import jax.numpy as jnp
from jax import lax
from jax.sharding import PartitionSpec as P

EPSILON = 1e-06
ROPE_BASE = 1000000.0


def rms_scale(values, gain_row):
    return (
        values * lax.rsqrt(jnp.mean(values * values, axis=-1, keepdims=True) + EPSILON) * gain_row
    )


def positions_of(segment_row):
    sequence_length = segment_row.shape[0]
    position_index = jnp.arange(sequence_length, dtype=jnp.int32)
    starts = jnp.concatenate([jnp.ones((1,), dtype=jnp.bool_), segment_row[1:] != segment_row[:-1]])
    first_index = lax.cummax(
        jnp.where(starts, position_index, jnp.zeros_like(position_index)), axis=0
    )
    return position_index - first_index


def rope_tables(positions, head_size):
    half_size = head_size // 2
    steps_float = jnp.arange(half_size, dtype=jnp.float32)
    inverse = jnp.exp(steps_float * (-2.0 * math.log(ROPE_BASE) / head_size))
    angles = positions.astype(jnp.float32)[:, None] * inverse[None, :]
    angles = jnp.concatenate([angles, angles], axis=-1)
    return (jnp.cos(angles), jnp.sin(angles))


def rotate(values, cosine_table, sine_table):
    half_size = values.shape[-1] // 2
    turned = jnp.concatenate([-values[..., half_size:], values[..., :half_size]], axis=-1)
    return values * cosine_table[:, None, :] + turned * sine_table[:, None, :]


def head_norm(raw_rows, gain_row, cosine_table, sine_table):
    head_size = gain_row.shape[-1]
    shaped = raw_rows.reshape(raw_rows.shape[0], raw_rows.shape[1] // head_size, head_size)
    return rotate(rms_scale(shaped, gain_row), cosine_table, sine_table)


def swiglu(gate_proj, upward):
    return jax.nn.silu(gate_proj) * upward


def contract_rows(left_side, right_side):
    return lax.dot_general(
        left_side, right_side, (((0,), (0,)), ((), ())), preferred_element_type=jnp.float32
    )


def contract_cols(left_side, right_side):
    return lax.dot_general(
        left_side, right_side, (((1,), (1,)), ((), ())), preferred_element_type=jnp.float32
    )


def spread_rows(rows_low):
    return lax.all_gather(rows_low, "tp", axis=0, tiled=True)


def spread_grads(grad_low):
    return lax.all_gather(grad_low, "tp", axis=0, tiled=True)


def collect_rows(left_side, right_side):
    return lax.psum_scatter(
        jnp.dot(left_side, right_side, preferred_element_type=jnp.float32).astype(jnp.bfloat16),
        "tp",
        scatter_dimension=0,
        tiled=True,
    ).astype(jnp.float32)


def collect_grads(pairs_list):
    running = None
    for left_side, right_side in pairs_list:
        product = contract_cols(left_side, right_side)
        running = product if running is None else running + product
    return lax.psum_scatter(
        running.astype(jnp.bfloat16), "tp", scatter_dimension=0, tiled=True
    ).astype(jnp.float32)


def gather_layer(weight_set, layer_index):
    query_weight, key_matrix, value_matrix, out_weight, gate_weight, up_weight, down_weight = (
        weight_set
    )
    return (
        lax.all_gather(query_weight[layer_index], "fsdp", axis=0, tiled=True),
        lax.all_gather(key_matrix[layer_index], "fsdp", axis=0, tiled=True),
        lax.all_gather(value_matrix[layer_index], "fsdp", axis=0, tiled=True),
        lax.all_gather(out_weight[layer_index], "fsdp", axis=1, tiled=True),
        lax.all_gather(gate_weight[layer_index], "fsdp", axis=0, tiled=True),
        lax.all_gather(up_weight[layer_index], "fsdp", axis=0, tiled=True),
        lax.all_gather(down_weight[layer_index], "fsdp", axis=1, tiled=True),
    )


def score_block(
    query_block, heads_of_key, block_index, block_segment, position_index, segment_row, score_scale
):
    raw_dots = jnp.einsum(
        "qngd,knd->ngqk", query_block, heads_of_key, preferred_element_type=jnp.float32
    )
    allowed = (position_index[None, :] <= block_index[:, None]) & (
        segment_row[None, :] == block_segment[:, None]
    )
    return jnp.where(allowed[None, None], raw_dots * score_scale, -1e30)


def block_layout(heads_of_query, segment_row):
    sequence_length, kv_local, group_width, head_size = heads_of_query.shape
    rows_per_block = min(512, sequence_length)
    number_blocks = sequence_length // rows_per_block
    position_index = jnp.arange(sequence_length, dtype=jnp.int32)
    row_index = position_index.reshape(number_blocks, rows_per_block)
    row_segment = segment_row.reshape(number_blocks, rows_per_block)
    return (number_blocks, rows_per_block, position_index, row_index, row_segment)


def attend(heads_of_query, heads_of_key, heads_of_value, segment_row):
    sequence_length, kv_local, group_width, head_size = heads_of_query.shape
    score_scale = head_size ** (-0.5)
    number_blocks, rows_per_block, position_index, row_index, row_segment = block_layout(
        heads_of_query, segment_row
    )
    blocks_of_query = heads_of_query.reshape(
        number_blocks, rows_per_block, kv_local, group_width, head_size
    )

    def forward_block(inputs):
        query_block, block_index, block_segment = inputs
        scores = score_block(
            query_block,
            heads_of_key,
            block_index,
            block_segment,
            position_index,
            segment_row,
            score_scale,
        )
        top_score = jnp.max(scores, axis=-1, keepdims=True)
        weights = jnp.exp(scores - top_score)
        total_weight = jnp.sum(weights, axis=-1, keepdims=True)
        prob_low = (weights / total_weight).astype(jnp.bfloat16)
        block_out = jnp.einsum(
            "ngqk,knd->qngd", prob_low, heads_of_value, preferred_element_type=jnp.float32
        )
        return (block_out.astype(jnp.bfloat16), (top_score + jnp.log(total_weight))[..., 0])

    outputs, log_totals = lax.map(forward_block, (blocks_of_query, row_index, row_segment))
    return (outputs.reshape(sequence_length, kv_local * group_width * head_size), log_totals)


def attend_back(heads_of_query, heads_of_key, heads_of_value, segment_row, out_grad, log_totals):
    sequence_length, kv_local, group_width, head_size = heads_of_query.shape
    score_scale = head_size ** (-0.5)
    number_blocks, rows_per_block, position_index, row_index, row_segment = block_layout(
        heads_of_query, segment_row
    )
    blocks_of_query = heads_of_query.reshape(
        number_blocks, rows_per_block, kv_local, group_width, head_size
    )
    grad_blocks = out_grad.reshape(number_blocks, rows_per_block, kv_local, group_width, head_size)

    def backward_block(running_grads, inputs):
        key_grad, value_grad = running_grads
        query_block, grad_block, block_total, block_index, block_segment = inputs
        scores = score_block(
            query_block,
            heads_of_key,
            block_index,
            block_segment,
            position_index,
            segment_row,
            score_scale,
        )
        prob_block = jnp.exp(scores - block_total[..., None])
        prob_grad = jnp.einsum(
            "qngd,knd->ngqk", grad_block, heads_of_value, preferred_element_type=jnp.float32
        )
        inner_sum = jnp.sum(prob_block * prob_grad, axis=-1, keepdims=True)
        score_grad = (prob_block * (prob_grad - inner_sum)).astype(jnp.bfloat16)
        query_grad = (
            jnp.einsum(
                "ngqk,knd->qngd", score_grad, heads_of_key, preferred_element_type=jnp.float32
            )
            * score_scale
        )
        key_grad = (
            key_grad
            + jnp.einsum(
                "ngqk,qngd->knd", score_grad, query_block, preferred_element_type=jnp.float32
            )
            * score_scale
        )
        value_grad = value_grad + jnp.einsum(
            "ngqk,qngd->knd",
            prob_block.astype(jnp.bfloat16),
            grad_block,
            preferred_element_type=jnp.float32,
        )
        return ((key_grad, value_grad), query_grad)

    zero_keys = jnp.zeros(heads_of_key.shape, jnp.float32)
    (key_grad, value_grad), query_grad = lax.scan(
        backward_block,
        (zero_keys, zero_keys),
        (blocks_of_query, grad_blocks, log_totals, row_index, row_segment),
    )
    return (
        query_grad.reshape(sequence_length, kv_local * group_width, head_size),
        key_grad,
        value_grad,
    )


def on_device(
    tokens,
    segment_ids,
    attn_gain,
    query_gain,
    key_gain,
    query_weight,
    key_matrix,
    value_matrix,
    out_weight,
    mlp_gain,
    gate_weight,
    up_weight,
    down_weight,
    cotangent,
):
    layer_count = attn_gain.shape[0]
    head_size = query_gain.shape[-1]
    segment_row = segment_ids[0]
    cosine_table, sine_table = rope_tables(positions_of(segment_row), head_size)
    weight_set = (
        query_weight,
        key_matrix,
        value_matrix,
        out_weight,
        gate_weight,
        up_weight,
        down_weight,
    )

    def turn_heads(raw_rows, gain_row):
        return head_norm(raw_rows, gain_row, cosine_table, sine_table)

    residual = tokens.astype(jnp.float32)
    saved_layers = []
    for layer_index in range(layer_count):
        gathered = gather_layer(weight_set, layer_index)
        wide_query, wide_key, wide_value, wide_out, wide_gate, wide_up, wide_down = gathered
        attn_normed, attn_back = jax.vjp(rms_scale, residual, attn_gain[layer_index])
        seq_rows = spread_rows(attn_normed.astype(jnp.bfloat16))
        sequence_length = seq_rows.shape[0]
        query_raw = jnp.dot(seq_rows, wide_query, preferred_element_type=jnp.float32)
        key_raw = jnp.dot(seq_rows, wide_key, preferred_element_type=jnp.float32)
        value_raw = jnp.dot(seq_rows, wide_value, preferred_element_type=jnp.float32)
        query_turned, query_back = jax.vjp(turn_heads, query_raw, query_gain[layer_index])
        key_turned, key_back = jax.vjp(turn_heads, key_raw, key_gain[layer_index])
        kv_local = key_raw.shape[1] // head_size
        heads_of_query = query_turned.astype(jnp.bfloat16).reshape(
            sequence_length, kv_local, -1, head_size
        )
        heads_of_key = key_turned.astype(jnp.bfloat16)
        heads_of_value = value_raw.astype(jnp.bfloat16).reshape(
            sequence_length, kv_local, head_size
        )
        attn_rows, log_totals = attend(heads_of_query, heads_of_key, heads_of_value, segment_row)
        residual_mid = residual + collect_rows(attn_rows, wide_out)
        mlp_normed, mlp_back = jax.vjp(rms_scale, residual_mid, mlp_gain[layer_index])
        mlp_rows = spread_rows(mlp_normed.astype(jnp.bfloat16))
        gate_proj = jnp.dot(mlp_rows, wide_gate, preferred_element_type=jnp.float32)
        upward = jnp.dot(mlp_rows, wide_up, preferred_element_type=jnp.float32)
        hidden_float, swiglu_back = jax.vjp(swiglu, gate_proj, upward)
        hidden = hidden_float.astype(jnp.bfloat16)
        residual = residual_mid + collect_rows(hidden, wide_down)
        saved_layers.append(
            (
                gathered,
                attn_back,
                seq_rows,
                query_back,
                key_back,
                heads_of_query,
                heads_of_key,
                heads_of_value,
                attn_rows,
                log_totals,
                mlp_back,
                mlp_rows,
                swiglu_back,
                hidden,
            )
        )
    result = residual.astype(jnp.bfloat16)
    residual_grad = cotangent.astype(jnp.float32)
    grad_weights = [None] * layer_count
    gain_grads = [None] * layer_count
    for layer_index in reversed(range(layer_count)):
        (
            gathered,
            attn_back,
            seq_rows,
            query_back,
            key_back,
            heads_of_query,
            heads_of_key,
            heads_of_value,
            attn_rows,
            log_totals,
            mlp_back,
            mlp_rows,
            swiglu_back,
            hidden,
        ) = saved_layers[layer_index]
        gathered = gather_layer(weight_set, layer_index)
        wide_query, wide_key, wide_value, wide_out, wide_gate, wide_up, wide_down = gathered
        grad_rows = spread_grads(residual_grad.astype(jnp.bfloat16))
        down_grad = contract_rows(hidden, grad_rows)
        hidden_grad = contract_cols(grad_rows, wide_down)
        gate_grad, upward_grad = swiglu_back(hidden_grad)
        gate_low = gate_grad.astype(jnp.bfloat16)
        upward_low = upward_grad.astype(jnp.bfloat16)
        gate_wgrad = contract_rows(mlp_rows, gate_low)
        upward_wgrad = contract_rows(mlp_rows, upward_low)
        normed_grad = collect_grads(((gate_low, wide_gate), (upward_low, wide_up)))
        residual_part, mlp_gain_grad = mlp_back(normed_grad)
        residual_grad = residual_grad + residual_part
        grad_rows = spread_grads(residual_grad.astype(jnp.bfloat16))
        sequence_length = grad_rows.shape[0]
        out_wgrad = contract_rows(attn_rows, grad_rows)
        mixed_grad = contract_cols(grad_rows, wide_out).astype(jnp.bfloat16)
        query_grad, key_grad, value_grad = attend_back(
            heads_of_query,
            heads_of_key,
            heads_of_value,
            segment_row,
            mixed_grad.reshape(heads_of_query.shape),
            log_totals,
        )
        query_raw_grad, query_gain_grad = query_back(query_grad)
        key_raw_grad, key_gain_grad = key_back(key_grad)
        query_low = query_raw_grad.astype(jnp.bfloat16)
        key_low = key_raw_grad.astype(jnp.bfloat16)
        value_low = value_grad.reshape(sequence_length, -1).astype(jnp.bfloat16)
        query_wgrad = contract_rows(seq_rows, query_low)
        key_wgrad = contract_rows(seq_rows, key_low)
        value_wgrad = contract_rows(seq_rows, value_low)
        normed_grad = collect_grads(
            ((query_low, wide_query), (key_low, wide_key), (value_low, wide_value))
        )
        residual_part, attn_gain_grad = attn_back(normed_grad)
        residual_grad = residual_grad + residual_part
        grad_weights[layer_index] = (
            lax.psum_scatter(
                query_wgrad.astype(jnp.bfloat16), "fsdp", scatter_dimension=0, tiled=True
            ).astype(jnp.float32),
            lax.psum_scatter(
                key_wgrad.astype(jnp.bfloat16), "fsdp", scatter_dimension=0, tiled=True
            ).astype(jnp.float32),
            lax.psum_scatter(
                value_wgrad.astype(jnp.bfloat16), "fsdp", scatter_dimension=0, tiled=True
            ).astype(jnp.float32),
            lax.psum_scatter(
                out_wgrad.astype(jnp.bfloat16), "fsdp", scatter_dimension=1, tiled=True
            ).astype(jnp.float32),
            lax.psum_scatter(
                gate_wgrad.astype(jnp.bfloat16), "fsdp", scatter_dimension=0, tiled=True
            ).astype(jnp.float32),
            lax.psum_scatter(
                upward_wgrad.astype(jnp.bfloat16), "fsdp", scatter_dimension=0, tiled=True
            ).astype(jnp.float32),
            lax.psum_scatter(
                down_grad.astype(jnp.bfloat16), "fsdp", scatter_dimension=1, tiled=True
            ).astype(jnp.float32),
        )
        gain_grads[layer_index] = (attn_gain_grad, query_gain_grad, key_gain_grad, mlp_gain_grad)
    local_stacks = tuple(
        (
            jnp.stack([grad_weights[layer_index][member] for layer_index in range(layer_count)])
            for member in range(7)
        )
    )
    gain_stacks = tuple(
        (
            jnp.stack([gain_grads[layer_index][member] for layer_index in range(layer_count)])
            for member in range(4)
        )
    )
    summed = lax.psum(
        (gain_stacks[0], gain_stacks[1], gain_stacks[2], gain_stacks[3]), ("fsdp", "tp")
    )
    return (
        result,
        residual_grad,
        summed[0],
        summed[1],
        summed[2],
        local_stacks[0],
        local_stacks[1],
        local_stacks[2],
        local_stacks[3],
        summed[3],
        local_stacks[4],
        local_stacks[5],
        local_stacks[6],
    )


def solution(mesh):
    placed = (
        P(("fsdp", "tp"), None),
        P("fsdp", None),
        P(),
        P(),
        P(),
        P(None, "fsdp", "tp"),
        P(None, "fsdp", "tp"),
        P(None, "fsdp", "tp"),
        P(None, "tp", "fsdp"),
        P(),
        P(None, "fsdp", "tp"),
        P(None, "fsdp", "tp"),
        P(None, "tp", "fsdp"),
        P(("fsdp", "tp"), None),
    )
    return jax.shard_map(
        on_device,
        mesh=mesh,
        in_specs=placed,
        out_specs=(
            P(("fsdp", "tp"), None),
            P(("fsdp", "tp"), None),
            P(),
            P(),
            P(),
            P(None, "fsdp", "tp"),
            P(None, "fsdp", "tp"),
            P(None, "fsdp", "tp"),
            P(None, "tp", "fsdp"),
            P(),
            P(None, "fsdp", "tp"),
            P(None, "fsdp", "tp"),
            P(None, "tp", "fsdp"),
        ),
        check_vma=False,
    )
```

profile of v0, /device:TPU:8, one launch (start us, length us, event | category | flops | bytes accessed | tf_op | source)
XLA Modules:
  0.0 2766.5 jit_solution(14443399296406095398)
XLA Ops:
  35.3 80.3 %all-gather.37.cloned.1.call-done = bf16[1024,2048]{1,0:T(8,128)(2,1)} async-done(((bf16[256,2048]{1,0:T(8,128)(2,1)}), bf16[1024,2048]{1,0:T(8,128)(2,1)}) %all-gather.37.cloned.1.call-update) | async-done | bytes 4194320 | tf_op jit(solution)/shard_map/all_gather | solution.py:66
  212.8 73.6 %reduce-scatter.23.cloned.1.call-done = bf16[256,2048]{1,0:T(8,128)(2,1)} async-done(((bf16[1024,2048]{1,0:T(8,128)(2,1)}), bf16[256,2048]{1,0:T(8,128)(2,1)}) %reduce-scatter.23.cloned.1.call-update) | async-done | bytes 1048592 | tf_op jit(solution)/shard_map/reduce_scatter | solution.py:74
  294.8 40.3 %all-gather.61.cloned.1.call-done = bf16[1,2048,1536]{2,1,0:T(8,128)(2,1)} async-done(((bf16[1,256,1536]{2,1,0:T(8,128)(2,1)}), bf16[1,2048,1536]{2,1,0:T(8,128)(2,1)}) %all-gather.61.cloned.1.call-update) | async-done | bytes 6291472 | tf_op jit(solution)/shard_map/all_gather | solution.py:101
  335.1 80.4 %all-gather.39.cloned.1.call-done = bf16[1024,2048]{1,0:T(8,128)(2,1)} async-done(((bf16[256,2048]{1,0:T(8,128)(2,1)}), bf16[1024,2048]{1,0:T(8,128)(2,1)}) %all-gather.39.cloned.1.call-update) | async-done | bytes 4194320 | tf_op jit(solution)/shard_map/all_gather | solution.py:66
  525.7 76.3 %reduce-scatter.25.cloned.1.call-done = bf16[256,2048]{1,0:T(8,128)(2,1)} async-done(((bf16[1024,2048]{1,0:T(8,128)(2,1)}), bf16[256,2048]{1,0:T(8,128)(2,1)}) %reduce-scatter.25.cloned.1.call-update) | async-done | bytes 1048592 | tf_op jit(solution)/shard_map/reduce_scatter | solution.py:74
  627.8 80.3 %all-gather.41.cloned.1.call-done = bf16[1024,2048]{1,0:T(8,128)(2,1)} async-done(((bf16[256,2048]{1,0:T(8,128)(2,1)}), bf16[1024,2048]{1,0:T(8,128)(2,1)}) %all-gather.41.cloned.1.call-update) | async-done | bytes 4194320 | tf_op jit(solution)/shard_map/all_gather | solution.py:66
  807.7 74.9 %reduce-scatter.27.cloned.1.call-done = bf16[256,2048]{1,0:T(8,128)(2,1)} async-done(((bf16[1024,2048]{1,0:T(8,128)(2,1)}), bf16[256,2048]{1,0:T(8,128)(2,1)}) %reduce-scatter.27.cloned.1.call-update) | async-done | bytes 1048592 | tf_op jit(solution)/shard_map/reduce_scatter | solution.py:74
  886.5 76.3 %all-gather.45.cloned.1.call-done = bf16[1024,2048]{1,0:T(8,128)(2,1)} async-done(((bf16[256,2048]{1,0:T(8,128)(2,1)}), bf16[1024,2048]{1,0:T(8,128)(2,1)}) %all-gather.45.cloned.1.call-update) | async-done | bytes 4194320 | tf_op jit(solution)/shard_map/all_gather | solution.py:70
  962.9 49.9 %all-gather.79.cloned.1.call-done = bf16[1,1536,2048]{2,1,0:T(8,128)(2,1)} async-done(((bf16[1,1536,256]{2,1,0:T(8,128)(2,1)}), bf16[1,1536,2048]{2,1,0:T(8,128)(2,1)}) %all-gather.79.cloned.1.call-update) | async-done | bytes 6291472 | tf_op jit(solution)/shard_map/all_gather | solution.py:103
  1060.2 80.4 %all-gather.43.cloned.1.call-done = bf16[1024,2048]{1,0:T(8,128)(2,1)} async-done(((bf16[256,2048]{1,0:T(8,128)(2,1)}), bf16[1024,2048]{1,0:T(8,128)(2,1)}) %all-gather.43.cloned.1.call-update) | async-done | bytes 4194320 | tf_op jit(solution)/shard_map/all_gather | solution.py:66
  1152.3 37.1 %all-gather.75.cloned.1.call-done = bf16[1,2048,1536]{2,1,0:T(8,128)(2,1)} async-done(((bf16[1,256,1536]{2,1,0:T(8,128)(2,1)}), bf16[1,2048,1536]{2,1,0:T(8,128)(2,1)}) %all-gather.75.cloned.1.call-update) | async-done | bytes 6291472 | tf_op jit(solution)/shard_map/all_gather | solution.py:101
  1225.8 76.9 %reduce-scatter.31.cloned.1.call-done = bf16[256,2048]{1,0:T(8,128)(2,1)} async-done(((bf16[1024,2048]{1,0:T(8,128)(2,1)}), bf16[256,2048]{1,0:T(8,128)(2,1)}) %reduce-scatter.31.cloned.1.call-update) | async-done | bytes 1048592 | tf_op jit(solution)/shard_map/reduce_scatter | solution.py:87
  1307.8 78.7 %all-gather.47.cloned.1.call-done = bf16[1024,2048]{1,0:T(8,128)(2,1)} async-done(((bf16[256,2048]{1,0:T(8,128)(2,1)}), bf16[1024,2048]{1,0:T(8,128)(2,1)}) %all-gather.47.cloned.1.call-update) | async-done | bytes 4194320 | tf_op jit(solution)/shard_map/all_gather | solution.py:70
  1394.7 44.7 %while.58 = (s32[]{:T(128)}, f32[1024,2,128]{0,2,1:T(8,128)S(1)}, f32[1024,2,128]{0,2,1:T(8,128)}, f32[2,512,2,2,128]{4,1,0,3,2:T(8,128)}, bf16[2,512,2,2,128]{4...) while((s32[]{:T(128)}, f32[1024,2,128]{0,2,1:T(8,128)S(1)}, ...), condition=%wide.region_26.27_spmd.clone, body=%wide.region_24.26_spmd.clone.sunk | while | flops 2718955520 | bytes 165226272 | solution.py:214
  1474.1 64.9 %reduce-scatter.33.cloned.1.call-done = bf16[256,2048]{1,0:T(8,128)(2,1)} async-done(((bf16[1024,2048]{1,0:T(8,128)(2,1)}), bf16[256,2048]{1,0:T(8,128)(2,1)}) %reduce-scatter.33.cloned.1.call-update) | async-done | bytes 1048592 | tf_op jit(solution)/shard_map/reduce_scatter | solution.py:87
  1541.6 77.0 %reduce-scatter.29.cloned.1.call-done = bf16[256,2048]{1,0:T(8,128)(2,1)} async-done(((bf16[1024,2048]{1,0:T(8,128)(2,1)}), bf16[256,2048]{1,0:T(8,128)(2,1)}) %reduce-scatter.29.cloned.1.call-update) | async-done | bytes 1048592 | tf_op jit(solution)/shard_map/reduce_scatter | solution.py:74
  1624.4 78.7 %all-gather.49.cloned.1.call-done = bf16[1024,2048]{1,0:T(8,128)(2,1)} async-done(((bf16[256,2048]{1,0:T(8,128)(2,1)}), bf16[1024,2048]{1,0:T(8,128)(2,1)}) %all-gather.49.cloned.1.call-update) | async-done | bytes 4194320 | tf_op jit(solution)/shard_map/all_gather | solution.py:70
  1740.4 77.6 %reduce-scatter.35.cloned.1.call-done = bf16[256,2048]{1,0:T(8,128)(2,1)} async-done(((bf16[1024,2048]{1,0:T(8,128)(2,1)}), bf16[256,2048]{1,0:T(8,128)(2,1)}) %reduce-scatter.35.cloned.1.call-update) | async-done | bytes 1048592 | tf_op jit(solution)/shard_map/reduce_scatter | solution.py:87
  1913.3 45.6 %while.59 = (s32[]{:T(128)}, f32[1024,2,128]{0,2,1:T(8,128)S(1)}, f32[1024,2,128]{0,2,1:T(8,128)}, f32[2,512,2,2,128]{4,1,0,3,2:T(8,128)}, bf16[2,512,2,2,128]{4...) while((s32[]{:T(128)}, f32[1024,2,128]{0,2,1:T(8,128)S(1)}, ...), condition=%wide.region_35.36_spmd.clone, body=%wide.region_33.35_spmd.clone.sunk | while | flops 2718955520 | bytes 163129120 | solution.py:214
  2037.1 62.3 %reduce-scatter.61.cloned.1.call-done = bf16[256,1536]{1,0:T(8,128)(2,1)} async-done(((bf16[2048,1536]{1,0:T(8,128)(2,1)}), bf16[256,1536]{1,0:T(8,128)(2,1)}) %reduce-scatter.61.cloned.1.call-update) | async-done | bytes 786448 | tf_op jit(solution)/shard_map/reduce_scatter | solution.py:382
  2099.4 65.0 %reduce-scatter.59.cloned.1.call-done = bf16[256,1536]{1,0:T(8,128)(2,1)} async-done(((bf16[2048,1536]{1,0:T(8,128)(2,1)}), bf16[256,1536]{1,0:T(8,128)(2,1)}) %reduce-scatter.59.cloned.1.call-update) | async-done | bytes 786448 | tf_op jit(solution)/shard_map/reduce_scatter | solution.py:382
  2167.6 62.3 %reduce-scatter.57.cloned.1.call-done = bf16[256,1536]{1,0:T(8,128)(2,1)} async-done(((bf16[2048,1536]{1,0:T(8,128)(2,1)}), bf16[256,1536]{1,0:T(8,128)(2,1)}) %reduce-scatter.57.cloned.1.call-update) | async-done | bytes 786448 | tf_op jit(solution)/shard_map/reduce_scatter | solution.py:379
  2229.9 65.1 %reduce-scatter.55.cloned.1.call-done = bf16[256,1536]{1,0:T(8,128)(2,1)} async-done(((bf16[2048,1536]{1,0:T(8,128)(2,1)}), bf16[256,1536]{1,0:T(8,128)(2,1)}) %reduce-scatter.55.cloned.1.call-update) | async-done | bytes 786448 | tf_op jit(solution)/shard_map/reduce_scatter | solution.py:379
  2334.5 39.4 %reduce-scatter.47.cloned.1.call-done = bf16[256,256]{1,0:T(8,128)(2,1)} async-done(((bf16[2048,256]{1,0:T(8,128)(2,1)}), bf16[256,256]{1,0:T(8,128)(2,1)}) %reduce-scatter.47.cloned.1.call-update) | async-done | bytes 131088 | tf_op jit(solution)/shard_map/reduce_scatter | solution.py:373
  2375.8 38.3 %reduce-scatter.45.cloned.1.call-done = bf16[256,256]{1,0:T(8,128)(2,1)} async-done(((bf16[2048,256]{1,0:T(8,128)(2,1)}), bf16[256,256]{1,0:T(8,128)(2,1)}) %reduce-scatter.45.cloned.1.call-update) | async-done | bytes 131088 | tf_op jit(solution)/shard_map/reduce_scatter | solution.py:370
  2414.0 40.0 %reduce-scatter.43.cloned.1.call-done = bf16[256,256]{1,0:T(8,128)(2,1)} async-done(((bf16[2048,256]{1,0:T(8,128)(2,1)}), bf16[256,256]{1,0:T(8,128)(2,1)}) %reduce-scatter.43.cloned.1.call-update) | async-done | bytes 131088 | tf_op jit(solution)/shard_map/reduce_scatter | solution.py:370
  2455.8 43.1 %reduce-scatter.53.cloned.1.call-done = bf16[512,256]{1,0:T(8,128)(2,1)} async-done(((bf16[512,2048]{1,0:T(8,128)(2,1)}), bf16[512,256]{1,0:T(8,128)(2,1)}) %reduce-scatter.53.cloned.1.call-update) | async-done | bytes 262160 | tf_op jit(solution)/shard_map/reduce_scatter | solution.py:376
  2498.9 44.6 %reduce-scatter.51.cloned.1.call-done = bf16[512,256]{1,0:T(8,128)(2,1)} async-done(((bf16[512,2048]{1,0:T(8,128)(2,1)}), bf16[512,256]{1,0:T(8,128)(2,1)}) %reduce-scatter.51.cloned.1.call-update) | async-done | bytes 262160 | tf_op jit(solution)/shard_map/reduce_scatter | solution.py:376
  2545.6 42.8 %reduce-scatter.41.cloned.1.call-done = bf16[256,512]{1,0:T(8,128)(2,1)} async-done(((bf16[2048,512]{1,0:T(8,128)(2,1)}), bf16[256,512]{1,0:T(8,128)(2,1)}) %reduce-scatter.41.cloned.1.call-update) | async-done | bytes 262160 | tf_op jit(solution)/shard_map/reduce_scatter | solution.py:367
  2588.4 44.4 %reduce-scatter.39.cloned.1.call-done = bf16[256,512]{1,0:T(8,128)(2,1)} async-done(((bf16[2048,512]{1,0:T(8,128)(2,1)}), bf16[256,512]{1,0:T(8,128)(2,1)}) %reduce-scatter.39.cloned.1.call-update) | async-done | bytes 262160 | tf_op jit(solution)/shard_map/reduce_scatter | solution.py:367
  2634.9 77.1 %reduce-scatter.37.cloned.1.call-done = bf16[256,2048]{1,0:T(8,128)(2,1)} async-done(((bf16[1024,2048]{1,0:T(8,128)(2,1)}), bf16[256,2048]{1,0:T(8,128)(2,1)}) %reduce-scatter.37.cloned.1.call-update) | async-done | bytes 1048592 | tf_op jit(solution)/shard_map/reduce_scatter | solution.py:87
  2714.3 40.7 %all-reduce.8 = (f32[2,2048]{1,0:T(2,128)}, f32[2,128]{1,0:T(2,128)}, f32[2,128]{1,0:T(2,128)}, f32[2,2048]{1,0:T(2,128)}) all-reduce(f32[2,2048]{1,0:T(2,128)S(1)} %get-tuple-element.743, f32[2,128]{1,0:T(2,128)S(1)} %get-tuple-element.745, f32[2,128]{1,0:T(2,128)S(1)} %get-tuple-element.746, ...), channel_id=1, replica_groups=mesh['fsdp'=8,'tp'=4] {'fsdp','tp'}, use_global_device_ids=true, to_apply=%region_42.43 | all-reduce | flops 8704 | bytes 69632 | tf_op jit(solution)/shard_map/psum | solution.py:402
  (679 shorter events, 921.3 us)
Async XLA Ops:
  16.9 186.6 %all-gather.59.cloned.1.call-start = ((), (), s32[]{:S(2)}) async-start(), calls=%async_computation.55 | async-start | bytes 2359296 | tf_op jit(solution)/shard_map/all_gather | solution.py:100
  17.8 268.6 %reduce-scatter.23.cloned.1.call-start = ((), (), s32[]{:S(2)}) async-start(), calls=%async_computation.23 | async-start | bytes 5242880 | tf_op jit(solution)/shard_map/reduce_scatter | solution.py:74
  212.1 203.4 %all-gather.39.cloned.1.call-start = ((), (), s32[]{:S(2)}) async-start(), calls=%async_computation.24 | async-start | bytes 5242880 | tf_op jit(solution)/shard_map/all_gather | solution.py:66
  290.7 174.1 %all-gather.63.cloned.1.call-start = ((), (), s32[]{:S(2)}) async-start(), calls=%async_computation.57 | async-start | bytes 7077888 | tf_op jit(solution)/shard_map/all_gather | solution.py:102
  292.1 221.9 %all-gather.65.cloned.1.call-start = ((), (), s32[]{:S(2)}) async-start(), calls=%async_computation.58 | async-start | bytes 7077888 | tf_op jit(solution)/shard_map/all_gather | solution.py:103
  294.7 307.2 %reduce-scatter.25.cloned.1.call-start = ((), (), s32[]{:S(2)}) async-start(), calls=%async_computation.25 | async-start | bytes 5242880 | tf_op jit(solution)/shard_map/reduce_scatter | solution.py:74
  525.6 182.4 %all-gather.41.cloned.1.call-start = ((), (), s32[]{:S(2)}) async-start(), calls=%async_computation.26 | async-start | bytes 5242880 | tf_op jit(solution)/shard_map/all_gather | solution.py:66
  607.0 192.5 %all-gather.73.cloned.1.call-start = ((), (), s32[]{:S(2)}) async-start(), calls=%async_computation.62 | async-start | bytes 2359296 | tf_op jit(solution)/shard_map/all_gather | solution.py:100
  607.6 275.0 %reduce-scatter.27.cloned.1.call-start = ((), (), s32[]{:S(2)}) async-start(), calls=%async_computation.27 | async-start | bytes 5242880 | tf_op jit(solution)/shard_map/reduce_scatter | solution.py:74
  806.4 206.4 %all-gather.79.cloned.1.call-start = ((), (), s32[]{:S(2)}) async-start(), calls=%async_computation.65 | async-start | bytes 7077888 | tf_op jit(solution)/shard_map/all_gather | solution.py:103
  807.1 253.1 %all-gather.77.cloned.1.call-start = ((), (), s32[]{:S(2)}) async-start(), calls=%async_computation.64 | async-start | bytes 7077888 | tf_op jit(solution)/shard_map/all_gather | solution.py:102
  807.7 332.9 %all-gather.43.cloned.1.call-start = ((), (), s32[]{:S(2)}) async-start(), calls=%async_computation.28 | async-start | bytes 5242880 | tf_op jit(solution)/shard_map/all_gather | solution.py:66
  885.7 303.6 %all-gather.75.cloned.1.call-start = ((), (), s32[]{:S(2)}) async-start(), calls=%async_computation.63 | async-start | bytes 7077888 | tf_op jit(solution)/shard_map/all_gather | solution.py:101
  886.5 416.2 %reduce-scatter.31.cloned.1.call-start = ((), (), s32[]{:S(2)}) async-start(), calls=%async_computation.31 | async-start | bytes 5242880 | tf_op jit(solution)/shard_map/reduce_scatter | solution.py:87
  1307.8 231.3 %reduce-scatter.33.cloned.1.call-start = ((), (), s32[]{:S(2)}) async-start(), calls=%async_computation.33 | async-start | bytes 5242880 | tf_op jit(solution)/shard_map/reduce_scatter | solution.py:87
  1473.9 229.2 %all-gather.49.cloned.1.call-start = ((), (), s32[]{:S(2)}) async-start(), calls=%async_computation.34 | async-start | bytes 5242880 | tf_op jit(solution)/shard_map/all_gather | solution.py:70
  1624.3 193.7 %reduce-scatter.35.cloned.1.call-start = ((), (), s32[]{:S(2)}) async-start(), calls=%async_computation.35 | async-start | bytes 5242880 | tf_op jit(solution)/shard_map/reduce_scatter | solution.py:87
  1823.4 192.0 %reduce-scatter.65.cloned.1.call-start = ((), (), s32[]{:S(2)}) async-start(), calls=%async_computation.51 | async-start | bytes 7077888 | tf_op jit(solution)/shard_map/reduce_scatter | solution.py:385
  1834.7 199.1 %reduce-scatter.63.cloned.1.call-start = ((), (), s32[]{:S(2)}) async-start(), calls=%async_computation.50 | async-start | bytes 7077888 | tf_op jit(solution)/shard_map/reduce_scatter | solution.py:385
  1847.5 251.9 %reduce-scatter.61.cloned.1.call-start = ((), (), s32[]{:S(2)}) async-start(), calls=%async_computation.49 | async-start | bytes 7077888 | tf_op jit(solution)/shard_map/reduce_scatter | solution.py:382
  1860.4 304.0 %reduce-scatter.59.cloned.1.call-start = ((), (), s32[]{:S(2)}) async-start(), calls=%async_computation.48 | async-start | bytes 7077888 | tf_op jit(solution)/shard_map/reduce_scatter | solution.py:382
  1873.4 356.6 %reduce-scatter.57.cloned.1.call-start = ((), (), s32[]{:S(2)}) async-start(), calls=%async_computation.47 | async-start | bytes 7077888 | tf_op jit(solution)/shard_map/reduce_scatter | solution.py:379
  1886.3 408.8 %reduce-scatter.55.cloned.1.call-start = ((), (), s32[]{:S(2)}) async-start(), calls=%async_computation.46 | async-start | bytes 7077888 | tf_op jit(solution)/shard_map/reduce_scatter | solution.py:379
  1899.4 435.1 %reduce-scatter.49.cloned.1.call-start = ((), (), s32[]{:S(2)}) async-start(), calls=%async_computation.43 | async-start | bytes 1179648 | tf_op jit(solution)/shard_map/reduce_scatter | solution.py:373
  1904.9 469.0 %reduce-scatter.47.cloned.1.call-start = ((), (), s32[]{:S(2)}) async-start(), calls=%async_computation.42 | async-start | bytes 1179648 | tf_op jit(solution)/shard_map/reduce_scatter | solution.py:373
  1965.7 448.3 %reduce-scatter.45.cloned.1.call-start = ((), (), s32[]{:S(2)}) async-start(), calls=%async_computation.41 | async-start | bytes 1179648 | tf_op jit(solution)/shard_map/reduce_scatter | solution.py:370
  1970.5 483.5 %reduce-scatter.43.cloned.1.call-start = ((), (), s32[]{:S(2)}) async-start(), calls=%async_computation.40 | async-start | bytes 1179648 | tf_op jit(solution)/shard_map/reduce_scatter | solution.py:370
  1976.6 522.3 %reduce-scatter.53.cloned.1.call-start = ((), (), s32[]{:S(2)}) async-start(), calls=%async_computation.45 | async-start | bytes 2359296 | tf_op jit(solution)/shard_map/reduce_scatter | solution.py:376
  1983.3 560.2 %reduce-scatter.51.cloned.1.call-start = ((), (), s32[]{:S(2)}) async-start(), calls=%async_computation.44 | async-start | bytes 2359296 | tf_op jit(solution)/shard_map/reduce_scatter | solution.py:376
  1990.0 598.4 %reduce-scatter.41.cloned.1.call-start = ((), (), s32[]{:S(2)}) async-start(), calls=%async_computation.39 | async-start | bytes 2359296 | tf_op jit(solution)/shard_map/reduce_scatter | solution.py:367
  1996.0 636.8 %reduce-scatter.39.cloned.1.call-start = ((), (), s32[]{:S(2)}) async-start(), calls=%async_computation.38 | async-start | bytes 2359296 | tf_op jit(solution)/shard_map/reduce_scatter | solution.py:367
  2007.7 704.3 %reduce-scatter.37.cloned.1.call-start = ((), (), s32[]{:S(2)}) async-start(), calls=%async_computation.37 | async-start | bytes 5242880 | tf_op jit(solution)/shard_map/reduce_scatter | solution.py:87
  (178 other events, 10280.6 us)
Sparse Core Ops, SparseCore 0:
  37.4 78.0 all-gather.36
  209.6 76.7 reduce-scatter.22
  289.0 46.0 all-gather.60
  337.3 78.1 all-gather.38
  418.1 46.6 all-gather.62
  467.3 46.6 all-gather.64
  525.2 76.7 reduce-scatter.24
  629.9 78.1 all-gather.40
  805.9 76.7 reduce-scatter.26
  884.2 78.6 all-gather.44
  964.9 47.8 all-gather.78
  1014.7 45.5 all-gather.76
  1062.4 78.1 all-gather.42
  1142.6 46.6 all-gather.74
  1225.9 76.7 reduce-scatter.30
  1307.9 78.6 all-gather.46
  1461.1 77.9 reduce-scatter.32
  1541.3 77.2 reduce-scatter.28
  1624.5 78.6 all-gather.48
  1740.1 77.9 reduce-scatter.34
  1823.5 78.6 all-gather.50
  1905.8 62.9 reduce-scatter.64
  1972.1 61.7 reduce-scatter.62
  2037.6 61.7 reduce-scatter.60
  2102.6 61.7 reduce-scatter.58
  2168.2 61.7 reduce-scatter.56
  2233.3 61.7 reduce-scatter.54
  2457.7 41.2 reduce-scatter.52
  2502.2 41.2 reduce-scatter.50
  2547.1 41.2 reduce-scatter.40
  2591.5 41.2 reduce-scatter.38
  2635.2 76.7 reduce-scatter.36
  (12 shorter events, 353.6 us)
where the time goes:
time: 2780 us; the launch traced here: 2770 us
  waiting for transfers between devices  2070 us (74%)
  matrix products  411 us (15%)
  other arithmetic  120 us (4%)
  local copies, waits for them, and re-layouts  107 us (4%)
  blocking collectives  40.7 us (1%)
    all_gather x4, waiting for transfers between devices, spread_rows(): return lax.all_gather(rows_low, 'tp', axis=0, tiled=True)  321 us
    reduce_scatter x4, waiting for transfers between devices, collect_rows(): lax.psum_scatter(jnp.dot(left_side, right_side, preferred_element_type=jn...  302 us
    reduce_scatter x4, waiting for transfers between devices, collect_grads(): lax.psum_scatter(running.astype(jnp.bfloat16), 'tp', scatter_dimension=0,...  297 us
    all_gather x4, waiting for transfers between devices, spread_grads(): return lax.all_gather(grad_low, 'tp', axis=0, tiled=True)  234 us
    reduce_scatter x2, waiting for transfers between devices, on_device(): lax.psum_scatter(gate_wgrad.astype(jnp.bfloat16), 'fsdp', scatter_dimensi...  127 us
    reduce_scatter x2, waiting for transfers between devices, on_device(): lax.psum_scatter(upward_wgrad.astype(jnp.bfloat16), 'fsdp', scatter_dimen...  127 us
    dot_general x14, matrix products, contract_rows(): lax.dot_general(left_side, right_side, (((0,), (0,)), ((), ())), preferre...  105 us
    dot_general x14, matrix products, contract_cols(): lax.dot_general(left_side, right_side, (((1,), (1,)), ((), ())), preferre...  93 us
  transfers between devices with their start and end apart: 44, of which 40 were waited for; matrix products, arithmetic and copies ran while one was open for 15% of the time, Pallas kernels for 0%

commit v1 on v0

--- a/solution.py
+++ b/solution.py
@@ -1,8 +1,11 @@
+import functools
 import math
 
 import jax
 import jax.numpy as jnp
 from jax import lax
+from jax.experimental import pallas as pl
+from jax.experimental.pallas import tpu as pltpu
 from jax.sharding import PartitionSpec as P
 
 EPSILON = 1e-06
@@ -223,7 +226,7 @@
     )
 
 
-def on_device(
+def general_plan(
     tokens,
     segment_ids,
     attn_gain,
@@ -419,6 +422,642 @@
     )
 
 
+def plane_send(values, distance):
+    size = lax.axis_size("fsdp")
+    return lax.ppermute(values, "fsdp", [(i, i ^ distance) for i in range(size)])
+
+
+def plane_place():
+    return lax.axis_index("fsdp").astype(jnp.int32).reshape(1)
+
+
+def low(values):
+    return values.astype(jnp.bfloat16)
+
+
+def wide(values):
+    return values.astype(jnp.float32)
+
+
+def add_low(left, right):
+    return low(wide(left) + wide(right))
+
+
+def gather_plane(own):
+    half = own.shape[0] // 2
+    core = plane_send(own, 1)
+    across_x = plane_send(own, 2)
+    across_y = plane_send(own, 4)
+    diagonal = jnp.concatenate(
+        [plane_send(across_y[:half], 2), plane_send(across_x[half:], 4)]
+    )
+    return [
+        own,
+        core,
+        across_x,
+        plane_send(across_x, 1),
+        across_y,
+        plane_send(across_y, 1),
+        diagonal,
+        plane_send(diagonal, 1),
+    ]
+
+
+def reduce_plane(part):
+    received = {d: plane_send(low(part(d)), 1) for d in (7, 5, 3, 1)}
+    far, by_y, by_x, here = (
+        low(part(d) + wide(received[d + 1])) if d else part(d) + wide(received[d + 1])
+        for d in (6, 4, 2, 0)
+    )
+    half = far.shape[0] // 2
+    top = plane_send(far[:half], 2)
+    bottom = plane_send(far[half:], 4)
+    by_y = jnp.concatenate([add_low(by_y[:half], top), by_y[half:]])
+    by_x = jnp.concatenate([by_x[:half], add_low(by_x[half:], bottom)])
+    from_x = plane_send(by_x, 2)
+    from_y = plane_send(by_y, 4)
+    return here + wide(from_x) + wide(from_y), far, by_x
+
+
+def reduce_all(values):
+    for distance in (1, 2, 4):
+        values = values + plane_send(values, distance)
+    size = lax.axis_size("tp")
+    if size & (size - 1):
+        return lax.psum(values, "tp")
+    distance = 1
+    while distance < size:
+        pairs = [(i, i ^ distance) for i in range(size)]
+        values = values + lax.ppermute(values, "tp", pairs)
+        distance *= 2
+    return values
+
+
+def after(token, *values):
+    if token is None:
+        return values
+    return lax.optimization_barrier((token, *values))[1:]
+
+
+def line_gather(own, axis=0):
+    return lax.all_gather(own, "tp", axis=axis, tiled=True)
+
+
+def line_reduce(terms, axis=0):
+    return lax.psum_scatter(terms, "tp", scatter_dimension=axis, tiled=True)
+
+
+def assemble(pieces, axis, places):
+    size = len(pieces)
+    block = pieces[0].shape[axis]
+    shape = list(pieces[0].shape)
+    shape[axis] = size * block
+
+    def kernel(place_ref, *refs):
+        out = refs[size]
+        for d in range(size):
+            start = pl.multiple_of(place_ref[d] * block, block)
+            where = tuple([slice(None)] * axis + [pl.ds(start, block)])
+            out[where] = refs[d][...]
+
+    return pl.pallas_call(
+        kernel,
+        out_shape=jax.ShapeDtypeStruct(tuple(shape), pieces[0].dtype),
+        in_specs=[pl.BlockSpec(memory_space=pltpu.SMEM)]
+        + [pl.BlockSpec(memory_space=pltpu.VMEM)] * size,
+        out_specs=pl.BlockSpec(memory_space=pltpu.VMEM),
+        compiler_params=pltpu.CompilerParams(vmem_limit_bytes=32 * 1024 * 1024),
+        name="assemble",
+    )(places, *pieces)
+
+
+def block_at(array, index, block, axis):
+    return lax.dynamic_slice_in_dim(array, index * block, block, axis)
+
+
+def swap(array, axis, into, start=None, done=None):
+    size = lax.axis_size("fsdp")
+    places = lax.axis_index("fsdp").astype(jnp.int32) ^ jnp.arange(size, dtype=jnp.int32)
+    block = array.shape[axis] // size
+    (array,) = after(start, array)
+    pieces = [block_at(array, places[d], block, axis) for d in range(size)]
+    order = (6, 7, 4, 5, 2, 3, 1)
+    moved = {d: plane_send(pieces[d], d) for d in order}
+    moved = after(done, *(moved[d] for d in range(1, size)))
+    return assemble([pieces[0], *moved], into, places)
+
+
+def line_swap(array, start=None, done=None):
+    size = lax.axis_size("tp")
+    place = lax.axis_index("tp").astype(jnp.int32)
+    block = array.shape[0] // size
+    sources = (place - jnp.arange(size, dtype=jnp.int32)) % size
+    (array,) = after(start, array)
+    moved = []
+    for step in range(1, size):
+        piece = block_at(array, (place + step) % size, block, 0)
+        pairs = [(i, (i + step) % size) for i in range(size)]
+        moved.append(lax.ppermute(piece, "tp", pairs))
+    moved = after(done, *moved)
+    return assemble([block_at(array, place, block, 0), *moved], 0, sources)
+
+
+def line_rows(rows, start=None, done=None):
+    size, line = lax.axis_size("fsdp"), lax.axis_size("tp")
+    count, width = rows.shape
+    blocks = line_swap(rows, start, done).reshape(line, size // line, count // size, width)
+    return blocks.transpose(1, 0, 2, 3).reshape(count, width)
+
+
+def line_rows_back(rows, start=None, done=None):
+    size, line = lax.axis_size("fsdp"), lax.axis_size("tp")
+    count, width = rows.shape
+    blocks = rows.reshape(size // line, line, count // size, width).transpose(1, 0, 2, 3)
+    return line_swap(blocks.reshape(count, width), start, done)
+
+
+def plane_segments(segment_ids):
+    size, line = lax.axis_size("fsdp"), lax.axis_size("tp")
+    rows = segment_ids
+    for distance in (1, 2, 4):
+        rows = jnp.concatenate([rows, plane_send(rows, distance)])
+    local = size // line
+    wanted = lax.axis_index("tp") * local + jnp.arange(local)
+    return rows[wanted ^ lax.axis_index("fsdp")]
+
+
+def attention_weights(query_shard, key_shard, value_shard, out_shard):
+    size, line = lax.axis_size("fsdp"), lax.axis_size("tp")
+    per, depth = size // line, query_shard.shape[0]
+    pack = jnp.concatenate(
+        [
+            query_shard.T.reshape(per, -1, depth),
+            key_shard.T.reshape(per, -1, depth),
+            value_shard.T.reshape(per, -1, depth),
+            out_shard.reshape(per, -1, depth),
+        ],
+        axis=1,
+    )
+    gathered = line_gather(pack)
+    return swap(gathered, 0, 2)[0], gathered
+
+
+def turn(values, cosine, sine):
+    return values * cosine + pltpu.roll(values, values.shape[1] // 2, 1) * sine
+
+
+def turn_back(values, cosine, sine):
+    return values * cosine - pltpu.roll(values, values.shape[1] // 2, 1) * sine
+
+
+def inverse_rms(values):
+    return lax.rsqrt(jnp.mean(values * values, axis=-1, keepdims=True) + EPSILON)
+
+
+def rows_in_order(place, groups, target, pick):
+    for d in range(2 * len(groups)):
+        ref = groups[d // 2]
+        blocks, block = ref.shape[2], ref.shape[3]
+        for i in range(blocks):
+            start = pl.multiple_of((i * 2 * len(groups) + (place ^ d)) * block, block)
+            target[pl.ds(start, block), :] = pick(ref[d % 2, 0, i])
+
+
+def rows_from_order(place, source, groups):
+    for d in range(2 * len(groups)):
+        ref = groups[d // 2]
+        blocks, block = ref.shape[2], ref.shape[3]
+        for i in range(blocks):
+            start = pl.multiple_of((i * 2 * len(groups) + (place ^ d)) * block, block)
+            ref[d % 2, 0, i] = source[pl.ds(start, block), :].astype(ref.dtype)
+
+
+def head_columns(index, head):
+    return slice(index * head, (index + 1) * head)
+
+
+def heads_from_raw(nat, cos_ref, sin_ref, gains, heads, low_ref, rows):
+    head = cos_ref.shape[-1]
+    for start in range(0, nat.shape[0], rows):
+        here = slice(start, start + rows)
+        cosine, sine = cos_ref[0, here, :], sin_ref[0, here, :]
+        for h in range(heads + 2):
+            raw = nat[here, head_columns(h, head)]
+            if h <= heads:
+                gain = gains[0] if h < heads else gains[1]
+                raw = turn(raw * inverse_rms(raw) * gain[...], cosine, sine)
+            low_ref[here, head_columns(h, head)] = raw.astype(low_ref.dtype)
+
+
+def block_operands(low_ref, start, rows, heads, head):
+    query = jnp.concatenate(
+        [low_ref[start : start + rows, head_columns(h, head)] for h in range(heads)], axis=0
+    )
+    key = low_ref[: start + rows, head_columns(heads, head)]
+    value = low_ref[: start + rows, head_columns(heads + 1, head)]
+    return query, key, value
+
+
+def masked_scores(key, query, first_ref, start, rows, heads, scale):
+    scores = lax.dot_general(
+        key, query, (((1,), (1,)), ((), ())), preferred_element_type=jnp.float32
+    )
+    shape = (key.shape[0], rows)
+    index = lax.broadcasted_iota(jnp.int32, shape, 0)
+    mine = lax.broadcasted_iota(jnp.int32, shape, 1) + start
+    first = first_ref[0, :, start : start + rows]
+    allowed = (index <= mine) & (index >= first)
+    allowed = jnp.concatenate([allowed] * heads, axis=1)
+    return jnp.where(allowed, scores * scale, -1e30)
+
+
+def attend_kernel(groups, heads, rows, *refs):
+    place = refs[0][0]
+    raw_refs = refs[1 : 1 + groups]
+    cos_ref, sin_ref, first_ref, query_gain, key_gain = refs[1 + groups : 6 + groups]
+    out_refs = refs[6 + groups : 6 + 2 * groups]
+    total_ref, nat, low_ref, mixed = refs[6 + 2 * groups :]
+    head = cos_ref.shape[-1]
+    rows_in_order(place, raw_refs, nat, lambda v: v)
+    heads_from_raw(nat, cos_ref, sin_ref, (query_gain, key_gain), heads, low_ref, rows)
+    for i in range(nat.shape[0] // rows):
+        start = i * rows
+        query, key, value = block_operands(low_ref, start, rows, heads, head)
+        scores = masked_scores(key, query, first_ref, start, rows, heads, head ** (-0.5))
+        top = jnp.max(scores, axis=0, keepdims=True)
+        weights = jnp.exp(scores - top)
+        total = jnp.sum(weights, axis=0, keepdims=True)
+        total_ref[0, i : i + 1, :] = top + jnp.log(total)
+        prob = (weights * (1.0 / total)).astype(jnp.bfloat16)
+        out = lax.dot_general(
+            prob, value, (((0,), (0,)), ((), ())), preferred_element_type=jnp.float32
+        ).astype(jnp.bfloat16)
+        for h in range(heads):
+            mixed[start : start + rows, head_columns(h, head)] = out[h * rows : (h + 1) * rows]
+    rows_from_order(place, mixed, out_refs)
+
+
+def attend_back_kernel(groups, heads, rows, *refs):
+    place = refs[0][0]
+    raw_refs = refs[1 : 1 + groups]
+    grad_refs = refs[1 + groups : 1 + 2 * groups]
+    rest = refs[1 + 2 * groups :]
+    total_ref, cos_ref, sin_ref, first_ref, query_gain, key_gain = rest[:6]
+    out_refs = rest[6 : 6 + groups]
+    gain_ref, nat, low_ref, mixed, grads, key_sum, value_sum, done = rest[6 + groups :]
+    head = cos_ref.shape[-1]
+    scale = head ** (-0.5)
+    rows_in_order(place, raw_refs, nat, lambda v: v)
+    rows_in_order(place, grad_refs, mixed, lambda v: v)
+    heads_from_raw(nat, cos_ref, sin_ref, (query_gain, key_gain), heads, low_ref, rows)
+    key_sum[...] = jnp.zeros_like(key_sum)
+    value_sum[...] = jnp.zeros_like(value_sum)
+    for i in range(nat.shape[0] // rows):
+        start = i * rows
+        stop = start + rows
+        query, key, value = block_operands(low_ref, start, rows, heads, head)
+        out_grad = jnp.concatenate(
+            [mixed[start:stop, head_columns(h, head)] for h in range(heads)], axis=0
+        )
+        scores = masked_scores(key, query, first_ref, start, rows, heads, scale)
+        prob = jnp.exp(scores - total_ref[0, i : i + 1, :])
+        prob_grad = lax.dot_general(
+            value, out_grad, (((1,), (1,)), ((), ())), preferred_element_type=jnp.float32
+        )
+        inner = jnp.sum(prob * prob_grad, axis=0, keepdims=True)
+        score_grad = (prob * (prob_grad - inner)).astype(jnp.bfloat16)
+        value_sum[:stop, :] += jnp.dot(
+            prob.astype(jnp.bfloat16), out_grad, preferred_element_type=jnp.float32
+        )
+        key_sum[:stop, :] += jnp.dot(score_grad, query, preferred_element_type=jnp.float32)
+        query_grad = lax.dot_general(
+            score_grad, key, (((0,), (0,)), ((), ())), preferred_element_type=jnp.float32
+        )
+        for h in range(heads):
+            grads[start:stop, head_columns(h, head)] = query_grad[h * rows : (h + 1) * rows] * scale
+    sums = [jnp.zeros((1, head), jnp.float32)] * 2
+    for start in range(0, nat.shape[0], rows):
+        here = slice(start, start + rows)
+        cosine, sine = cos_ref[0, here, :], sin_ref[0, here, :]
+        for h in range(heads + 1):
+            kind = 0 if h < heads else 1
+            gain = (query_gain, key_gain)[kind][...]
+            grad = grads[here, head_columns(h, head)] if h < heads else key_sum[here, :] * scale
+            raw = nat[here, head_columns(h, head)]
+            inverse = inverse_rms(raw)
+            grad = turn_back(grad, cosine, sine)
+            sums[kind] += jnp.sum(grad * raw * inverse, axis=0, keepdims=True)
+            grad = grad * gain
+            middle = jnp.mean(grad * raw, axis=-1, keepdims=True)
+            done[here, head_columns(h, head)] = (
+                inverse * grad - raw * (inverse * inverse * inverse) * middle
+            ).astype(done.dtype)
+        done[here, head_columns(heads + 1, head)] = value_sum[here, :].astype(done.dtype)
+    gain_ref[0] = jnp.concatenate(sums, axis=0)
+    rows_from_order(place, done, out_refs)
+
+
+def attend_specs(raw, tables, first, length, head):
+    local = tables[0].shape[0]
+    group = pl.BlockSpec((2, 1) + raw[0].shape[2:], lambda s: (0, s, 0, 0, 0))
+    table = pl.BlockSpec((1, length, head), lambda s: (s, 0, 0))
+    line = pl.BlockSpec((1, 1, length), lambda s: (s, 0, 0))
+    gain = pl.BlockSpec((1, head), lambda s: (0, 0))
+    return local, group, table, line, gain
+
+
+def grouped(rows, local, blocks):
+    count, width = rows.shape
+    return rows.reshape(2, local, blocks, count // (2 * local * blocks), width)
+
+
+def plane_attend(raw, tables, first, gains, rows=256):
+    head = tables[0].shape[-1]
+    length = tables[0].shape[1]
+    local, group, table, line, gain = attend_specs(raw, tables, first, length, head)
+    width = raw[0].shape[-1]
+    heads = width // head - 2
+    groups = len(raw)
+    out_shape = raw[0].shape[:-1] + (heads * head,)
+    out_group = pl.BlockSpec((2, 1) + out_shape[2:], lambda s: (0, s, 0, 0, 0))
+    totals = jax.ShapeDtypeStruct((local, length // rows, heads * rows), jnp.float32)
+    out = pl.pallas_call(
+        functools.partial(attend_kernel, groups, heads, rows),
+        grid=(local,),
+        out_shape=[jax.ShapeDtypeStruct(out_shape, jnp.bfloat16)] * groups + [totals],
+        in_specs=[pl.BlockSpec(memory_space=pltpu.SMEM)]
+        + [group] * groups
+        + [table, table, line, gain, gain],
+        out_specs=[out_group] * groups
+        + [pl.BlockSpec((1,) + totals.shape[1:], lambda s: (s, 0, 0))],
+        scratch_shapes=[
+            pltpu.VMEM((length, width), jnp.float32),
+            pltpu.VMEM((length, width), jnp.bfloat16),
+            pltpu.VMEM((length, heads * head), jnp.bfloat16),
+        ],
+        compiler_params=pltpu.CompilerParams(vmem_limit_bytes=48 * 1024 * 1024),
+        cost_estimate=pl.CostEstimate(
+            flops=local * heads * length * length * head * 5 // 2,
+            bytes_accessed=local * length * width * 6,
+            transcendentals=local * heads * length * length * 5 // 8,
+        ),
+        name="attend",
+    )(plane_place(), *raw, *tables, first, *gains)
+    return out[:groups], out[groups]
+
+
+def plane_attend_back(raw, out_grad, totals, tables, first, gains, rows=256):
+    head = tables[0].shape[-1]
+    length = tables[0].shape[1]
+    local, group, table, line, gain = attend_specs(raw, tables, first, length, head)
+    width = raw[0].shape[-1]
+    heads = width // head - 2
+    groups = len(raw)
+    grad_group = pl.BlockSpec((2, 1) + out_grad[0].shape[2:], lambda s: (0, s, 0, 0, 0))
+    out = pl.pallas_call(
+        functools.partial(attend_back_kernel, groups, heads, rows),
+        grid=(local,),
+        out_shape=[jax.ShapeDtypeStruct(raw[0].shape, jnp.bfloat16)] * groups
+        + [jax.ShapeDtypeStruct((local, 2, head), jnp.float32)],
+        in_specs=[pl.BlockSpec(memory_space=pltpu.SMEM)]
+        + [group] * groups
+        + [grad_group] * groups
+        + [pl.BlockSpec((1,) + totals.shape[1:], lambda s: (s, 0, 0))]
+        + [table, table, line, gain, gain],
+        out_specs=[group] * groups + [pl.BlockSpec((1, 2, head), lambda s: (s, 0, 0))],
+        scratch_shapes=[
+            pltpu.VMEM((length, width), jnp.float32),
+            pltpu.VMEM((length, width), jnp.bfloat16),
+            pltpu.VMEM((length, heads * head), jnp.bfloat16),
+            pltpu.VMEM((length, heads * head), jnp.float32),
+            pltpu.VMEM((length, head), jnp.float32),
+            pltpu.VMEM((length, head), jnp.float32),
+            pltpu.VMEM((length, width), jnp.bfloat16),
+        ],
+        compiler_params=pltpu.CompilerParams(vmem_limit_bytes=56 * 1024 * 1024),
+        cost_estimate=pl.CostEstimate(
+            flops=local * heads * length * length * head * 25 // 4,
+            bytes_accessed=local * length * width * 8,
+            transcendentals=local * heads * length * length * 5 // 8,
+        ),
+        name="attend_back",
+    )(plane_place(), *raw, *out_grad, totals, *tables, first, *gains)
+    return out[:groups], jnp.sum(out[groups], axis=0)
+
+
+def plane_plan(
+    tokens,
+    segment_ids,
+    attn_gain,
+    query_gain,
+    key_gain,
+    query_weight,
+    key_matrix,
+    value_matrix,
+    out_weight,
+    mlp_gain,
+    gate_weight,
+    up_weight,
+    down_weight,
+    cotangent,
+):
+    layers = attn_gain.shape[0]
+    head = query_gain.shape[-1]
+    size, line = lax.axis_size("fsdp"), lax.axis_size("tp")
+    local = size // line
+    segments = plane_segments(segment_ids)
+    length = segments.shape[1]
+    positions = jax.vmap(positions_of)(segments)
+    first = (jnp.arange(length, dtype=jnp.int32)[None] - positions).reshape(local, 1, length)
+    cosine_table, sine_table = rope_tables(positions.reshape(-1), head)
+    turned_sign = jnp.where(jnp.arange(head) < head // 2, -1.0, 1.0)
+    tables = (
+        cosine_table.reshape(local, length, head),
+        (sine_table * turned_sign).reshape(local, length, head),
+    )
+    query_count = query_weight.shape[2] * line // size
+    key_count = key_matrix.shape[2] * line // size
+    split = query_count + 2 * key_count
+
+    def pairs_of(pieces):
+        return [jnp.concatenate(pieces[d : d + 2]) for d in range(0, size, 2)]
+
+    def piece(pairs, d):
+        half = pairs[d // 2].shape[0] // 2
+        return pairs[d // 2][half * (d % 2) : half * (d % 2 + 1)]
+
+    def dot(left, right):
+        return jnp.dot(left, right, preferred_element_type=jnp.float32)
+
+    attn_sets, attn_gathered, hidden_sets = ([None] * layers for _ in range(3))
+
+    def fetch_attn(index, token):
+        shards = (query_weight[index], key_matrix[index], value_matrix[index], out_weight[index])
+        attn_sets[index], attn_gathered[index] = attention_weights(*after(token, *shards))
+
+    def shard_hidden(index, start, done):
+        shards = jnp.stack([gate_weight[index].T, up_weight[index].T, down_weight[index]])
+        return swap(shards, 1, 2, start, done)
+
+    fetch_attn(0, segment_ids)
+    first_rows = swap(tokens, 0, 0)
+    residual = line_rows(first_rows)
+    residual = wide(residual)
+    grad = None
+    saved = []
+    for index in range(layers):
+        pack = attn_sets[index]
+        gains = (query_gain[index][None], key_gain[index][None])
+        normed, attn_back = jax.vjp(rms_scale, residual, attn_gain[index])
+        pieces = gather_plane(low(normed))
+        if index == 0:
+            shards = shard_hidden(0, first_rows, pieces[1])
+            hidden_sets[0] = line_gather(after(attn_gathered[0], shards)[0], 1)
+            pieces[6:] = after(shards, *pieces[6:])
+        rows = pairs_of(pieces)
+        raw = [grouped(contract_cols(v, pack[:split]), local, line) for v in rows]
+        if index + 1 < layers:
+            fetch_attn(index + 1, raw[0])
+        mixed, totals = plane_attend(raw, tables, first, gains)
+        mixed = [v.reshape(-1, query_count) for v in mixed]
+        if index == 0:
+            grad = swap(cotangent, 0, 0, raw[0])
+            mixed = after(grad, *mixed)
+        total, *_ = reduce_plane(lambda d: dot(piece(mixed, d), pack[split:]))
+        middle = residual + total
+        if index == 0:
+            grad = line_rows(grad, mixed[0])
+            middle, grad = lax.optimization_barrier((middle, grad))
+            grad = wide(grad)
+        gate_rows, up_rows, down_rows = hidden_sets[index]
+        normed, mlp_back = jax.vjp(rms_scale, middle, mlp_gain[index])
+        mlp_rows = pairs_of(gather_plane(low(normed)))
+        hidden, swiglu_backs = [], []
+        for v in mlp_rows:
+            gate, upward = contract_cols(v, gate_rows), contract_cols(v, up_rows)
+            units, swiglu_back = jax.vjp(swiglu, gate, upward)
+            hidden.append(low(units))
+            swiglu_backs.append(swiglu_back)
+        if index + 1 < layers:
+            shards = shard_hidden(index + 1, mlp_rows[-1], None)
+            hidden_sets[index + 1] = line_gather(shards, 1)
+            hidden = list(after(shards, *hidden))
+        total, *_ = reduce_plane(lambda d: dot(piece(hidden, d), down_rows))
+        residual = middle + total
+        saved.append(
+            (attn_back, rows, raw, mixed, totals, mlp_back, mlp_rows, swiglu_backs, hidden)
+        )
+    result = residual
+    pack_grads, pack_sums, gain_grads, hidden_sums, hidden_grads = (
+        [None] * layers for _ in range(5)
+    )
+    for index in reversed(range(layers)):
+        pack = attn_sets[index]
+        gains = (query_gain[index][None], key_gain[index][None])
+        gate_rows, up_rows, down_rows = hidden_sets[index]
+        attn_back, rows, raw, mixed, totals, mlp_back, mlp_rows, swiglu_backs, hidden = saved[index]
+        if index + 1 == layers:
+            (grad,) = after(tuple(mlp_rows), grad)
+        grad_rows = pairs_of(gather_plane(low(grad)))
+        gate_grads, up_grads = [], []
+        for v, swiglu_back in zip(grad_rows, swiglu_backs):
+            gate_grad, up_grad = swiglu_back(contract_cols(v, down_rows))
+            gate_grads.append(low(gate_grad))
+            up_grads.append(low(up_grad))
+        if index + 1 == layers:
+            gate_grads = after(result, *gate_grads)
+        normed_grad, token, token_next = reduce_plane(
+            lambda d: dot(piece(gate_grads, d), gate_rows) + dot(piece(up_grads, d), up_rows)
+        )
+        hidden, grad_rows = (after(token, *v) for v in (hidden, grad_rows))
+        gate_grads, up_grads, mlp_rows = (
+            after(token_next, *v) for v in (gate_grads, up_grads, mlp_rows)
+        )
+        all_grads, all_rows = jnp.concatenate(grad_rows), jnp.concatenate(mlp_rows)
+        terms = [
+            low(contract_rows(jnp.concatenate(gate_grads), all_rows)),
+            low(contract_rows(jnp.concatenate(up_grads), all_rows)),
+            low(contract_rows(jnp.concatenate(hidden), all_grads)),
+        ]
+        normed_grad, *terms = lax.optimization_barrier((normed_grad, *terms))
+        if index + 1 < layers:
+            done = hidden_sums[index + 1]
+            above = swap(pack_grads[index + 1][None], 2, 0, grad_rows[-1])
+            result = swap(result, 0, 0, grad_rows[-1])
+            normed_grad, above, result = lax.optimization_barrier((normed_grad, above, result))
+            pack_sums[index + 1] = line_reduce(after(done, above)[0])
+            terms = after(done, *terms)
+        hidden_sums[index] = line_reduce(jnp.stack(terms), 1)
+        grad_part, mlp_gain_grad = mlp_back(normed_grad)
+        grad = grad + grad_part
+        grad_rows = pairs_of(gather_plane(low(grad)))
+        mixed_grad = [
+            grouped(low(contract_cols(v, pack[split:])), local, line) for v in grad_rows
+        ]
+        raw_grad, head_gain_grads = plane_attend_back(raw, mixed_grad, totals, tables, first, gains)
+        if index + 1 < layers:
+            hidden_grads[index + 1] = swap(hidden_sums[index + 1], 2, 1, mixed_grad[-1])
+            raw_grad = after(hidden_grads[index + 1], *raw_grad)
+        raw_grad = [v.reshape(-1, split) for v in raw_grad]
+        normed_grad, token, token_next = reduce_plane(lambda d: dot(piece(raw_grad, d), pack[:split]))
+        mixed, grad_rows = (after(token, *v) for v in (mixed, grad_rows))
+        raw_grad, rows = (after(token_next, *v) for v in (raw_grad, rows))
+        pack_grad = jnp.concatenate(
+            [
+                low(contract_rows(jnp.concatenate(raw_grad), jnp.concatenate(rows))),
+                low(contract_rows(jnp.concatenate(mixed), jnp.concatenate(grad_rows))),
+            ]
+        )
+        normed_grad, pack_grad = lax.optimization_barrier((normed_grad, pack_grad))
+        pack_grads[index] = pack_grad
+        if index + 1 == layers:
+            result = line_rows_back(low(result), raw_grad[0])
+            normed_grad, result = lax.optimization_barrier((normed_grad, result))
+        grad_part, attn_gain_grad = attn_back(normed_grad)
+        grad = grad + grad_part
+        gain_grads[index] = jnp.concatenate(
+            [attn_gain_grad, mlp_gain_grad, head_gain_grads[0], head_gain_grads[1]]
+        )
+    token_grad = wide(swap(line_rows_back(low(grad)), 0, 0))
+    below = swap(pack_grads[0][None], 2, 0)
+    pack_sums[0] = line_reduce(after((hidden_sums[0], pack_sums[1:]), below)[0])
+    hidden_grads[0] = swap(hidden_sums[0], 2, 1)
+    kinds = wide(jnp.stack(hidden_grads, 1))
+    hidden_stacks = (kinds[0].swapaxes(1, 2), kinds[1].swapaxes(1, 2), kinds[2])
+    marks = (0, query_count, query_count + key_count, split, pack_sums[0].shape[1])
+    kinds = [
+        jnp.stack(
+            [wide(v[:, low_mark:high_mark]).reshape(-1, v.shape[-1]) for v in pack_sums]
+        )
+        for low_mark, high_mark in zip(marks, marks[1:])
+    ]
+    weight_stacks = [v.swapaxes(1, 2) for v in kinds[:3]] + kinds[3:]
+    width = attn_gain.shape[1]
+    gain_stack = reduce_all(jnp.stack(gain_grads).reshape(-1, head)).reshape(layers, -1)
+    attn_sum, mlp_sum, query_sum, key_sum = (
+        gain_stack[:, :width],
+        gain_stack[:, width : 2 * width],
+        gain_stack[:, 2 * width : 2 * width + head],
+        gain_stack[:, 2 * width + head :],
+    )
+    return (
+        result,
+        token_grad,
+        attn_sum,
+        query_sum,
+        key_sum,
+        *weight_stacks,
+        mlp_sum,
+        *hidden_stacks,
+    )
+
+
+def plane_fits(mesh, shapes):
+    size, line = mesh.shape["fsdp"], mesh.shape["tp"]
+    heads = shapes[6].shape[2] // shapes[4].shape[1]
+    return size == 8 and heads == size and size % line == 0 and shapes[1].shape[0] == size
+
+
 def solution(mesh):
     placed = (
         P(("fsdp", "tp"), None),
@@ -436,8 +1075,9 @@
         P(None, "tp", "fsdp"),
         P(("fsdp", "tp"), None),
     )
-    return jax.shard_map(
-        on_device,
+    def mapped(plan):
+      return jax.shard_map(
+        plan,
         mesh=mesh,
         in_specs=placed,
         out_specs=(
@@ -457,3 +1097,8 @@
         ),
         check_vma=False,
     )
+
+    def whole(*args):
+        return mapped(plane_plan if plane_fits(mesh, args) else general_plan)(*args)
+
+    return whole

time: 2780 us -> 1580 us (0.57)
  waiting for transfers between devices: 2070 us -> 734 us
  starting transfers between devices: 3.39 us -> 197 us
  matrix products: 411 us -> 280 us
  Pallas kernels: 0 us -> 89.1 us
  blocking collectives: 40.7 us -> 0 us
  between operations: 16.5 us -> 50.1 us
  other arithmetic: 120 us -> 90.3 us
    reduce_scatter x22 -> x4, waiting for transfers between devices: 1200 us -> 38.6 us  [line_reduce(): return lax.psum_scatter(terms, 'tp', scatter_dimension=axis, tiled=True)]
    all_gather x22 -> x4, waiting for transfers between devices: 862 us -> 0.01 us  [line_gather(): return lax.all_gather(own, 'tp', axis=axis, tiled=True)]
    ppermute x0 -> x232, waiting for transfers between devices: none -> 696 us  [the longest x218 548 us: plane_send(): lax.ppermute(values, 'fsdp', [(i, i ^ distance) for i in range(size)])]
    ppermute x0 -> x232, starting transfers between devices: none -> 195 us  [the longest x218 178 us: plane_send(): lax.ppermute(values, 'fsdp', [(i, i ^ distance) for i in range(size)])]
    dot_general x42 -> x80, matrix products: 213 us -> 93.6 us  [dot(): return jnp.dot(left, right, preferred_element_type=jnp.float32)]
    pallas_call x0 -> x20, Pallas kernels: none -> 89.1 us  [the longest x2 43.6 us: plane_attend_back(): pl.pallas_call(functools.partial(attend_back_kernel, groups, heads, rows)...]
    psum x1 -> x0, blocking collectives: 40.7 us -> none  [on_device(): lax.psum((gain_stacks[0], gain_stacks[1], gain_stacks[2], gain_stacks[3])...]
    unnamed x304 -> x529, local copies, waits for them, and re-layouts: 39 us -> 66.6 us
  transfers between devices with their start and end apart: 44 -> 240, of which waited for: 40 -> 91; matrix products, arithmetic and copies ran while one was open for 15% -> 28% of each run, Pallas kernels for 0% -> 4%
where the time goes in v1:
time: 1580 us; the launch traced here: 1570 us
  waiting for transfers between devices  734 us (46%)
  matrix products  280 us (18%)
  starting transfers between devices  197 us (12%)
  local copies, waits for them, and re-layouts  131 us (8%)
  other arithmetic  90.3 us (6%)
  Pallas kernels  89.1 us (6%)
  between operations  50.1 us (3%)
    ppermute x218, waiting for transfers between devices, plane_send(): lax.ppermute(values, 'fsdp', [(i, i ^ distance) for i in range(size)])  548 us
    ppermute x218, starting transfers between devices, plane_send(): lax.ppermute(values, 'fsdp', [(i, i ^ distance) for i in range(size)])  178 us
    ppermute x12, waiting for transfers between devices, line_swap(): moved.append(lax.ppermute(piece, 'tp', pairs))  108 us
    dot_general x40, matrix products, contract_cols(): lax.dot_general(left_side, right_side, (((1,), (1,)), ((), ())), preferre...  106 us
    dot_general x80, matrix products, dot(): return jnp.dot(left, right, preferred_element_type=jnp.float32)  93.6 us
    dot_general x10, matrix products, contract_rows(): lax.dot_general(left_side, right_side, (((0,), (0,)), ((), ())), preferre...  80.3 us
    unnamed x529, local copies, waits for them, and re-layouts  66.6 us
    pallas_call x2, Pallas kernels, plane_attend_back(): pl.pallas_call(functools.partial(attend_back_kernel, groups, heads, rows)...  43.6 us
  transfers between devices with their start and end apart: 240, of which 91 were waited for; matrix products, arithmetic and copies ran while one was open for 28% of the time, Pallas kernels for 4%

profile of v1, /device:TPU:8, one launch (start us, length us, event | category | flops | bytes accessed | tf_op | source)
XLA Modules:
  0.0 1571.5 jit_solution(16032027787548746081)
XLA Ops:
  49.7 16.2 %collective-permute-done.7.refs_1_ = bf16[64,2048]{1,0:T(8,128)(2,1)S(1)} collective-permute-done((bf16[64,2048]{1,0:T(8,128)(2,1)S(1)}, bf16[64,2048]{1,0:T(8,128)(2,1)S(1)}, u32[]{:S(2)}, u32[]{:S(2)}) %collective-permute-start.7) | collective-permute-done | bytes 262176 | tf_op jit(solution)/shard_map/ppermute | solution.py:560
  68.2 26.5 %collective-permute-done.8.refs_2_ = bf16[64,2048]{1,0:T(8,128)(2,1)S(1)} collective-permute-done((bf16[64,2048]{1,0:T(8,128)(2,1)S(1)}, bf16[64,2048]{1,0:T(8,128)(2,1)S(1)}, u32[]{:S(2)}, u32[]{:S(2)}) %collective-permute-start.8) | collective-permute-done | bytes 262176 | tf_op jit(solution)/shard_map/ppermute | solution.py:560
  135.3 23.1 %collective-permute-done.34.refs_6_ = bf16[3,192,256]{2,1,0:T(8,128)(2,1)S(1)} collective-permute-done((bf16[3,192,256]{2,1,0:T(8,128)(2,1)}, bf16[3,192,256]{2,1,0:T(8,128)(2,1)S(1)}, u32[]{:S(2)}, u32[]{:S(2)}) %collective-permute-start.34) | collective-permute-done | bytes 294944 | tf_op jit(solution)/shard_map/ppermute | solution.py:427
  212.7 19.1 %collective-permute-done.15.refs_5_ = bf16[1,768,256]{2,1,0:T(8,128)(2,1)S(1)} collective-permute-done((bf16[1,768,256]{2,1,0:T(8,128)(2,1)S(1)}, bf16[1,768,256]{2,1,0:T(8,128)(2,1)S(1)}, u32[]{:S(2)}, u32[]{:S(2)}) %collective-permute-start.15) | collective-permute-done | bytes 393248 | tf_op jit(solution)/shard_map/ppermute | solution.py:427
  245.4 13.0 attend.2
  285.6 13.2 collective-permute-done.50.refs_1_
  299.8 32.3 %collective-permute-done.51.refs_2_ = bf16[64,2048]{1,0:T(8,128)(2,1)S(1)} collective-permute-done((bf16[64,2048]{1,0:T(8,128)(2,1)S(1)}, bf16[64,2048]{1,0:T(8,128)(2,1)S(1)}, u32[]{:S(2)}, u32[]{:S(2)}) %collective-permute-start.51) | collective-permute-done | bytes 262176 | tf_op jit(solution)/shard_map/ppermute | solution.py:560
  341.2 22.3 %collective-permute-done.53 = bf16[256,2048]{1,0:T(8,128)(2,1)S(1)} collective-permute-done((bf16[256,2048]{1,0:T(8,128)(2,1)S(1)}, bf16[256,2048]{1,0:T(8,128)(2,1)S(1)}, u32[]{:S(2)}, u32[]{:S(2)}) %collective-permute-start.53) | collective-permute-done | bytes 1048608 | tf_op jit(solution)/shard_map/ppermute | solution.py:427
  417.7 13.0 collective-permute-done.62.refs_5_
  497.9 13.9 collective-permute-done.72
  529.9 21.0 %collective-permute-done.80.refs_4_ = bf16[1,768,256]{2,1,0:T(8,128)(2,1)S(1)} collective-permute-done((bf16[1,768,256]{2,1,0:T(8,128)(2,1)S(1)}, bf16[1,768,256]{2,1,0:T(8,128)(2,1)S(1)}, u32[]{:S(2)}, u32[]{:S(2)}) %collective-permute-start.80) | collective-permute-done | bytes 393248 | tf_op jit(solution)/shard_map/ppermute | solution.py:427
  580.1 9.9 collective-permute-done.88
  597.0 13.4 attend.3
  632.5 21.4 %collective-permute-done.95 = bf16[256,2048]{1,0:T(8,128)(2,1)S(1)} collective-permute-done((bf16[256,2048]{1,0:T(8,128)(2,1)S(1)}, bf16[256,2048]{1,0:T(8,128)(2,1)S(1)}, u32[]{:S(2)}, u32[]{:S(2)}) %collective-permute-start.95) | collective-permute-done | bytes 1048608 | tf_op jit(solution)/shard_map/ppermute | solution.py:427
  660.5 20.8 %collective-permute-done.102 = bf16[256,2048]{1,0:T(8,128)(2,1)} collective-permute-done((bf16[256,2048]{1,0:T(8,128)(2,1)S(1)}, bf16[256,2048]{1,0:T(8,128)(2,1)}, u32[]{:S(2)}, u32[]{:S(2)}) %collective-permute-start.102) | collective-permute-done | bytes 1048608 | tf_op jit(solution)/shard_map/ppermute | solution.py:427
  724.3 16.5 %collective-permute-done.118 = bf16[256,2048]{1,0:T(8,128)(2,1)S(1)} collective-permute-done((bf16[256,2048]{1,0:T(8,128)(2,1)S(1)}, bf16[256,2048]{1,0:T(8,128)(2,1)S(1)}, u32[]{:S(2)}, u32[]{:S(2)}) %collective-permute-start.118) | collective-permute-done | bytes 1048608 | tf_op jit(solution)/shard_map/ppermute | solution.py:427
  810.7 16.4 %collective-permute-done.111 = bf16[256,2048]{1,0:T(8,128)(2,1)S(1)} collective-permute-done((bf16[256,2048]{1,0:T(8,128)(2,1)S(1)}, bf16[256,2048]{1,0:T(8,128)(2,1)S(1)}, u32[]{:S(2)}, u32[]{:S(2)}) %collective-permute-start.111) | collective-permute-done | bytes 1048608 | tf_op jit(solution)/shard_map/ppermute | solution.py:427
  841.5 11.4 fusion.51
  872.1 10.6 convolution_convert_fusion.2
  882.7 11.0 convolution_convert_fusion.3
  901.6 22.4 %collective-permute-done.134 = bf16[256,2048]{1,0:T(8,128)(2,1)S(1)} collective-permute-done((bf16[256,2048]{1,0:T(8,128)(2,1)S(1)}, bf16[256,2048]{1,0:T(8,128)(2,1)S(1)}, u32[]{:S(2)}, u32[]{:S(2)}) %collective-permute-start.134) | collective-permute-done | bytes 1048608 | tf_op jit(solution)/shard_map/ppermute | solution.py:427
  942.2 21.7 %attend_back.2 = (bf16[2,2,4,32,512]{4,3,2,1,0:T(8,128)(2,1)}, bf16[2,2,4,32,512]{4,3,2,1,0:T(8,128)(2,1)}, bf16[2,2,4,32,512]{4,3,2,1,0:T(8,128)(2,1)}, bf16[2,2,4,32,512]{4,3,2,1,0:T(8,128)(2,1)}, f32[2,2,128]{2,1,0:T(2,128)}) custom-call(s32[1]{0:T(128)} %bitcast.28.refs_0_, f32[2,2,4,32,512]{4,3,2,1,0:T(8,128)} %copy-done.8, ...), custom_call_target="tpu_custom_call" | custom-call | flops 3355443200 | bytes 8388608 | tf_op jit(solution)/shard_map/attend_back/pallas_call | solution.py:817
  999.9 10.0 collective-permute-done.148.refs_2_
  1130.0 11.3 fusion.48
  1142.9 12.4 collective-permute-done.169.refs_4_
  1224.0 23.4 %collective-permute-done.180 = bf16[256,2048]{1,0:T(8,128)(2,1)S(1)} collective-permute-done((bf16[256,2048]{1,0:T(8,128)(2,1)S(1)}, bf16[256,2048]{1,0:T(8,128)(2,1)S(1)}, u32[]{:S(2)}, u32[]{:S(2)}) %collective-permute-start.180) | collective-permute-done | bytes 1048608 | tf_op jit(solution)/shard_map/ppermute | solution.py:427
  1277.4 21.9 %attend_back.3 = (bf16[2,2,4,32,512]{4,3,2,1,0:T(8,128)(2,1)}, bf16[2,2,4,32,512]{4,3,2,1,0:T(8,128)(2,1)}, bf16[2,2,4,32,512]{4,3,2,1,0:T(8,128)(2,1)}, bf16[2,2,4,32,512]{4,3,2,1,0:T(8,128)(2,1)}, f32[2,2,128]{2,1,0:T(2,128)}) custom-call(s32[1]{0:T(128)} %bitcast.28.refs_0_, f32[2,2,4,32,512]{4,3,2,1,0:T(8,128)} %copy-done.4, ...), custom_call_target="tpu_custom_call" | custom-call | flops 3355443200 | bytes 8388608 | tf_op jit(solution)/shard_map/attend_back/pallas_call | solution.py:817
  1332.1 14.7 collective-permute-done.199
  1370.4 18.4 %collective-permute-done.222.refs_5_ = bf16[1,768,256]{2,1,0:T(8,128)(2,1)S(1)} collective-permute-done((bf16[1,768,256]{2,1,0:T(8,128)(2,1)S(1)}, bf16[1,768,256]{2,1,0:T(8,128)(2,1)S(1)}, u32[]{:S(2)}, u32[]{:S(2)}) %collective-permute-start.222) | collective-permute-done | bytes 393248 | tf_op jit(solution)/shard_map/ppermute | solution.py:427
  1391.3 38.6 %reduce-scatter.7.cloned.1.call-done = bf16[3,192,2048]{2,1,0:T(8,128)(2,1)} async-done(((bf16[3,768,2048]{2,1,0:T(8,128)(2,1)}), bf16[3,192,2048]{2,1,0:T(8,128)(2,1)}) %reduce-scatter.7.cloned.1.call-update) | async-done | bytes 2359312 | tf_op jit(solution)/shard_map/reduce_scatter | solution.py:507
  1453.3 22.0 %collective-permute-done.216 = f32[68,128]{1,0:T(8,128)S(1)} collective-permute-done((f32[68,128]{1,0:T(8,128)S(1)}, f32[68,128]{1,0:T(8,128)S(1)}, u32[]{:S(2)}, u32[]{:S(2)}) %collective-permute-start.216) | collective-permute-done | bytes 34848 | tf_op jit(solution)/shard_map/ppermute | solution.py:491
  1475.2 18.0 %collective-permute-done.217 = f32[68,128]{1,0:T(8,128)S(1)} collective-permute-done((f32[68,128]{1,0:T(8,128)S(1)}, f32[68,128]{1,0:T(8,128)S(1)}, u32[]{:S(2)}, u32[]{:S(2)}) %collective-permute-start.217) | collective-permute-done | bytes 34848 | tf_op jit(solution)/shard_map/ppermute | solution.py:491
  (1394 shorter events, 941.7 us)
Async XLA Ops:
  7.2 159.4 %all-gather.5.cloned.1.call-start = ((), (), s32[]{:S(2)}) async-start(), calls=%async_computation.4 | async-start | bytes 3932160 | tf_op jit(solution)/shard_map/all_gather | solution.py:503
  22.4 410.6 %all-gather.7.cloned.1.call-start = ((), (), s32[]{:S(2)}) async-start(), calls=%async_computation.5 | async-start | bytes 11796480 | tf_op jit(solution)/shard_map/all_gather | solution.py:503
  45.0 49.8 %collective-permute-start.8 = (bf16[64,2048]{1,0:T(8,128)(2,1)S(1)}, bf16[64,2048]{1,0:T(8,128)(2,1)S(1)}, u32[]{:S(2)}, u32[]{:S(2)}) collective-permute-start(bf16[64,2048]{1,0:T(8,128)(2,1)S(1)} %get-tuple-element.547), channel_id=1, source_target_pairs={{0,2},{1,3},{2,0},{3,1},{4,6},{5,7},{6,4},{7,5},{8,10},{9,11},{10,... | collective-permute-start | bytes 786440 | tf_op jit(solution)/shard_map/ppermute | solution.py:560
  46.2 51.8 %collective-permute-start.9 = (bf16[64,2048]{1,0:T(8,128)(2,1)S(1)}, bf16[64,2048]{1,0:T(8,128)(2,1)S(1)}, u32[]{:S(2)}, u32[]{:S(2)}) collective-permute-start(bf16[64,2048]{1,0:T(8,128)(2,1)S(1)} %get-tuple-element.546), channel_id=1, source_target_pairs={{0,3},{1,0},{2,1},{3,2},{4,7},{5,4},{6,5},{7,6},{8,11},{9,8},{10,9... | collective-permute-start | bytes 786440 | tf_op jit(solution)/shard_map/ppermute | solution.py:560
  48.0 68.0 %collective-permute-start.41 = (s32[4,1024]{1,0:T(4,128)S(1)}, s32[4,1024]{1,0:T(4,128)S(1)}, u32[]{:S(2)}, u32[]{:S(2)}) collective-permute-start(s32[4,1024]{1,0:T(4,128)S(1)} %pad_add_fusion.1), channel_id=1, source_target_pairs={{0,16},{4,20},{8,24},{12,28},{16,0},{20,4},{24,8},{28,12},{1,17},{... | collective-permute-start | bytes 49160 | tf_op jit(solution)/shard_map/ppermute | solution.py:427
  49.7 69.4 %collective-permute-start.29 = (bf16[3,192,256]{2,1,0:T(8,128)(2,1)}, bf16[3,192,256]{2,1,0:T(8,128)(2,1)S(1)}, u32[]{:S(2)}, u32[]{:S(2)}) collective-permute-start(bf16[3,192,256]{2,1,0:T(8,128)(2,1)} %get-tuple-element.484), channel_id=1, source_target_pairs={{0,4},{4,0},{8,12},{12,8},{16,20},{20,16},{24,28},{28,24},{1,5},{5... | collective-permute-start | bytes 884744 | tf_op jit(solution)/shard_map/ppermute | solution.py:427
  65.9 53.8 %collective-permute-start.30 = (bf16[3,192,256]{2,1,0:T(8,128)(2,1)}, bf16[3,192,256]{2,1,0:T(8,128)(2,1)S(1)}, u32[]{:S(2)}, u32[]{:S(2)}) collective-permute-start(bf16[3,192,256]{2,1,0:T(8,128)(2,1)} %get-tuple-element.483), channel_id=1, source_target_pairs={{0,8},{4,12},{8,0},{12,4},{16,24},{20,28},{24,16},{28,20},{1,9},{5... | collective-permute-start | bytes 884744 | tf_op jit(solution)/shard_map/ppermute | solution.py:427
  100.8 63.5 %collective-permute-start.10 = (bf16[256,2048]{1,0:T(8,128)(2,1)}, bf16[256,2048]{1,0:T(8,128)(2,1)}, u32[]{:S(2)}, u32[]{:S(2)}) collective-permute-start(bf16[256,2048]{1,0:T(8,128)(2,1)} %multiply_convert_fusion.3), channel_id=1, source_target_pairs={{0,4},{4,0},{8,12},{12,8},{16,20},{20,16},{24,28},{28,24},{1,5},{5... | collective-permute-start | bytes 3145736 | tf_op jit(solution)/shard_map/ppermute | solution.py:427
  119.7 49.2 %collective-permute-start.27 = (bf16[256,2048]{1,0:T(8,128)(2,1)}, bf16[256,2048]{1,0:T(8,128)(2,1)S(1)}, u32[]{:S(2)}, u32[]{:S(2)}) collective-permute-start(bf16[256,2048]{1,0:T(8,128)(2,1)} %multiply_convert_fusion.3), channel_id=1, source_target_pairs={{0,16},{4,20},{8,24},{12,28},{16,0},{20,4},{24,8},{28,12},{1,17},{... | collective-permute-start | bytes 3145736 | tf_op jit(solution)/shard_map/ppermute | solution.py:427
  125.8 48.6 %collective-permute-start.25 = (bf16[256,2048]{1,0:T(8,128)(2,1)}, bf16[256,2048]{1,0:T(8,128)(2,1)}, u32[]{:S(2)}, u32[]{:S(2)}) collective-permute-start(bf16[256,2048]{1,0:T(8,128)(2,1)} %multiply_convert_fusion.3), channel_id=1, source_target_pairs={{0,8},{4,12},{8,0},{12,4},{16,24},{20,28},{24,16},{28,20},{1,9},{5... | collective-permute-start | bytes 3145736 | tf_op jit(solution)/shard_map/ppermute | solution.py:427
  166.6 322.6 %all-gather.9.cloned.1.call-start = ((), (), s32[]{:S(2)}) async-start(), calls=%async_computation.6 | async-start | bytes 3932160 | tf_op jit(solution)/shard_map/all_gather | solution.py:503
  260.7 76.1 %collective-permute-start.42 = (bf16[256,2048]{1,0:T(8,128)(2,1)S(1)}, bf16[256,2048]{1,0:T(8,128)(2,1)S(1)}, u32[]{:S(2)}, u32[]{:S(2)}) collective-permute-start(bf16[256,2048]{1,0:T(8,128)(2,1)S(1)} %convolution_convert_fusion.19), channel_id=1, source_target_pairs={{0,4},{4,0},{8,12},{12,8},{16,20},{20,16},{24,28},{28,24},{1,5},{5... | collective-permute-start | bytes 3145736 | tf_op jit(solution)/shard_map/ppermute | solution.py:427
  277.6 59.2 %collective-permute-start.46 = (bf16[256,2048]{1,0:T(8,128)(2,1)S(1)}, bf16[256,2048]{1,0:T(8,128)(2,1)S(1)}, u32[]{:S(2)}, u32[]{:S(2)}) collective-permute-start(bf16[256,2048]{1,0:T(8,128)(2,1)S(1)} %pad_maximum_fusion.15), channel_id=1, source_target_pairs={{0,8},{4,12},{8,0},{12,4},{16,24},{20,28},{24,16},{28,20},{1,9},{5... | collective-permute-start | bytes 3145736 | tf_op jit(solution)/shard_map/ppermute | solution.py:427
  280.9 56.0 %collective-permute-start.49 = (bf16[256,2048]{1,0:T(8,128)(2,1)S(1)}, bf16[256,2048]{1,0:T(8,128)(2,1)S(1)}, u32[]{:S(2)}, u32[]{:S(2)}) collective-permute-start(bf16[256,2048]{1,0:T(8,128)(2,1)S(1)} %pad_maximum_fusion.16), channel_id=1, source_target_pairs={{0,16},{4,20},{8,24},{12,28},{16,0},{20,4},{24,8},{28,12},{1,17},{... | collective-permute-start | bytes 3145736 | tf_op jit(solution)/shard_map/ppermute | solution.py:427
  282.0 50.1 %collective-permute-start.51 = (bf16[64,2048]{1,0:T(8,128)(2,1)S(1)}, bf16[64,2048]{1,0:T(8,128)(2,1)S(1)}, u32[]{:S(2)}, u32[]{:S(2)}) collective-permute-start(bf16[64,2048]{1,0:T(8,128)(2,1)S(1)} %get-tuple-element.531), channel_id=1, source_target_pairs={{0,2},{1,3},{2,0},{3,1},{4,6},{5,7},{6,4},{7,5},{8,10},{9,11},{10,... | collective-permute-start | bytes 786440 | tf_op jit(solution)/shard_map/ppermute | solution.py:560
  393.1 296.0 %all-gather.11.cloned.1.call-start = ((), (), s32[]{:S(2)}) async-start(), calls=%async_computation.7 | async-start | bytes 11796480 | tf_op jit(solution)/shard_map/all_gather | solution.py:503
  493.6 712.5 %reduce-scatter.5.cloned.1.call-start = ((), (), s32[]{:S(2)}) async-start(), calls=%async_computation.8 | async-start | bytes 11796480 | tf_op jit(solution)/shard_map/reduce_scatter | solution.py:507
  515.5 59.9 %collective-permute-start.86 = (bf16[256,2048]{1,0:T(8,128)(2,1)S(1)}, bf16[256,2048]{1,0:T(8,128)(2,1)S(1)}, u32[]{:S(2)}, u32[]{:S(2)}) collective-permute-start(bf16[256,2048]{1,0:T(8,128)(2,1)S(1)} %multiply_convert_fusion.1), channel_id=1, source_target_pairs={{0,16},{4,20},{8,24},{12,28},{16,0},{20,4},{24,8},{28,12},{1,17},{... | collective-permute-start | bytes 3145736 | tf_op jit(solution)/shard_map/ppermute | solution.py:427
  517.1 59.6 %collective-permute-start.84 = (bf16[256,2048]{1,0:T(8,128)(2,1)S(1)}, bf16[256,2048]{1,0:T(8,128)(2,1)S(1)}, u32[]{:S(2)}, u32[]{:S(2)}) collective-permute-start(bf16[256,2048]{1,0:T(8,128)(2,1)S(1)} %multiply_convert_fusion.1), channel_id=1, source_target_pairs={{0,8},{4,12},{8,0},{12,4},{16,24},{20,28},{24,16},{28,20},{1,9},{5... | collective-permute-start | bytes 3145736 | tf_op jit(solution)/shard_map/ppermute | solution.py:427
  518.0 59.1 %collective-permute-start.76 = (bf16[256,2048]{1,0:T(8,128)(2,1)S(1)}, bf16[256,2048]{1,0:T(8,128)(2,1)S(1)}, u32[]{:S(2)}, u32[]{:S(2)}) collective-permute-start(bf16[256,2048]{1,0:T(8,128)(2,1)S(1)} %multiply_convert_fusion.1), channel_id=1, source_target_pairs={{0,4},{4,0},{8,12},{12,8},{16,20},{20,16},{24,28},{28,24},{1,5},{5... | collective-permute-start | bytes 3145736 | tf_op jit(solution)/shard_map/ppermute | solution.py:427
  750.5 60.1 %collective-permute-start.107 = (bf16[256,2048]{1,0:T(8,128)(2,1)S(1)}, bf16[256,2048]{1,0:T(8,128)(2,1)S(1)}, u32[]{:S(2)}, u32[]{:S(2)}) collective-permute-start(bf16[256,2048]{1,0:T(8,128)(2,1)S(1)} %convolution_convert_fusion.23), channel_id=1, source_target_pairs={{0,4},{4,0},{8,12},{12,8},{16,20},{20,16},{24,28},{28,24},{1,5},{5... | collective-permute-start | bytes 3145736 | tf_op jit(solution)/shard_map/ppermute | solution.py:427
  835.4 58.3 %collective-permute-start.123 = (bf16[256,2048]{1,0:T(8,128)(2,1)S(1)}, bf16[256,2048]{1,0:T(8,128)(2,1)}, u32[]{:S(2)}, u32[]{:S(2)}) collective-permute-start(bf16[256,2048]{1,0:T(8,128)(2,1)S(1)} %fusion.127), channel_id=1, source_target_pairs={{0,4},{4,0},{8,12},{12,8},{16,20},{20,16},{24,28},{28,24},{1,5},{5... | collective-permute-start | bytes 3145736 | tf_op jit(solution)/shard_map/ppermute | solution.py:427
  969.1 44.2 %collective-permute-start.139 = (bf16[256,2048]{1,0:T(8,128)(2,1)}, bf16[256,2048]{1,0:T(8,128)(2,1)S(1)}, u32[]{:S(2)}, u32[]{:S(2)}) collective-permute-start(bf16[256,2048]{1,0:T(8,128)(2,1)} %convolution_convert_fusion.11), channel_id=1, source_target_pairs={{0,4},{4,0},{8,12},{12,8},{16,20},{20,16},{24,28},{28,24},{1,5},{5... | collective-permute-start | bytes 3145736 | tf_op jit(solution)/shard_map/ppermute | solution.py:427
  1035.9 355.3 %reduce-scatter.9.cloned.1.call-start = ((), (), s32[]{:S(2)}) async-start(), calls=%async_computation.10 | async-start | bytes 3932160 | tf_op jit(solution)/shard_map/reduce_scatter | solution.py:507
  1114.9 49.4 %collective-permute-start.160 = (bf16[128,2048]{1,0:T(8,128)(2,1)}, bf16[128,2048]{1,0:T(8,128)(2,1)}, u32[]{:S(2)}, u32[]{:S(2)}) collective-permute-start(bf16[128,2048]{1,0:T(8,128)(2,1)} %get-tuple-element.514), channel_id=1, source_target_pairs={{0,16},{4,20},{8,24},{12,28},{16,0},{20,4},{24,8},{28,12},{1,17},{... | collective-permute-start | bytes 1572872 | tf_op jit(solution)/shard_map/ppermute | solution.py:427
  1117.0 44.1 %collective-permute-start.170 = (bf16[1,768,256]{2,1,0:T(8,128)(2,1)S(1)}, bf16[1,768,256]{2,1,0:T(8,128)(2,1)S(1)}, u32[]{:S(2)}, u32[]{:S(2)}) collective-permute-start(bf16[1,768,256]{2,1,0:T(8,128)(2,1)S(1)} %get-tuple-element.412), channel_id=1, source_target_pairs={{0,20},{4,16},{8,28},{12,24},{16,4},{20,0},{24,12},{28,8},{1,21},{... | collective-permute-start | bytes 1179656 | tf_op jit(solution)/shard_map/ppermute | solution.py:427
  1155.2 45.1 %collective-permute-start.151 = (bf16[256,2048]{1,0:T(8,128)(2,1)}, bf16[256,2048]{1,0:T(8,128)(2,1)}, u32[]{:S(2)}, u32[]{:S(2)}) collective-permute-start(bf16[256,2048]{1,0:T(8,128)(2,1)} %fusion.134), channel_id=1, source_target_pairs={{0,4},{4,0},{8,12},{12,8},{16,20},{20,16},{24,28},{28,24},{1,5},{5... | collective-permute-start | bytes 3145736 | tf_op jit(solution)/shard_map/ppermute | solution.py:427
  1206.2 223.7 %reduce-scatter.7.cloned.1.call-start = ((), (), s32[]{:S(2)}) async-start(), calls=%async_computation.9 | async-start | bytes 11796480 | tf_op jit(solution)/shard_map/reduce_scatter | solution.py:507
  1215.7 342.4 %reduce-scatter.11.cloned.1.call-start = ((), (), s32[]{:S(2)}) async-start(), calls=%async_computation.11 | async-start | bytes 3932160 | tf_op jit(solution)/shard_map/reduce_scatter | solution.py:507
  1437.0 56.2 %collective-permute-start.203 = (bf16[64,2048]{1,0:T(8,128)(2,1)}, bf16[64,2048]{1,0:T(8,128)(2,1)S(1)}, u32[]{:S(2)}, u32[]{:S(2)}) collective-permute-start(bf16[64,2048]{1,0:T(8,128)(2,1)} %get-tuple-element.502), channel_id=1, source_target_pairs={{0,1},{1,2},{2,3},{3,0},{4,5},{5,6},{6,7},{7,4},{8,9},{9,10},{10,1... | collective-permute-start | bytes 786440 | tf_op jit(solution)/shard_map/ppermute | solution.py:560
  1439.6 53.7 %collective-permute-start.204 = (bf16[64,2048]{1,0:T(8,128)(2,1)}, bf16[64,2048]{1,0:T(8,128)(2,1)S(1)}, u32[]{:S(2)}, u32[]{:S(2)}) collective-permute-start(bf16[64,2048]{1,0:T(8,128)(2,1)} %get-tuple-element.501), channel_id=1, source_target_pairs={{0,2},{1,3},{2,0},{3,1},{4,6},{5,7},{6,4},{7,5},{8,10},{9,11},{10,... | collective-permute-start | bytes 786440 | tf_op jit(solution)/shard_map/ppermute | solution.py:560
  1440.2 53.1 %collective-permute-start.205 = (bf16[64,2048]{1,0:T(8,128)(2,1)}, bf16[64,2048]{1,0:T(8,128)(2,1)S(1)}, u32[]{:S(2)}, u32[]{:S(2)}) collective-permute-start(bf16[64,2048]{1,0:T(8,128)(2,1)} %get-tuple-element.500), channel_id=1, source_target_pairs={{0,3},{1,0},{2,1},{3,2},{4,7},{5,4},{6,5},{7,6},{8,11},{9,8},{10,9... | collective-permute-start | bytes 786440 | tf_op jit(solution)/shard_map/ppermute | solution.py:560
  (451 other events, 11675.2 us)
Sparse Core Ops, SparseCore 0:
  22.5 82.1 all-gather.4
  166.8 185.6 all-gather.6
  393.2 60.0 all-gather.8
  493.7 161.5 all-gather.10
  1036.1 161.0 reduce-scatter.4
  1206.3 59.5 reduce-scatter.8
  1268.2 161.5 reduce-scatter.6
  1432.2 84.0 reduce-scatter.10

commit v2 on v1

--- a/solution.py
+++ b/solution.py
@@ -443,45 +443,46 @@
     return low(wide(left) + wide(right))
 
 
-def gather_plane(own):
+def gather_plane(own, use=None):
     half = own.shape[0] // 2
-    core = plane_send(own, 1)
-    across_x = plane_send(own, 2)
-    across_y = plane_send(own, 4)
-    diagonal = jnp.concatenate(
-        [plane_send(across_y[:half], 2), plane_send(across_x[half:], 4)]
-    )
-    return [
-        own,
-        core,
-        across_x,
-        plane_send(across_x, 1),
-        across_y,
-        plane_send(across_y, 1),
-        diagonal,
-        plane_send(diagonal, 1),
-    ]
+    near = [own, plane_send(own, 1)]
+    made = [use(near, 0)] if use else []
+    across_x, across_y, made = lax.optimization_barrier(
+        (plane_send(own, 2), plane_send(own, 4), made)
+    )
+    far = plane_send(across_y[:half], 2), plane_send(across_x[half:], 4)
+    across = [across_x, plane_send(across_x, 1), across_y, plane_send(across_y, 1)]
+    if use:
+        made = made + [use(across, 1)]
+    top, bottom, made = lax.optimization_barrier((*far, made))
+    last = [top, bottom, plane_send(top, 1), plane_send(bottom, 1)]
+    if use:
+        return [near, across, last], made + [use(last, 2)]
+    return [near, across, last]
+
+
+def shard_of(sets, d):
+    return (sets[0], d) if d < 2 else (sets[1], d - 2) if d < 6 else (sets[2], d - 6)
 
 
 def reduce_plane(part):
-    received = {d: plane_send(low(part(d)), 1) for d in (7, 5, 3, 1)}
-    far, by_y, by_x, here = (
-        low(part(d) + wide(received[d + 1])) if d else part(d) + wide(received[d + 1])
-        for d in (6, 4, 2, 0)
-    )
+    odd = part((7, 5, 3, 1), None)
+    received = [plane_send(v, 1) for v in odd]
+    (far,) = part((6,), received[:1])
     half = far.shape[0] // 2
-    top = plane_send(far[:half], 2)
-    bottom = plane_send(far[half:], 4)
+    top, bottom = lax.optimization_barrier(
+        (plane_send(far[:half], 2), plane_send(far[half:], 4))
+    )
+    by_y, by_x, here = part((4, 2, 0), received[1:])
     by_y = jnp.concatenate([add_low(by_y[:half], top), by_y[half:]])
     by_x = jnp.concatenate([by_x[:half], add_low(by_x[half:], bottom)])
+    by_x, by_y = lax.optimization_barrier((by_x, by_y))
     from_x = plane_send(by_x, 2)
     from_y = plane_send(by_y, 4)
-    return here + wide(from_x) + wide(from_y), far, by_x
-
-
-def reduce_all(values):
-    for distance in (1, 2, 4):
-        values = values + plane_send(values, distance)
+    return wide(here) + wide(from_x) + wide(from_y), far, by_x
+
+
+def sum_line(values):
     size = lax.axis_size("tp")
     if size & (size - 1):
         return lax.psum(values, "tp")
@@ -493,6 +494,12 @@
     return values
 
 
+def sum_plane(values):
+    for distance in (1, 2, 4):
+        values = values + plane_send(values, distance)
+    return values
+
+
 def after(token, *values):
     if token is None:
         return values
@@ -507,44 +514,50 @@
     return lax.psum_scatter(terms, "tp", scatter_dimension=axis, tiled=True)
 
 
-def assemble(pieces, axis, places):
-    size = len(pieces)
-    block = pieces[0].shape[axis]
-    shape = list(pieces[0].shape)
+def assemble(sets, block_shape, axis, places):
+    size = sum(len(held) for _, held in sets)
+    block = block_shape[axis]
+    shape = list(block_shape)
     shape[axis] = size * block
 
     def kernel(place_ref, *refs):
-        out = refs[size]
-        for d in range(size):
-            start = pl.multiple_of(place_ref[d] * block, block)
-            where = tuple([slice(None)] * axis + [pl.ds(start, block)])
-            out[where] = refs[d][...]
+        out, d = refs[len(sets)], 0
+        for (_, held), ref in zip(sets, refs):
+            for i in held:
+                start = pl.multiple_of(place_ref[d] * block, block)
+                where = tuple([slice(None)] * axis + [pl.ds(start, block)])
+                out[where] = ref[...] if i is None else ref[i]
+                d += 1
 
     return pl.pallas_call(
         kernel,
-        out_shape=jax.ShapeDtypeStruct(tuple(shape), pieces[0].dtype),
+        out_shape=jax.ShapeDtypeStruct(tuple(shape), sets[0][0].dtype),
         in_specs=[pl.BlockSpec(memory_space=pltpu.SMEM)]
-        + [pl.BlockSpec(memory_space=pltpu.VMEM)] * size,
+        + [pl.BlockSpec(memory_space=pltpu.VMEM)] * len(sets),
         out_specs=pl.BlockSpec(memory_space=pltpu.VMEM),
-        compiler_params=pltpu.CompilerParams(vmem_limit_bytes=32 * 1024 * 1024),
+        compiler_params=kernel_params(12),
+        cost_estimate=kernel_cost(),
         name="assemble",
-    )(places, *pieces)
+    )(places, *(array for array, _ in sets))
 
 
 def block_at(array, index, block, axis):
     return lax.dynamic_slice_in_dim(array, index * block, block, axis)
 
 
-def swap(array, axis, into, start=None, done=None):
+def swap(array, axis, into, start=None, done=None, first=None):
     size = lax.axis_size("fsdp")
     places = lax.axis_index("fsdp").astype(jnp.int32) ^ jnp.arange(size, dtype=jnp.int32)
     block = array.shape[axis] // size
     (array,) = after(start, array)
     pieces = [block_at(array, places[d], block, axis) for d in range(size)]
-    order = (6, 7, 4, 5, 2, 3, 1)
-    moved = {d: plane_send(pieces[d], d) for d in order}
-    moved = after(done, *(moved[d] for d in range(1, size)))
-    return assemble([pieces[0], *moved], into, places)
+    other = plane_send(jnp.stack(pieces[1::2]), 1)
+    if first is not None:
+        first.append(other)
+    chips = [plane_send(jnp.stack([pieces[d], other[d // 2]]), d) for d in (6, 4, 2)]
+    other, *chips = after(done, other[0], *chips)
+    sets = [(pieces[0], (None,)), (other, (None,))] + [(v, (0, 1)) for v in reversed(chips)]
+    return assemble(sets, pieces[0].shape, into, places)
 
 
 def line_swap(array, start=None, done=None):
@@ -559,7 +572,8 @@
         pairs = [(i, (i + step) % size) for i in range(size)]
         moved.append(lax.ppermute(piece, "tp", pairs))
     moved = after(done, *moved)
-    return assemble([block_at(array, place, block, 0), *moved], 0, sources)
+    own = block_at(array, place, block, 0)
+    return assemble([(v, (None,)) for v in (own, *moved)], own.shape, 0, sources)
 
 
 def line_rows(rows, start=None, done=None):
@@ -615,21 +629,21 @@
 
 
 def rows_in_order(place, groups, target, pick):
-    for d in range(2 * len(groups)):
-        ref = groups[d // 2]
+    shards = [(ref, e) for ref in groups for e in range(ref.shape[0])]
+    for d, (ref, e) in enumerate(shards):
         blocks, block = ref.shape[2], ref.shape[3]
         for i in range(blocks):
-            start = pl.multiple_of((i * 2 * len(groups) + (place ^ d)) * block, block)
-            target[pl.ds(start, block), :] = pick(ref[d % 2, 0, i])
+            start = pl.multiple_of((i * len(shards) + (place ^ d)) * block, block)
+            target[pl.ds(start, block), :] = pick(ref[e, 0, i])
 
 
 def rows_from_order(place, source, groups):
-    for d in range(2 * len(groups)):
-        ref = groups[d // 2]
+    shards = [(ref, e) for ref in groups for e in range(ref.shape[0])]
+    for d, (ref, e) in enumerate(shards):
         blocks, block = ref.shape[2], ref.shape[3]
         for i in range(blocks):
-            start = pl.multiple_of((i * 2 * len(groups) + (place ^ d)) * block, block)
-            ref[d % 2, 0, i] = source[pl.ds(start, block), :].astype(ref.dtype)
+            start = pl.multiple_of((i * len(shards) + (place ^ d)) * block, block)
+            ref[e, 0, i] = source[pl.ds(start, block), :].astype(ref.dtype)
 
 
 def head_columns(index, head):
@@ -757,74 +771,76 @@
     rows_from_order(place, done, out_refs)
 
 
-def attend_specs(raw, tables, first, length, head):
-    local = tables[0].shape[0]
-    group = pl.BlockSpec((2, 1) + raw[0].shape[2:], lambda s: (0, s, 0, 0, 0))
+def kernel_cost(flops=1024):
+    return pl.CostEstimate(flops=flops // 2, bytes_accessed=1024, transcendentals=0)
+
+
+def kernel_params(mib=48):
+    return pltpu.CompilerParams(vmem_limit_bytes=mib * 1024 * 1024)
+
+
+def group_specs(arrays):
+    def spec(array):
+        return pl.BlockSpec((array.shape[0], 1) + array.shape[2:], lambda s: (0, s, 0, 0, 0))
+
+    return [spec(array) for array in arrays]
+
+
+def table_specs(length, head):
     table = pl.BlockSpec((1, length, head), lambda s: (s, 0, 0))
-    line = pl.BlockSpec((1, 1, length), lambda s: (s, 0, 0))
     gain = pl.BlockSpec((1, head), lambda s: (0, 0))
-    return local, group, table, line, gain
-
-
-def grouped(rows, local, blocks):
+    return [table, table, pl.BlockSpec((1, 1, length), lambda s: (s, 0, 0)), gain, gain]
+
+
+def grouped(rows, shards, local, blocks):
     count, width = rows.shape
-    return rows.reshape(2, local, blocks, count // (2 * local * blocks), width)
+    return rows.reshape(shards, local, blocks, count // (shards * local * blocks), width)
 
 
 def plane_attend(raw, tables, first, gains, rows=256):
-    head = tables[0].shape[-1]
-    length = tables[0].shape[1]
-    local, group, table, line, gain = attend_specs(raw, tables, first, length, head)
+    local, length, head = tables[0].shape
     width = raw[0].shape[-1]
     heads = width // head - 2
     groups = len(raw)
-    out_shape = raw[0].shape[:-1] + (heads * head,)
-    out_group = pl.BlockSpec((2, 1) + out_shape[2:], lambda s: (0, s, 0, 0, 0))
+    outs = [jax.ShapeDtypeStruct(v.shape[:-1] + (heads * head,), jnp.bfloat16) for v in raw]
     totals = jax.ShapeDtypeStruct((local, length // rows, heads * rows), jnp.float32)
     out = pl.pallas_call(
         functools.partial(attend_kernel, groups, heads, rows),
         grid=(local,),
-        out_shape=[jax.ShapeDtypeStruct(out_shape, jnp.bfloat16)] * groups + [totals],
+        out_shape=outs + [totals],
         in_specs=[pl.BlockSpec(memory_space=pltpu.SMEM)]
-        + [group] * groups
-        + [table, table, line, gain, gain],
-        out_specs=[out_group] * groups
+        + group_specs(raw)
+        + table_specs(length, head),
+        out_specs=group_specs(outs)
         + [pl.BlockSpec((1,) + totals.shape[1:], lambda s: (s, 0, 0))],
         scratch_shapes=[
             pltpu.VMEM((length, width), jnp.float32),
             pltpu.VMEM((length, width), jnp.bfloat16),
             pltpu.VMEM((length, heads * head), jnp.bfloat16),
         ],
-        compiler_params=pltpu.CompilerParams(vmem_limit_bytes=48 * 1024 * 1024),
-        cost_estimate=pl.CostEstimate(
-            flops=local * heads * length * length * head * 5 // 2,
-            bytes_accessed=local * length * width * 6,
-            transcendentals=local * heads * length * length * 5 // 8,
-        ),
+        compiler_params=kernel_params(24),
+        cost_estimate=kernel_cost(local * heads * length * length * head * 8),
         name="attend",
     )(plane_place(), *raw, *tables, first, *gains)
     return out[:groups], out[groups]
 
 
 def plane_attend_back(raw, out_grad, totals, tables, first, gains, rows=256):
-    head = tables[0].shape[-1]
-    length = tables[0].shape[1]
-    local, group, table, line, gain = attend_specs(raw, tables, first, length, head)
+    local, length, head = tables[0].shape
     width = raw[0].shape[-1]
     heads = width // head - 2
     groups = len(raw)
-    grad_group = pl.BlockSpec((2, 1) + out_grad[0].shape[2:], lambda s: (0, s, 0, 0, 0))
     out = pl.pallas_call(
         functools.partial(attend_back_kernel, groups, heads, rows),
         grid=(local,),
-        out_shape=[jax.ShapeDtypeStruct(raw[0].shape, jnp.bfloat16)] * groups
+        out_shape=[jax.ShapeDtypeStruct(v.shape, jnp.bfloat16) for v in raw]
         + [jax.ShapeDtypeStruct((local, 2, head), jnp.float32)],
         in_specs=[pl.BlockSpec(memory_space=pltpu.SMEM)]
-        + [group] * groups
-        + [grad_group] * groups
+        + group_specs(raw)
+        + group_specs(out_grad)
         + [pl.BlockSpec((1,) + totals.shape[1:], lambda s: (s, 0, 0))]
-        + [table, table, line, gain, gain],
-        out_specs=[group] * groups + [pl.BlockSpec((1, 2, head), lambda s: (s, 0, 0))],
+        + table_specs(length, head),
+        out_specs=group_specs(raw) + [pl.BlockSpec((1, 2, head), lambda s: (s, 0, 0))],
         scratch_shapes=[
             pltpu.VMEM((length, width), jnp.float32),
             pltpu.VMEM((length, width), jnp.bfloat16),
@@ -834,15 +850,221 @@
             pltpu.VMEM((length, head), jnp.float32),
             pltpu.VMEM((length, width), jnp.bfloat16),
         ],
-        compiler_params=pltpu.CompilerParams(vmem_limit_bytes=56 * 1024 * 1024),
-        cost_estimate=pl.CostEstimate(
-            flops=local * heads * length * length * head * 25 // 4,
-            bytes_accessed=local * length * width * 8,
-            transcendentals=local * heads * length * length * 5 // 8,
-        ),
+        compiler_params=kernel_params(32),
+        cost_estimate=kernel_cost(local * heads * length * length * head * 16),
         name="attend_back",
     )(plane_place(), *raw, *out_grad, totals, *tables, first, *gains)
     return out[:groups], jnp.sum(out[groups], axis=0)
+
+
+def whole_spec(array):
+    return pl.BlockSpec(
+        array.shape, lambda n: (0,) * array.ndim, pipeline_mode=pl.Buffered(buffer_count=1)
+    )
+
+
+def dot_cols(left, right):
+    return lax.dot_general(
+        left, right, (((1,), (1,)), ((), ())), preferred_element_type=jnp.float32
+    )
+
+
+def joined(refs, rows_ref):
+    @pl.when(pl.program_id(0) == 0)
+    def _():
+        start = 0
+        for ref in refs:
+            rows_ref[start : start + ref.shape[0], :] = ref[...]
+            start += ref.shape[0]
+
+    return rows_ref[...]
+
+
+def joined_scratch(pieces):
+    count = sum(v.shape[0] for v in pieces)
+    return [pltpu.VMEM((count, pieces[0].shape[1]), pieces[0].dtype)]
+
+
+def project_kernel(count, *refs):
+    weight, out, rows_ref = refs[count:]
+    out[...] = dot_cols(joined(refs[:count], rows_ref), weight[...]).astype(out.dtype)
+
+
+def project(pieces, weight, first, width, dtype, tile=256):
+    count = sum(v.shape[0] for v in pieces)
+    return pl.pallas_call(
+        functools.partial(project_kernel, len(pieces)),
+        grid=(width // tile,),
+        out_shape=jax.ShapeDtypeStruct((count, width), dtype),
+        in_specs=[whole_spec(v) for v in pieces]
+        + [pl.BlockSpec((tile, weight.shape[1]), lambda n: (first // tile + n, 0))],
+        out_specs=pl.BlockSpec((count, tile), lambda n: (0, n)),
+        scratch_shapes=joined_scratch(pieces),
+        compiler_params=kernel_params(16),
+        cost_estimate=kernel_cost(2 * count * width * weight.shape[1]),
+        name="project",
+    )(*pieces, weight)
+
+
+def units_kernel(count, *refs):
+    gate_rows, up_rows, hidden_ref, gate_ref, up_ref, rows_ref = refs[count:]
+    rows = joined(refs[:count], rows_ref)
+    gate = dot_cols(rows, gate_rows[0])
+    up = dot_cols(rows, up_rows[0])
+    hidden_ref[...] = (gate * up / (1.0 + jnp.exp(-gate))).astype(hidden_ref.dtype)
+    gate_ref[...] = gate.astype(gate_ref.dtype)
+    up_ref[...] = up.astype(up_ref.dtype)
+
+
+def unit_spec(weights, kind, tile):
+    return pl.BlockSpec((1, tile, weights.shape[2]), lambda n: (kind, n, 0))
+
+
+def hidden_units(pieces, weights, tile=256):
+    count = sum(v.shape[0] for v in pieces)
+    shape = jax.ShapeDtypeStruct((count, weights.shape[1]), jnp.bfloat16)
+    return pl.pallas_call(
+        functools.partial(units_kernel, len(pieces)),
+        grid=(weights.shape[1] // tile,),
+        out_shape=[shape] * 3,
+        in_specs=[whole_spec(v) for v in pieces]
+        + [unit_spec(weights, kind, tile) for kind in (0, 1)],
+        out_specs=[pl.BlockSpec((count, tile), lambda n: (0, n))] * 3,
+        scratch_shapes=joined_scratch(pieces),
+        compiler_params=kernel_params(20),
+        cost_estimate=kernel_cost(4 * count * weights.shape[1] * weights.shape[2]),
+        name="hidden_units",
+    )(*pieces, weights, weights)
+
+
+def units_back_kernel(count, *refs):
+    down_rows, gate_ref, up_ref, gate_grad, up_grad, rows_ref = refs[count:]
+    grad = dot_cols(joined(refs[:count], rows_ref), down_rows[0])
+    gate, up = wide(gate_ref[...]), wide(up_ref[...])
+    sigmoid = 1.0 / (1.0 + jnp.exp(-gate))
+    gate_grad[...] = (grad * up * sigmoid * (1.0 + gate * (1.0 - sigmoid))).astype(gate_grad.dtype)
+    up_grad[...] = (grad * gate * sigmoid).astype(up_grad.dtype)
+
+
+def hidden_units_back(pieces, weights, gate, up, tile=256):
+    count = gate.shape[0]
+    side = pl.BlockSpec((count, tile), lambda n: (0, n))
+    return pl.pallas_call(
+        functools.partial(units_back_kernel, len(pieces)),
+        grid=(weights.shape[1] // tile,),
+        out_shape=[jax.ShapeDtypeStruct(gate.shape, jnp.bfloat16)] * 2,
+        in_specs=[whole_spec(v) for v in pieces] + [unit_spec(weights, 2, tile), side, side],
+        out_specs=[side, side],
+        scratch_shapes=joined_scratch(pieces),
+        compiler_params=kernel_params(20),
+        cost_estimate=kernel_cost(2 * count * weights.shape[1] * weights.shape[2]),
+        name="hidden_units_back",
+    )(*pieces, weights, gate, up)
+
+
+def parts_kernel(shards, terms, adding, *refs):
+    lefts, weights = refs[: shards * terms], refs[shards * terms : (shards + 1) * terms]
+    adds = refs[(shards + 1) * terms : -shards]
+    outs = refs[-shards:]
+    total = None
+    for t in range(terms):
+        weight = weights[t][...]
+        left = jnp.concatenate([lefts[i * terms + t][...] for i in range(shards)], axis=0)
+        term = jnp.dot(
+            left, weight.reshape(weight.shape[-2:]), preferred_element_type=jnp.float32
+        )
+        total = term if total is None else total + term
+    rows = outs[0].shape[0]
+    for i in range(shards):
+        mine = total[i * rows : (i + 1) * rows]
+        if adding:
+            mine = mine + wide(adds[i][...])
+        outs[i][...] = mine.astype(outs[i].dtype)
+
+
+def parts_of(terms, ds, adds, tile=512):
+    lefts, specs = [], []
+    for d in ds:
+        for sets, _, _ in terms:
+            array, place = shard_of(sets, d)
+            rows = sets[0].shape[0] // 2
+            lefts.append(array)
+            specs.append(
+                pl.BlockSpec(
+                    (rows, array.shape[1]),
+                    lambda n, p=place: (p, 0),
+                    pipeline_mode=pl.Buffered(buffer_count=1),
+                )
+            )
+    width = terms[0][1].shape[-1]
+    side = pl.BlockSpec((rows, tile), lambda n: (0, n))
+    return pl.pallas_call(
+        functools.partial(parts_kernel, len(ds), len(terms), adds is not None),
+        grid=(width // tile,),
+        out_shape=[jax.ShapeDtypeStruct((rows, width), jnp.bfloat16)] * len(ds),
+        in_specs=specs + [spec for _, _, spec in terms] + [side] * len(adds or ()),
+        out_specs=[side] * len(ds),
+        compiler_params=kernel_params(16),
+        cost_estimate=kernel_cost(2 * len(ds) * rows * width * sum(v.shape[-1] for v in lefts[: len(terms)])),
+        name="parts",
+    )(*lefts, *(weights for _, weights, _ in terms), *(adds or ()))
+
+
+def rows_spec(kind, weights, tile=512):
+    return pl.BlockSpec((1, weights.shape[1], tile), lambda n: (kind, 0, n))
+
+
+def pack_spec(block, height, tile=512):
+    return pl.BlockSpec((height, tile), lambda n: (block, n))
+
+
+def outer_kernel(plan, *refs):
+    for lefts, rights, place in plan:
+        total = None
+        for left, pieces in zip(lefts, rights):
+            right = jnp.concatenate([refs[p][...] for p in pieces], axis=0)
+            term = lax.dot_general(
+                refs[left][...], right, (((0,), (0,)), ((), ())), preferred_element_type=jnp.float32
+            )
+            total = term if total is None else total + term
+        refs[-1][place] = total.astype(refs[-1].dtype)
+
+
+def outer(products, shape, tile=512):
+    operands, specs, plan, seen = [], [], [], {}
+
+    def operand(array, split):
+        if id(array) not in seen:
+            seen[id(array)] = len(operands)
+            operands.append(array)
+            specs.append(
+                pl.BlockSpec((array.shape[0], tile), lambda n: (0, n))
+                if split
+                else pl.BlockSpec(
+                    array.shape, lambda n: (0, 0), pipeline_mode=pl.Buffered(buffer_count=1)
+                )
+            )
+        return seen[id(array)]
+
+    for lefts, rights, place in products:
+        plan.append(
+            (
+                [operand(v, False) for v in lefts],
+                [[operand(v, True) for v in pieces] for pieces in rights],
+                place,
+            )
+        )
+    block = shape[:-1] + (tile,)
+    return pl.pallas_call(
+        functools.partial(outer_kernel, plan),
+        grid=(shape[-1] // tile,),
+        out_shape=jax.ShapeDtypeStruct(shape, jnp.bfloat16),
+        in_specs=specs,
+        out_specs=pl.BlockSpec(block, lambda n: (0,) * (len(shape) - 1) + (n,)),
+        compiler_params=kernel_params(56),
+        cost_estimate=kernel_cost(2 * shape[-1] * sum(v.size for lefts, _, _ in products for v in lefts)),
+        name="outer",
+    )(*operands)
 
 
 def plane_plan(
@@ -879,15 +1101,19 @@
     key_count = key_matrix.shape[2] * line // size
     split = query_count + 2 * key_count
 
-    def pairs_of(pieces):
-        return [jnp.concatenate(pieces[d : d + 2]) for d in range(0, size, 2)]
-
-    def piece(pairs, d):
-        half = pairs[d // 2].shape[0] // 2
-        return pairs[d // 2][half * (d % 2) : half * (d % 2 + 1)]
-
-    def dot(left, right):
-        return jnp.dot(left, right, preferred_element_type=jnp.float32)
+    def group(sets):
+        counts = [v.shape[0] * size // sum(u.shape[0] for u in sets) for v in sets]
+        return [grouped(v, count, local, line) for v, count in zip(sets, counts)]
+
+    def flat(sets):
+        return [v.reshape(-1, v.shape[-1]) for v in sets]
+
+    def hold(token, sets):
+        return [list(after(token, *v)) for v in sets]
+
+    def reduce_down(hidden, weights):
+        term = (hidden, weights, rows_spec(2, weights))
+        return reduce_plane(lambda ds, adds: parts_of([term], ds, adds))[0]
 
     attn_sets, attn_gathered, hidden_sets = ([None] * layers for _ in range(3))
 
@@ -895,133 +1121,132 @@
         shards = (query_weight[index], key_matrix[index], value_matrix[index], out_weight[index])
         attn_sets[index], attn_gathered[index] = attention_weights(*after(token, *shards))
 
-    def shard_hidden(index, start, done):
-        shards = jnp.stack([gate_weight[index].T, up_weight[index].T, down_weight[index]])
-        return swap(shards, 1, 2, start, done)
-
-    fetch_attn(0, segment_ids)
-    first_rows = swap(tokens, 0, 0)
-    residual = line_rows(first_rows)
-    residual = wide(residual)
-    grad = None
+    fetch_attn(0, None)
+    exchanged = []
+    both = jnp.concatenate([tokens, cotangent], axis=1)
+    both = swap(both, 0, 0, None, None, exchanged)
+    hidden_shards = jnp.stack(
+        [gate_weight.swapaxes(1, 2), up_weight.swapaxes(1, 2), down_weight], axis=1
+    ).reshape(-1, *down_weight.shape[1:])
+    both = line_rows(both)
+    hidden_shards, first = lax.optimization_barrier((hidden_shards, first))
+    hidden_shards = swap(hidden_shards, 1, 2, exchanged[0], both)
+    hidden_shards = hidden_shards.reshape(layers, -1, *hidden_shards.shape[1:])
+    residual, grad = wide(both[:, : tokens.shape[1]]), wide(both[:, tokens.shape[1] :])
     saved = []
     for index in range(layers):
         pack = attn_sets[index]
         gains = (query_gain[index][None], key_gain[index][None])
         normed, attn_back = jax.vjp(rms_scale, residual, attn_gain[index])
-        pieces = gather_plane(low(normed))
+        rows = gather_plane(low(normed))
         if index == 0:
-            shards = shard_hidden(0, first_rows, pieces[1])
-            hidden_sets[0] = line_gather(after(attn_gathered[0], shards)[0], 1)
-            pieces[6:] = after(shards, *pieces[6:])
-        rows = pairs_of(pieces)
-        raw = [grouped(contract_cols(v, pack[:split]), local, line) for v in rows]
+            hidden_sets[0] = line_gather(after(attn_gathered[0], hidden_shards[0])[0], 1)
+        raw = group([project(v, pack, 0, split, jnp.float32) for v in rows])
         if index + 1 < layers:
             fetch_attn(index + 1, raw[0])
         mixed, totals = plane_attend(raw, tables, first, gains)
-        mixed = [v.reshape(-1, query_count) for v in mixed]
-        if index == 0:
-            grad = swap(cotangent, 0, 0, raw[0])
-            mixed = after(grad, *mixed)
-        total, *_ = reduce_plane(lambda d: dot(piece(mixed, d), pack[split:]))
+        mixed = flat(mixed)
+        out_term = (mixed, pack, pack_spec(split // query_count, query_count))
+        total, *_ = reduce_plane(lambda ds, adds: parts_of([out_term], ds, adds))
         middle = residual + total
-        if index == 0:
-            grad = line_rows(grad, mixed[0])
-            middle, grad = lax.optimization_barrier((middle, grad))
-            grad = wide(grad)
-        gate_rows, up_rows, down_rows = hidden_sets[index]
+        weights = hidden_sets[index]
         normed, mlp_back = jax.vjp(rms_scale, middle, mlp_gain[index])
-        mlp_rows = pairs_of(gather_plane(low(normed)))
-        hidden, swiglu_backs = [], []
-        for v in mlp_rows:
-            gate, upward = contract_cols(v, gate_rows), contract_cols(v, up_rows)
-            units, swiglu_back = jax.vjp(swiglu, gate, upward)
-            hidden.append(low(units))
-            swiglu_backs.append(swiglu_back)
+        mlp_rows = gather_plane(low(normed))
+        hidden, gates, ups = zip(*(hidden_units(v, weights) for v in mlp_rows))
         if index + 1 < layers:
-            shards = shard_hidden(index + 1, mlp_rows[-1], None)
-            hidden_sets[index + 1] = line_gather(shards, 1)
-            hidden = list(after(shards, *hidden))
-        total, *_ = reduce_plane(lambda d: dot(piece(hidden, d), down_rows))
-        residual = middle + total
+            hidden_sets[index + 1] = line_gather(
+                after(mlp_rows[2][0], hidden_shards[index + 1])[0], 1
+            )
+        if index + 1 < layers:
+            residual = middle + reduce_down(hidden, weights)
+        else:
+            residual = middle
         saved.append(
-            (attn_back, rows, raw, mixed, totals, mlp_back, mlp_rows, swiglu_backs, hidden)
-        )
-    result = residual
+            (attn_back, rows, raw, mixed, totals, mlp_back, mlp_rows, gates, ups, hidden)
+        )
     pack_grads, pack_sums, gain_grads, hidden_sums, hidden_grads = (
         [None] * layers for _ in range(5)
     )
     for index in reversed(range(layers)):
         pack = attn_sets[index]
         gains = (query_gain[index][None], key_gain[index][None])
-        gate_rows, up_rows, down_rows = hidden_sets[index]
-        attn_back, rows, raw, mixed, totals, mlp_back, mlp_rows, swiglu_backs, hidden = saved[index]
+        weights = hidden_sets[index]
+        attn_back, rows, raw, mixed, totals = saved[index][:5]
+        mlp_back, mlp_rows, gates, ups, hidden = saved[index][5:]
         if index + 1 == layers:
-            (grad,) = after(tuple(mlp_rows), grad)
-        grad_rows = pairs_of(gather_plane(low(grad)))
-        gate_grads, up_grads = [], []
-        for v, swiglu_back in zip(grad_rows, swiglu_backs):
-            gate_grad, up_grad = swiglu_back(contract_cols(v, down_rows))
-            gate_grads.append(low(gate_grad))
-            up_grads.append(low(up_grad))
-        if index + 1 == layers:
-            gate_grads = after(result, *gate_grads)
-        normed_grad, token, token_next = reduce_plane(
-            lambda d: dot(piece(gate_grads, d), gate_rows) + dot(piece(up_grads, d), up_rows)
-        )
-        hidden, grad_rows = (after(token, *v) for v in (hidden, grad_rows))
-        gate_grads, up_grads, mlp_rows = (
-            after(token_next, *v) for v in (gate_grads, up_grads, mlp_rows)
-        )
-        all_grads, all_rows = jnp.concatenate(grad_rows), jnp.concatenate(mlp_rows)
-        terms = [
-            low(contract_rows(jnp.concatenate(gate_grads), all_rows)),
-            low(contract_rows(jnp.concatenate(up_grads), all_rows)),
-            low(contract_rows(jnp.concatenate(hidden), all_grads)),
+            (grad,) = after(tuple(mlp_rows[2]), grad)
+        grad_rows, unit_grads = gather_plane(
+            low(grad), lambda v, i: hidden_units_back(v, weights, gates[i], ups[i])
+        )
+        gate_grads, up_grads = zip(*unit_grads)
+        unit_terms = [
+            (gate_grads, weights, rows_spec(0, weights)),
+            (up_grads, weights, rows_spec(1, weights)),
         ]
-        normed_grad, *terms = lax.optimization_barrier((normed_grad, *terms))
+        normed_grad, token, *_ = reduce_plane(
+            lambda ds, adds: parts_of(unit_terms, ds, adds)
+        )
+        (held,) = after(token, gate_grads[0])
+        terms = outer(
+            [
+                ((held, *gate_grads[1:]), mlp_rows, 0),
+                (up_grads, mlp_rows, 1),
+                (hidden, grad_rows, 2),
+            ],
+            weights.shape,
+        )
+        normed_grad, terms = lax.optimization_barrier((normed_grad, terms))
         if index + 1 < layers:
             done = hidden_sums[index + 1]
-            above = swap(pack_grads[index + 1][None], 2, 0, grad_rows[-1])
-            result = swap(result, 0, 0, grad_rows[-1])
-            normed_grad, above, result = lax.optimization_barrier((normed_grad, above, result))
+            above = swap(pack_grads[index + 1][None], 2, 0, gate_grads[1])
             pack_sums[index + 1] = line_reduce(after(done, above)[0])
-            terms = after(done, *terms)
-        hidden_sums[index] = line_reduce(jnp.stack(terms), 1)
+            (terms,) = after(pack_sums[index + 1], terms)
+        hidden_sums[index] = line_reduce(terms, 1)
         grad_part, mlp_gain_grad = mlp_back(normed_grad)
         grad = grad + grad_part
-        grad_rows = pairs_of(gather_plane(low(grad)))
-        mixed_grad = [
-            grouped(low(contract_cols(v, pack[split:])), local, line) for v in grad_rows
-        ]
+        grad_rows, mixed_grad = gather_plane(
+            low(grad), lambda v, i: project(v, pack, split, query_count, jnp.bfloat16)
+        )
+        mixed_grad = group(mixed_grad)
         raw_grad, head_gain_grads = plane_attend_back(raw, mixed_grad, totals, tables, first, gains)
+        raw_grad = flat(raw_grad)
+        if index + 1 == layers:
+            result = residual + reduce_down(after(normed_grad, *hidden), weights)
+            result, *raw_grad = lax.optimization_barrier((result, *raw_grad))
         if index + 1 < layers:
-            hidden_grads[index + 1] = swap(hidden_sums[index + 1], 2, 1, mixed_grad[-1])
-            raw_grad = after(hidden_grads[index + 1], *raw_grad)
-        raw_grad = [v.reshape(-1, split) for v in raw_grad]
-        normed_grad, token, token_next = reduce_plane(lambda d: dot(piece(raw_grad, d), pack[:split]))
-        mixed, grad_rows = (after(token, *v) for v in (mixed, grad_rows))
-        raw_grad, rows = (after(token_next, *v) for v in (raw_grad, rows))
-        pack_grad = jnp.concatenate(
+            hidden_grads[index + 1] = swap(hidden_sums[index + 1], 2, 1, mixed_grad[2])
+            hidden_grads[index + 1], *raw_grad = lax.optimization_barrier(
+                (hidden_grads[index + 1], *raw_grad)
+            )
+        raw_term = (raw_grad, pack, pack_spec(0, split))
+        normed_grad, token, *_ = reduce_plane(
+            lambda ds, adds: parts_of([raw_term], ds, adds)
+        )
+        (held,) = after(token, mixed[0])
+        pack_grad = outer(
             [
-                low(contract_rows(jnp.concatenate(raw_grad), jnp.concatenate(rows))),
-                low(contract_rows(jnp.concatenate(mixed), jnp.concatenate(grad_rows))),
-            ]
+                (raw_grad, rows, slice(0, split)),
+                ((held, *mixed[1:]), grad_rows, slice(split, split + query_count)),
+            ],
+            pack.shape,
         )
         normed_grad, pack_grad = lax.optimization_barrier((normed_grad, pack_grad))
         pack_grads[index] = pack_grad
-        if index + 1 == layers:
-            result = line_rows_back(low(result), raw_grad[0])
-            normed_grad, result = lax.optimization_barrier((normed_grad, result))
         grad_part, attn_gain_grad = attn_back(normed_grad)
         grad = grad + grad_part
         gain_grads[index] = jnp.concatenate(
             [attn_gain_grad, mlp_gain_grad, head_gain_grads[0], head_gain_grads[1]]
         )
-    token_grad = wide(swap(line_rows_back(low(grad)), 0, 0))
     below = swap(pack_grads[0][None], 2, 0)
     pack_sums[0] = line_reduce(after((hidden_sums[0], pack_sums[1:]), below)[0])
-    hidden_grads[0] = swap(hidden_sums[0], 2, 1)
+    both = jnp.concatenate([low(result), low(grad)], axis=1)
+    gain_stack = sum_line(jnp.stack(gain_grads).reshape(-1, head))
+    both, gain_stack = lax.optimization_barrier((both, gain_stack))
+    both = line_rows_back(both, below)
+    gain_stack = sum_plane(gain_stack)
+    hidden_grads[0] = swap(hidden_sums[0], 2, 1, below)
+    both = swap(both, 0, 0)
+    result, token_grad = both[:, : tokens.shape[1]], wide(both[:, tokens.shape[1] :])
     kinds = wide(jnp.stack(hidden_grads, 1))
     hidden_stacks = (kinds[0].swapaxes(1, 2), kinds[1].swapaxes(1, 2), kinds[2])
     marks = (0, query_count, query_count + key_count, split, pack_sums[0].shape[1])
@@ -1033,7 +1258,7 @@
     ]
     weight_stacks = [v.swapaxes(1, 2) for v in kinds[:3]] + kinds[3:]
     width = attn_gain.shape[1]
-    gain_stack = reduce_all(jnp.stack(gain_grads).reshape(-1, head)).reshape(layers, -1)
+    gain_stack = gain_stack.reshape(layers, -1)
     attn_sum, mlp_sum, query_sum, key_sum = (
         gain_stack[:, :width],
         gain_stack[:, width : 2 * width],

time: 1580 us -> 1410 us (0.89)
  matrix products: 280 us -> 0 us
  Pallas kernels: 89.1 us -> 325 us
  starting transfers between devices: 197 us -> 131 us
  waiting for transfers between devices: 734 us -> 670 us
    dot_general x130 -> x0, matrix products: 280 us -> none  [the longest x40 106 us: contract_cols(): lax.dot_general(left_side, right_side, (((1,), (1,)), ((), ())), preferre...]
    pallas_call x16 -> x63, Pallas kernels: 19.2 us -> 263 us  [the longest x24 83.6 us: parts_of(): pl.pallas_call(functools.partial(parts_kernel, len(ds), len(terms), adds...]
    ppermute x218 -> x178, starting transfers between devices: 178 us -> 120 us  [plane_send(): lax.ppermute(values, 'fsdp', [(i, i ^ distance) for i in range(size)])]
    reduce_scatter x4, waiting for transfers between devices: 38.6 us -> 0.03 us  [line_reduce(): return lax.psum_scatter(terms, 'tp', scatter_dimension=axis, tiled=True)]
    ppermute x2, waiting for transfers between devices: 39.9 us -> 2.94 us  [sum_line(): values = values + lax.ppermute(values, 'tp', pairs)]
    ppermute x218 -> x178, waiting for transfers between devices: 548 us -> 580 us  [plane_send(): lax.ppermute(values, 'fsdp', [(i, i ^ distance) for i in range(size)])]
    ppermute x12 -> x6, waiting for transfers between devices: 108 us -> 87 us  [line_swap(): moved.append(lax.ppermute(piece, 'tp', pairs))]
    another operation x2 -> x12, local copies, waits for them, and re-layouts: 0.03 us -> 16.9 us  [the longest x9 12.1 us: swap(): jnp.stack([pieces[d], other[d // 2]])]
  transfers between devices with their start and end apart: 240 -> 194, of which waited for: 91 -> 101; matrix products, arithmetic and copies ran while one was open for 28% -> 10% of each run, Pallas kernels for 4% -> 23%
where the time goes in v2:
time: 1410 us; the launch traced here: 1400 us
  waiting for transfers between devices  670 us (48%)
  Pallas kernels  325 us (23%)
  local copies, waits for them, and re-layouts  137 us (10%)
  starting transfers between devices  131 us (9%)
  other arithmetic  83.3 us (6%)
  between operations  48.7 us (3%)
    ppermute x178, waiting for transfers between devices, plane_send(): lax.ppermute(values, 'fsdp', [(i, i ^ distance) for i in range(size)])  580 us
    ppermute x178, starting transfers between devices, plane_send(): lax.ppermute(values, 'fsdp', [(i, i ^ distance) for i in range(size)])  120 us
    ppermute x6, waiting for transfers between devices, line_swap(): moved.append(lax.ppermute(piece, 'tp', pairs))  87 us
    pallas_call x24, Pallas kernels, parts_of(): pl.pallas_call(functools.partial(parts_kernel, len(ds), len(terms), adds...  83.6 us
    pallas_call x4, Pallas kernels, outer(): pl.pallas_call(functools.partial(outer_kernel, plan), grid=(shape[-1] //...  79.2 us
    unnamed x486, local copies, waits for them, and re-layouts  75.5 us
    pallas_call x6, Pallas kernels, hidden_units(): pl.pallas_call(functools.partial(units_kernel, len(pieces)), grid=(weight...  39.3 us
    pallas_call x2, Pallas kernels, plane_attend_back(): pl.pallas_call(functools.partial(attend_back_kernel, groups, heads, rows)...  39 us
  transfers between devices with their start and end apart: 194, of which 101 were waited for; matrix products, arithmetic and copies ran while one was open for 10% of the time, Pallas kernels for 23%

profile of v2, /device:TPU:8, one launch (start us, length us, event | category | flops | bytes accessed | tf_op | source)
XLA Modules:
  0.0 1396.0 jit_solution(12575686157862678890)
XLA Ops:
  58.1 10.5 collective-permute-done.1.refs_2_
  68.6 12.8 collective-permute-done.2.refs_3_
  91.1 33.6 %collective-permute-done.4.refs_1_ = bf16[64,4096]{1,0:T(8,128)(2,1)S(1)} collective-permute-done((bf16[64,4096]{1,0:T(8,128)(2,1)S(1)}, bf16[64,4096]{1,0:T(8,128)(2,1)S(1)}, u32[]{:S(2)}, u32[]{:S(2)}) %collective-permute-start.4) | collective-permute-done | bytes 524320 | tf_op jit(solution)/shard_map/ppermute | solution.py:573
  162.9 23.1 %collective-permute-done.12.refs_0_.refs_5_ = bf16[256,2048]{1,0:T(8,128)(2,1)S(1)} collective-permute-done((bf16[256,2048]{1,0:T(8,128)(2,1)S(1)}, bf16[256,2048]{1,0:T(8,128)(2,1)S(1)}, u32[]{:S(2)}, u32[]{:S(2)}) %collective-permute-start.12) | collective-permute-done | bytes 1048608 | tf_op jit(solution)/shard_map/ppermute | solution.py:427
  190.7 23.4 %collective-permute-done.16.refs_0_.refs_9_ = bf16[128,2048]{1,0:T(8,128)(2,1)S(1)} collective-permute-done((bf16[128,2048]{1,0:T(8,128)(2,1)S(1)}, bf16[128,2048]{1,0:T(8,128)(2,1)S(1)}, u32[]{:S(2)}, u32[]{:S(2)}) %collective-permute-start.16) | collective-permute-done | bytes 524320 | tf_op jit(solution)/shard_map/ppermute | solution.py:427
  214.8 18.6 %collective-permute-done.10.refs_3_ = bf16[2,1,768,256]{3,2,1,0:T(8,128)(2,1)S(1)} collective-permute-done((bf16[2,1,768,256]{3,2,1,0:T(8,128)(2,1)S(1)}, bf16[2,1,768,256]{3,2,1,0:T(8,128)(2,1)S(1)}, u32[]{:S(2)}, u32[]{:S(2)}) %collective-permute-start.10) | collective-permute-done | bytes 786464 | tf_op jit(solution)/shard_map/ppermute | solution.py:427
  246.6 11.7 attend.2
  286.7 17.9 %collective-permute-done.30 = bf16[256,2048]{1,0:T(8,128)(2,1)} collective-permute-done((bf16[256,2048]{1,0:T(8,128)(2,1)S(1)}, bf16[256,2048]{1,0:T(8,128)(2,1)}, u32[]{:S(2)}, u32[]{:S(2)}) %collective-permute-start.30) | collective-permute-done | bytes 1048608 | tf_op jit(solution)/shard_map/ppermute | solution.py:427
  312.2 20.2 %collective-permute-done.31.refs_0_.refs_5_ = bf16[256,2048]{1,0:T(8,128)(2,1)S(1)} collective-permute-done((bf16[256,2048]{1,0:T(8,128)(2,1)S(1)}, bf16[256,2048]{1,0:T(8,128)(2,1)S(1)}, u32[]{:S(2)}, u32[]{:S(2)}) %collective-permute-start.31) | collective-permute-done | bytes 1048608 | tf_op jit(solution)/shard_map/ppermute | solution.py:427
  364.8 10.4 hidden_units.6
  409.5 19.4 %collective-permute-done.51 = bf16[256,2048]{1,0:T(8,128)(2,1)S(1)} collective-permute-done((bf16[256,2048]{1,0:T(8,128)(2,1)S(1)}, bf16[256,2048]{1,0:T(8,128)(2,1)S(1)}, u32[]{:S(2)}, u32[]{:S(2)}) %collective-permute-start.51) | collective-permute-done | bytes 1048608 | tf_op jit(solution)/shard_map/ppermute | solution.py:427
  435.2 23.2 %collective-permute-done.57.refs_0_.refs_5_ = bf16[256,2048]{1,0:T(8,128)(2,1)S(1)} collective-permute-done((bf16[256,2048]{1,0:T(8,128)(2,1)S(1)}, bf16[256,2048]{1,0:T(8,128)(2,1)S(1)}, u32[]{:S(2)}, u32[]{:S(2)}) %collective-permute-start.57) | collective-permute-done | bytes 1048608 | tf_op jit(solution)/shard_map/ppermute | solution.py:427
  463.0 12.2 collective-permute-done.54.refs_2_
  475.2 11.2 collective-permute-done.61.refs_0_.refs_9_
  487.0 14.1 %collective-permute-done.55.refs_3_ = bf16[2,1,768,256]{3,2,1,0:T(8,128)(2,1)S(1)} collective-permute-done((bf16[2,1,768,256]{3,2,1,0:T(8,128)(2,1)S(1)}, bf16[2,1,768,256]{3,2,1,0:T(8,128)(2,1)S(1)}, u32[]{:S(2)}, u32[]{:S(2)}) %collective-permute-start.55) | collective-permute-done | bytes 786464 | tf_op jit(solution)/shard_map/ppermute | solution.py:427
  509.3 12.1 attend.3
  544.6 22.2 %collective-permute-done.72 = bf16[256,2048]{1,0:T(8,128)(2,1)S(1)} collective-permute-done((bf16[256,2048]{1,0:T(8,128)(2,1)S(1)}, bf16[256,2048]{1,0:T(8,128)(2,1)S(1)}, u32[]{:S(2)}, u32[]{:S(2)}) %collective-permute-start.72) | collective-permute-done | bytes 1048608 | tf_op jit(solution)/shard_map/ppermute | solution.py:427
  570.9 20.9 %collective-permute-done.73.refs_0_.refs_5_ = bf16[256,2048]{1,0:T(8,128)(2,1)} collective-permute-done((bf16[256,2048]{1,0:T(8,128)(2,1)S(1)}, bf16[256,2048]{1,0:T(8,128)(2,1)}, u32[]{:S(2)}, u32[]{:S(2)}) %collective-permute-start.73) | collective-permute-done | bytes 1048608 | tf_op jit(solution)/shard_map/ppermute | solution.py:427
  702.7 27.4 %outer.4 = bf16[3,768,2048]{2,1,0:T(8,128)(2,1)} custom-call(bf16[512,768]{1,0:T(8,128)(2,1)} %copy-done.62, bf16[1024,768]{1,0:T(8,128)(2,1)} %copy-done.13, bf16[512,768]{1,0:T(8,128)(2,1)} %copy-done.56, bf16[256,2048]{1,0:T(8,128)(2,1)} %copy-done.48, bf16[256,2048]{1,0:T(8,128)(2,1)} %copy-done.106, ...), custom_call_target="tpu_custom_call" | custom-call | flops 9663676416 | bytes 1024 | tf_op jit(solution)/shard_map/outer/pallas_call | solution.py:1058
  751.5 22.7 %collective-permute-done.107.refs_0_.refs_18_ = bf16[256,2048]{1,0:T(8,128)(2,1)S(1)} collective-permute-done((bf16[256,2048]{1,0:T(8,128)(2,1)S(1)}, bf16[256,2048]{1,0:T(8,128)(2,1)S(1)}, u32[]{:S(2)}, u32[]{:S(2)}) %collective-permute-start.107) | collective-permute-done | bytes 1048608 | tf_op jit(solution)/shard_map/ppermute | solution.py:427
  809.4 19.5 %attend_back.2 = (bf16[2,2,4,32,512]{4,3,2,1,0:T(8,128)(2,1)S(1)}, bf16[4,2,4,32,512]{4,3,2,1,0:T(8,128)(2,1)S(1)}, bf16[2,2,4,32,512]{4,3,2,1,0:T(8,128)(2,1)S(1)}, f32[2,2,128]{2,1,0:T(2,128)S(1)}) custom-call(s32[1]{0:T(128)} %bitcast.19.refs_0_, f32[2,2,4,32,512]{4,3,2,1,0:T(8,128)S(1)} %bitcast.370, f32[4,2,4,32,512]{4,3,2,1,0:T(8,128)S(1)} %bitcast.364, ...), custom_call_target="tpu_custom_call" | custom-call | flops 4294967296 | bytes 1024 | tf_op jit(solution)/shard_map/attend_back/pallas_call | solution.py:833
  856.8 12.4 outer.5
  894.5 18.1 %collective-permute-done.124.refs_0_.refs_21_ = bf16[256,2048]{1,0:T(8,128)(2,1)S(1)} collective-permute-done((bf16[256,2048]{1,0:T(8,128)(2,1)S(1)}, bf16[256,2048]{1,0:T(8,128)(2,1)S(1)}, u32[]{:S(2)}, u32[]{:S(2)}) %collective-permute-start.124) | collective-permute-done | bytes 1048608 | tf_op jit(solution)/shard_map/ppermute | solution.py:427
  947.0 16.6 %collective-permute-done.179.refs_2_ = bf16[2,1,768,256]{3,2,1,0:T(8,128)(2,1)S(1)} collective-permute-done((bf16[2,1,768,256]{3,2,1,0:T(8,128)(2,1)S(1)}, bf16[2,1,768,256]{3,2,1,0:T(8,128)(2,1)S(1)}, u32[]{:S(2)}, u32[]{:S(2)}) %collective-permute-start.179) | collective-permute-done | bytes 786464 | tf_op jit(solution)/shard_map/ppermute | solution.py:427
  963.6 17.3 %collective-permute-done.180.refs_3_ = bf16[2,1,768,256]{3,2,1,0:T(8,128)(2,1)S(1)} collective-permute-done((bf16[2,1,768,256]{3,2,1,0:T(8,128)(2,1)S(1)}, bf16[2,1,768,256]{3,2,1,0:T(8,128)(2,1)S(1)}, u32[]{:S(2)}, u32[]{:S(2)}) %collective-permute-start.180) | collective-permute-done | bytes 786464 | tf_op jit(solution)/shard_map/ppermute | solution.py:427
  1033.9 27.0 %outer.6 = bf16[3,768,2048]{2,1,0:T(8,128)(2,1)} custom-call(bf16[512,768]{1,0:T(8,128)(2,1)} %copy-done.58, bf16[1024,768]{1,0:T(8,128)(2,1)} %copy-done.11, bf16[512,768]{1,0:T(8,128)(2,1)} %copy-done.54, bf16[256,2048]{1,0:T(8,128)(2,1)} %copy-done.47, bf16[256,2048]{1,0:T(8,128)(2,1)} %copy-done.103, bf16[256,2048]{1,0:T(8,128)(2,1)} %copy-done.74, ...), custom_call_target="tpu_custom_call" | custom-call | flops 9663676416 | bytes 1024 | tf_op jit(solution)/shard_map/outer/pallas_call | solution.py:1058
  1072.9 21.9 %collective-permute-done.141.refs_0_.refs_18_ = bf16[256,2048]{1,0:T(8,128)(2,1)S(1)} collective-permute-done((bf16[256,2048]{1,0:T(8,128)(2,1)S(1)}, bf16[256,2048]{1,0:T(8,128)(2,1)S(1)}, u32[]{:S(2)}, u32[]{:S(2)}) %collective-permute-start.141) | collective-permute-done | bytes 1048608 | tf_op jit(solution)/shard_map/ppermute | solution.py:427
  1121.7 19.5 %attend_back.3 = (bf16[2,2,4,32,512]{4,3,2,1,0:T(8,128)(2,1)S(1)}, bf16[4,2,4,32,512]{4,3,2,1,0:T(8,128)(2,1)S(1)}, bf16[2,2,4,32,512]{4,3,2,1,0:T(8,128)(2,1)S(1)}, f32[2,2,128]{2,1,0:T(2,128)S(1)}) custom-call(s32[1]{0:T(128)} %bitcast.19.refs_0_, f32[2,2,4,32,512]{4,3,2,1,0:T(8,128)S(1)} %bitcast.366, f32[4,2,4,32,512]{4,3,2,1,0:T(8,128)S(1)} %bitcast.362, ...), custom_call_target="tpu_custom_call" | custom-call | flops 4294967296 | bytes 1024 | tf_op jit(solution)/shard_map/attend_back/pallas_call | solution.py:833
  1174.5 12.4 outer.7
  1231.2 16.6 %collective-permute-done.164.refs_3_ = bf16[2,1,768,256]{3,2,1,0:T(8,128)(2,1)S(1)} collective-permute-done((bf16[2,1,768,256]{3,2,1,0:T(8,128)(2,1)S(1)}, bf16[2,1,768,256]{3,2,1,0:T(8,128)(2,1)S(1)}, u32[]{:S(2)}, u32[]{:S(2)}) %collective-permute-start.164) | collective-permute-done | bytes 786464 | tf_op jit(solution)/shard_map/ppermute | solution.py:427
  1257.0 32.7 %collective-permute-done.168.refs_1_ = bf16[64,4096]{1,0:T(8,128)(2,1)S(1)} collective-permute-done((bf16[64,4096]{1,0:T(8,128)(2,1)S(1)}, bf16[64,4096]{1,0:T(8,128)(2,1)S(1)}, u32[]{:S(2)}, u32[]{:S(2)}) %collective-permute-start.168) | collective-permute-done | bytes 524320 | tf_op jit(solution)/shard_map/ppermute | solution.py:573
  1357.6 13.3 collective-permute-done.184.refs_3_
  (1157 shorter events, 752.4 us)
Async XLA Ops:
  7.2 134.2 %all-gather.5.cloned.1.call-start = ((), (), s32[]{:S(2)}) async-start(), calls=%async_computation.4 | async-start | bytes 3932160 | tf_op jit(solution)/shard_map/all_gather | solution.py:510
  20.3 327.3 %all-gather.7.cloned.1.call-start = ((), (), s32[]{:S(2)}) async-start(), calls=%async_computation.5 | async-start | bytes 11796480 | tf_op jit(solution)/shard_map/all_gather | solution.py:510
  84.1 52.0 %collective-permute-start.36 = (bf16[2,6,192,256]{3,2,1,0:T(8,128)(2,1)S(1)}, bf16[2,6,192,256]{3,2,1,0:T(8,128)(2,1)S(1)}, u32[]{:S(2)}, u32[]{:S(2)}) collective-permute-start(bf16[2,6,192,256]{3,2,1,0:T(8,128)(2,1)S(1)} %pad_maximum_fusion.7), channel_id=1, source_target_pairs={{0,24},{4,28},{8,16},{12,20},{16,8},{20,12},{24,0},{28,4},{1,25},{... | collective-permute-start | bytes 3538952 | tf_op jit(solution)/shard_map/ppermute | solution.py:427
  85.1 52.5 %collective-permute-start.37 = (bf16[2,6,192,256]{3,2,1,0:T(8,128)(2,1)S(1)}, bf16[2,6,192,256]{3,2,1,0:T(8,128)(2,1)S(1)}, u32[]{:S(2)}, u32[]{:S(2)}) collective-permute-start(bf16[2,6,192,256]{3,2,1,0:T(8,128)(2,1)S(1)} %pad_maximum_fusion.8), channel_id=1, source_target_pairs={{0,16},{4,20},{8,24},{12,28},{16,0},{20,4},{24,8},{28,12},{1,17},{... | collective-permute-start | bytes 3538952 | tf_op jit(solution)/shard_map/ppermute | solution.py:427
  86.4 51.2 %collective-permute-start.38 = (bf16[2,6,192,256]{3,2,1,0:T(8,128)(2,1)S(1)}, bf16[2,6,192,256]{3,2,1,0:T(8,128)(2,1)S(1)}, u32[]{:S(2)}, u32[]{:S(2)}) collective-permute-start(bf16[2,6,192,256]{3,2,1,0:T(8,128)(2,1)S(1)} %pad_maximum_fusion.9), channel_id=1, source_target_pairs={{0,8},{4,12},{8,0},{12,4},{16,24},{20,28},{24,16},{28,20},{1,9},{5... | collective-permute-start | bytes 3538952 | tf_op jit(solution)/shard_map/ppermute | solution.py:427
  88.2 36.5 %collective-permute-start.4 = (bf16[64,4096]{1,0:T(8,128)(2,1)S(1)}, bf16[64,4096]{1,0:T(8,128)(2,1)S(1)}, u32[]{:S(2)}, u32[]{:S(2)}) collective-permute-start(bf16[64,4096]{1,0:T(8,128)(2,1)S(1)} %get-tuple-element.613), channel_id=1, source_target_pairs={{0,1},{1,2},{2,3},{3,0},{4,5},{5,6},{6,7},{7,4},{8,9},{9,10},{10,1... | collective-permute-start | bytes 1572872 | tf_op jit(solution)/shard_map/ppermute | solution.py:573
  89.8 43.5 %collective-permute-start.5 = (bf16[64,4096]{1,0:T(8,128)(2,1)S(1)}, bf16[64,4096]{1,0:T(8,128)(2,1)S(1)}, u32[]{:S(2)}, u32[]{:S(2)}) collective-permute-start(bf16[64,4096]{1,0:T(8,128)(2,1)S(1)} %get-tuple-element.612), channel_id=1, source_target_pairs={{0,2},{1,3},{2,0},{3,1},{4,6},{5,7},{6,4},{7,5},{8,10},{9,11},{10,... | collective-permute-start | bytes 1572872 | tf_op jit(solution)/shard_map/ppermute | solution.py:573
  141.4 265.7 %all-gather.9.cloned.1.call-start = ((), (), s32[]{:S(2)}) async-start(), calls=%async_computation.6 | async-start | bytes 3932160 | tf_op jit(solution)/shard_map/all_gather | solution.py:510
  162.4 52.2 %collective-permute-start.9 = (bf16[2,1,768,256]{3,2,1,0:T(8,128)(2,1)S(1)}, bf16[2,1,768,256]{3,2,1,0:T(8,128)(2,1)S(1)}, u32[]{:S(2)}, u32[]{:S(2)}) collective-permute-start(bf16[2,1,768,256]{3,2,1,0:T(8,128)(2,1)S(1)} %pad_maximum_fusion.32), channel_id=1, source_target_pairs={{0,8},{4,12},{8,0},{12,4},{16,24},{20,28},{24,16},{28,20},{1,9},{5... | collective-permute-start | bytes 2359304 | tf_op jit(solution)/shard_map/ppermute | solution.py:427
  187.8 45.6 %collective-permute-start.10 = (bf16[2,1,768,256]{3,2,1,0:T(8,128)(2,1)S(1)}, bf16[2,1,768,256]{3,2,1,0:T(8,128)(2,1)S(1)}, u32[]{:S(2)}, u32[]{:S(2)}) collective-permute-start(bf16[2,1,768,256]{3,2,1,0:T(8,128)(2,1)S(1)} %pad_maximum_fusion.33), channel_id=1, source_target_pairs={{0,16},{4,20},{8,24},{12,28},{16,0},{20,4},{24,8},{28,12},{1,17},{... | collective-permute-start | bytes 2359304 | tf_op jit(solution)/shard_map/ppermute | solution.py:427
  189.4 44.0 %collective-permute-start.11 = (bf16[2,1,768,256]{3,2,1,0:T(8,128)(2,1)S(1)}, bf16[2,1,768,256]{3,2,1,0:T(8,128)(2,1)S(1)}, u32[]{:S(2)}, u32[]{:S(2)}) collective-permute-start(bf16[2,1,768,256]{3,2,1,0:T(8,128)(2,1)S(1)} %pad_maximum_fusion.34), channel_id=1, source_target_pairs={{0,24},{4,28},{8,16},{12,20},{16,8},{20,12},{24,0},{28,4},{1,25},{... | collective-permute-start | bytes 2359304 | tf_op jit(solution)/shard_map/ppermute | solution.py:427
  286.4 327.9 %all-gather.11.cloned.1.call-start = ((), (), s32[]{:S(2)}) async-start(), calls=%async_computation.7 | async-start | bytes 11796480 | tf_op jit(solution)/shard_map/all_gather | solution.py:510
  312.2 34.4 %collective-permute-start.39 = (bf16[256,2048]{1,0:T(8,128)(2,1)S(1)}, bf16[256,2048]{1,0:T(8,128)(2,1)S(1)}, u32[]{:S(2)}, u32[]{:S(2)}) collective-permute-start(bf16[256,2048]{1,0:T(8,128)(2,1)S(1)} %multiply_convert_fusion.2.refs_0_.refs_3_), channel_id=1, source_target_pairs={{0,4},{4,0},{8,12},{12,8},{16,20},{20,16},{24,28},{28,24},{1,5},{5... | collective-permute-start | bytes 3145736 | tf_op jit(solution)/shard_map/ppermute | solution.py:427
  389.5 593.8 %reduce-scatter.5.cloned.1.call-start = ((), (), s32[]{:S(2)}) async-start(), calls=%async_computation.8 | async-start | bytes 11796480 | tf_op jit(solution)/shard_map/reduce_scatter | solution.py:514
  434.0 41.2 %collective-permute-start.54 = (bf16[2,1,768,256]{3,2,1,0:T(8,128)(2,1)S(1)}, bf16[2,1,768,256]{3,2,1,0:T(8,128)(2,1)S(1)}, u32[]{:S(2)}, u32[]{:S(2)}) collective-permute-start(bf16[2,1,768,256]{3,2,1,0:T(8,128)(2,1)S(1)} %pad_maximum_fusion.36), channel_id=1, source_target_pairs={{0,8},{4,12},{8,0},{12,4},{16,24},{20,28},{24,16},{28,20},{1,9},{5... | collective-permute-start | bytes 2359304 | tf_op jit(solution)/shard_map/ppermute | solution.py:427
  460.2 40.9 %collective-permute-start.55 = (bf16[2,1,768,256]{3,2,1,0:T(8,128)(2,1)S(1)}, bf16[2,1,768,256]{3,2,1,0:T(8,128)(2,1)S(1)}, u32[]{:S(2)}, u32[]{:S(2)}) collective-permute-start(bf16[2,1,768,256]{3,2,1,0:T(8,128)(2,1)S(1)} %pad_maximum_fusion.37), channel_id=1, source_target_pairs={{0,16},{4,20},{8,24},{12,28},{16,0},{20,4},{24,8},{28,12},{1,17},{... | collective-permute-start | bytes 2359304 | tf_op jit(solution)/shard_map/ppermute | solution.py:427
  461.8 39.3 %collective-permute-start.56 = (bf16[2,1,768,256]{3,2,1,0:T(8,128)(2,1)S(1)}, bf16[2,1,768,256]{3,2,1,0:T(8,128)(2,1)S(1)}, u32[]{:S(2)}, u32[]{:S(2)}) collective-permute-start(bf16[2,1,768,256]{3,2,1,0:T(8,128)(2,1)S(1)} %pad_maximum_fusion.38), channel_id=1, source_target_pairs={{0,24},{4,28},{8,16},{12,20},{16,8},{20,12},{24,0},{28,4},{1,25},{... | collective-permute-start | bytes 2359304 | tf_op jit(solution)/shard_map/ppermute | solution.py:427
  733.8 329.1 %reduce-scatter.7.cloned.1.call-start = ((), (), s32[]{:S(2)}) async-start(), calls=%async_computation.9 | async-start | bytes 3932160 | tf_op jit(solution)/shard_map/reduce_scatter | solution.py:514
  791.8 37.2 %collective-permute-start.106 = (bf16[256,2048]{1,0:T(8,128)(2,1)S(1)}, bf16[256,2048]{1,0:T(8,128)(2,1)S(1)}, u32[]{:S(2)}, u32[]{:S(2)}) collective-permute-start(bf16[256,2048]{1,0:T(8,128)(2,1)S(1)} %pad_maximum_fusion.23), channel_id=1, source_target_pairs={{0,16},{4,20},{8,24},{12,28},{16,0},{20,4},{24,8},{28,12},{1,17},{... | collective-permute-start | bytes 3145736 | tf_op jit(solution)/shard_map/ppermute | solution.py:427
  793.6 35.3 %collective-permute-start.105 = (bf16[256,2048]{1,0:T(8,128)(2,1)S(1)}, bf16[256,2048]{1,0:T(8,128)(2,1)S(1)}, u32[]{:S(2)}, u32[]{:S(2)}) collective-permute-start(bf16[256,2048]{1,0:T(8,128)(2,1)S(1)} %pad_maximum_fusion.22), channel_id=1, source_target_pairs={{0,8},{4,12},{8,0},{12,4},{16,24},{20,28},{24,16},{28,20},{1,9},{5... | collective-permute-start | bytes 3145736 | tf_op jit(solution)/shard_map/ppermute | solution.py:427
  944.7 36.2 %collective-permute-start.180 = (bf16[2,1,768,256]{3,2,1,0:T(8,128)(2,1)S(1)}, bf16[2,1,768,256]{3,2,1,0:T(8,128)(2,1)S(1)}, u32[]{:S(2)}, u32[]{:S(2)}) collective-permute-start(bf16[2,1,768,256]{3,2,1,0:T(8,128)(2,1)S(1)} %pad_maximum_fusion.43), channel_id=1, source_target_pairs={{0,16},{4,20},{8,24},{12,28},{16,0},{20,4},{24,8},{28,12},{1,17},{... | collective-permute-start | bytes 2359304 | tf_op jit(solution)/shard_map/ppermute | solution.py:427
  945.2 35.7 %collective-permute-start.181 = (bf16[2,1,768,256]{3,2,1,0:T(8,128)(2,1)S(1)}, bf16[2,1,768,256]{3,2,1,0:T(8,128)(2,1)S(1)}, u32[]{:S(2)}, u32[]{:S(2)}) collective-permute-start(bf16[2,1,768,256]{3,2,1,0:T(8,128)(2,1)S(1)} %pad_maximum_fusion.44), channel_id=1, source_target_pairs={{0,24},{4,28},{8,16},{12,20},{16,8},{20,12},{24,0},{28,4},{1,25},{... | collective-permute-start | bytes 2359304 | tf_op jit(solution)/shard_map/ppermute | solution.py:427
  983.4 329.7 %reduce-scatter.9.cloned.1.call-start = ((), (), s32[]{:S(2)}) async-start(), calls=%async_computation.10 | async-start | bytes 11796480 | tf_op jit(solution)/shard_map/reduce_scatter | solution.py:514
  1062.9 319.8 %reduce-scatter.11.cloned.1.call-start = ((), (), s32[]{:S(2)}) async-start(), calls=%async_computation.11 | async-start | bytes 3932160 | tf_op jit(solution)/shard_map/reduce_scatter | solution.py:514
  1211.5 36.3 %collective-permute-start.164 = (bf16[2,1,768,256]{3,2,1,0:T(8,128)(2,1)S(1)}, bf16[2,1,768,256]{3,2,1,0:T(8,128)(2,1)S(1)}, u32[]{:S(2)}, u32[]{:S(2)}) collective-permute-start(bf16[2,1,768,256]{3,2,1,0:T(8,128)(2,1)S(1)} %pad_maximum_fusion.40), channel_id=1, source_target_pairs={{0,16},{4,20},{8,24},{12,28},{16,0},{20,4},{24,8},{28,12},{1,17},{... | collective-permute-start | bytes 2359304 | tf_op jit(solution)/shard_map/ppermute | solution.py:427
  1212.6 35.1 %collective-permute-start.165 = (bf16[2,1,768,256]{3,2,1,0:T(8,128)(2,1)S(1)}, bf16[2,1,768,256]{3,2,1,0:T(8,128)(2,1)S(1)}, u32[]{:S(2)}, u32[]{:S(2)}) collective-permute-start(bf16[2,1,768,256]{3,2,1,0:T(8,128)(2,1)S(1)} %pad_maximum_fusion.41), channel_id=1, source_target_pairs={{0,24},{4,28},{8,16},{12,20},{16,8},{20,12},{24,0},{28,4},{1,25},{... | collective-permute-start | bytes 2359304 | tf_op jit(solution)/shard_map/ppermute | solution.py:427
  1252.3 37.4 %collective-permute-start.168 = (bf16[64,4096]{1,0:T(8,128)(2,1)S(1)}, bf16[64,4096]{1,0:T(8,128)(2,1)S(1)}, u32[]{:S(2)}, u32[]{:S(2)}) collective-permute-start(bf16[64,4096]{1,0:T(8,128)(2,1)S(1)} %get-tuple-element.609), channel_id=1, source_target_pairs={{0,1},{1,2},{2,3},{3,0},{4,5},{5,6},{6,7},{7,4},{8,9},{9,10},{10,1... | collective-permute-start | bytes 1572872 | tf_op jit(solution)/shard_map/ppermute | solution.py:573
  1254.8 44.0 %collective-permute-start.169 = (bf16[64,4096]{1,0:T(8,128)(2,1)S(1)}, bf16[64,4096]{1,0:T(8,128)(2,1)S(1)}, u32[]{:S(2)}, u32[]{:S(2)}) collective-permute-start(bf16[64,4096]{1,0:T(8,128)(2,1)S(1)} %get-tuple-element.608), channel_id=1, source_target_pairs={{0,2},{1,3},{2,0},{3,1},{4,6},{5,7},{6,4},{7,5},{8,10},{9,11},{10,... | collective-permute-start | bytes 1572872 | tf_op jit(solution)/shard_map/ppermute | solution.py:573
  1255.9 44.0 %collective-permute-start.170 = (bf16[64,4096]{1,0:T(8,128)(2,1)S(1)}, bf16[64,4096]{1,0:T(8,128)(2,1)S(1)}, u32[]{:S(2)}, u32[]{:S(2)}) collective-permute-start(bf16[64,4096]{1,0:T(8,128)(2,1)S(1)} %get-tuple-element.607), channel_id=1, source_target_pairs={{0,3},{1,0},{2,1},{3,2},{4,7},{5,4},{6,5},{7,6},{8,11},{9,8},{10,9... | collective-permute-start | bytes 1572872 | tf_op jit(solution)/shard_map/ppermute | solution.py:573
  1324.9 32.7 %collective-permute-start.183 = (bf16[2,3,192,256]{3,2,1,0:T(8,128)(2,1)}, bf16[2,3,192,256]{3,2,1,0:T(8,128)(2,1)}, u32[]{:S(2)}, u32[]{:S(2)}) collective-permute-start(bf16[2,3,192,256]{3,2,1,0:T(8,128)(2,1)} %pad_maximum_fusion.48), channel_id=1, source_target_pairs={{0,8},{4,12},{8,0},{12,4},{16,24},{20,28},{24,16},{28,20},{1,9},{5... | collective-permute-start | bytes 1769480 | tf_op jit(solution)/shard_map/ppermute | solution.py:427
  1326.9 44.0 %collective-permute-start.184 = (bf16[2,3,192,256]{3,2,1,0:T(8,128)(2,1)}, bf16[2,3,192,256]{3,2,1,0:T(8,128)(2,1)}, u32[]{:S(2)}, u32[]{:S(2)}) collective-permute-start(bf16[2,3,192,256]{3,2,1,0:T(8,128)(2,1)} %pad_maximum_fusion.49), channel_id=1, source_target_pairs={{0,16},{4,20},{8,24},{12,28},{16,0},{20,4},{24,8},{28,12},{1,17},{... | collective-permute-start | bytes 1769480 | tf_op jit(solution)/shard_map/ppermute | solution.py:427
  1334.4 36.6 %collective-permute-start.185 = (bf16[2,3,192,256]{3,2,1,0:T(8,128)(2,1)}, bf16[2,3,192,256]{3,2,1,0:T(8,128)(2,1)}, u32[]{:S(2)}, u32[]{:S(2)}) collective-permute-start(bf16[2,3,192,256]{3,2,1,0:T(8,128)(2,1)} %pad_maximum_fusion.50), channel_id=1, source_target_pairs={{0,24},{4,28},{8,16},{12,20},{16,8},{20,12},{24,0},{28,4},{1,25},{... | collective-permute-start | bytes 1769480 | tf_op jit(solution)/shard_map/ppermute | solution.py:427
  (402 other events, 5198.5 us)
Sparse Core Ops, SparseCore 0:
  20.4 62.4 all-gather.4
  141.5 163.2 all-gather.6
  306.4 62.3 all-gather.8
  389.7 163.4 all-gather.10
  733.9 161.2 reduce-scatter.4
  983.5 59.7 reduce-scatter.6
  1063.0 163.1 reduce-scatter.8
  1313.2 59.7 reduce-scatter.10

commit v3 on v2

--- a/solution.py
+++ b/solution.py
@@ -465,7 +465,7 @@
     return (sets[0], d) if d < 2 else (sets[1], d - 2) if d < 6 else (sets[2], d - 6)
 
 
-def reduce_plane(part):
+def reduce_plane(part, join=()):
     odd = part((7, 5, 3, 1), None)
     received = [plane_send(v, 1) for v in odd]
     (far,) = part((6,), received[:1])
@@ -476,10 +476,10 @@
     by_y, by_x, here = part((4, 2, 0), received[1:])
     by_y = jnp.concatenate([add_low(by_y[:half], top), by_y[half:]])
     by_x = jnp.concatenate([by_x[:half], add_low(by_x[half:], bottom)])
-    by_x, by_y = lax.optimization_barrier((by_x, by_y))
+    by_x, by_y, join = lax.optimization_barrier((by_x, by_y, join))
     from_x = plane_send(by_x, 2)
     from_y = plane_send(by_y, 4)
-    return wide(here) + wide(from_x) + wide(from_y), far, by_x
+    return wide(here) + wide(from_x) + wide(from_y), far, join
 
 
 def sum_line(values):
@@ -552,9 +552,9 @@
     (array,) = after(start, array)
     pieces = [block_at(array, places[d], block, axis) for d in range(size)]
     other = plane_send(jnp.stack(pieces[1::2]), 1)
+    chips = [plane_send(jnp.stack([pieces[d], other[d // 2]]), d) for d in (6, 4, 2)]
     if first is not None:
-        first.append(other)
-    chips = [plane_send(jnp.stack([pieces[d], other[d // 2]]), d) for d in (6, 4, 2)]
+        first.extend(chips)
     other, *chips = after(done, other[0], *chips)
     sets = [(pieces[0], (None,)), (other, (None,))] + [(v, (0, 1)) for v in reversed(chips)]
     return assemble(sets, pieces[0].shape, into, places)
@@ -612,8 +612,7 @@
         ],
         axis=1,
     )
-    gathered = line_gather(pack)
-    return swap(gathered, 0, 2)[0], gathered
+    return line_gather(pack)
 
 
 def turn(values, cosine, sine):
@@ -1119,23 +1118,27 @@
 
     def fetch_attn(index, token):
         shards = (query_weight[index], key_matrix[index], value_matrix[index], out_weight[index])
-        attn_sets[index], attn_gathered[index] = attention_weights(*after(token, *shards))
+        attn_gathered[index] = attention_weights(*after(token, *shards))
 
     fetch_attn(0, None)
     exchanged = []
     both = jnp.concatenate([tokens, cotangent], axis=1)
     both = swap(both, 0, 0, None, None, exchanged)
+    gate_weight, up_weight, down_weight = after(
+        tuple(exchanged), gate_weight, up_weight, down_weight
+    )
     hidden_shards = jnp.stack(
         [gate_weight.swapaxes(1, 2), up_weight.swapaxes(1, 2), down_weight], axis=1
     ).reshape(-1, *down_weight.shape[1:])
     both = line_rows(both)
+    both, attn_gathered[0] = lax.optimization_barrier((both, attn_gathered[0]))
     hidden_shards, first = lax.optimization_barrier((hidden_shards, first))
-    hidden_shards = swap(hidden_shards, 1, 2, exchanged[0], both)
+    hidden_shards = swap(hidden_shards, 1, 2, None, both)
     hidden_shards = hidden_shards.reshape(layers, -1, *hidden_shards.shape[1:])
     residual, grad = wide(both[:, : tokens.shape[1]]), wide(both[:, tokens.shape[1] :])
     saved = []
     for index in range(layers):
-        pack = attn_sets[index]
+        attn_sets[index] = pack = swap(attn_gathered[index], 0, 2)[0]
         gains = (query_gain[index][None], key_gain[index][None])
         normed, attn_back = jax.vjp(rms_scale, residual, attn_gain[index])
         rows = gather_plane(low(normed))
@@ -1183,8 +1186,11 @@
             (gate_grads, weights, rows_spec(0, weights)),
             (up_grads, weights, rows_spec(1, weights)),
         ]
-        normed_grad, token, *_ = reduce_plane(
-            lambda ds, adds: parts_of(unit_terms, ds, adds)
+        above = ()
+        if index + 1 < layers:
+            above = swap(pack_grads[index + 1][None], 2, 0, gate_grads[2])
+        normed_grad, token, above = reduce_plane(
+            lambda ds, adds: parts_of(unit_terms, ds, adds), above
         )
         (held,) = after(token, gate_grads[0])
         terms = outer(
@@ -1198,9 +1204,7 @@
         normed_grad, terms = lax.optimization_barrier((normed_grad, terms))
         if index + 1 < layers:
             done = hidden_sums[index + 1]
-            above = swap(pack_grads[index + 1][None], 2, 0, gate_grads[1])
             pack_sums[index + 1] = line_reduce(after(done, above)[0])
-            (terms,) = after(pack_sums[index + 1], terms)
         hidden_sums[index] = line_reduce(terms, 1)
         grad_part, mlp_gain_grad = mlp_back(normed_grad)
         grad = grad + grad_part

time: 1410 us -> 1400 us (level)
    unnamed x486 -> x492, local copies, waits for them, and re-layouts: 75.5 us -> 60.7 us
  transfers between devices with their start and end apart: 194 -> 194, of which waited for: 101 -> 100; matrix products, arithmetic and copies ran while one was open for 10% -> 10% of each run, Pallas kernels for 23% -> 23%
where the time goes in v3:
time: 1400 us; the launch traced here: 1390 us
  waiting for transfers between devices  665 us (48%)
  Pallas kernels  333 us (24%)
  starting transfers between devices  132 us (9%)
  local copies, waits for them, and re-layouts  123 us (9%)
  other arithmetic  85.5 us (6%)
  between operations  49 us (4%)
    ppermute x178, waiting for transfers between devices, plane_send(): lax.ppermute(values, 'fsdp', [(i, i ^ distance) for i in range(size)])  571 us
    ppermute x178, starting transfers between devices, plane_send(): lax.ppermute(values, 'fsdp', [(i, i ^ distance) for i in range(size)])  121 us
    ppermute x6, waiting for transfers between devices, line_swap(): moved.append(lax.ppermute(piece, 'tp', pairs))  88.4 us
    pallas_call x24, Pallas kernels, parts_of(): pl.pallas_call(functools.partial(parts_kernel, len(ds), len(terms), adds...  88 us
    pallas_call x4, Pallas kernels, outer(): pl.pallas_call(functools.partial(outer_kernel, plan), grid=(shape[-1] //...  79.8 us
    unnamed x492, local copies, waits for them, and re-layouts  60.7 us
    pallas_call x2, Pallas kernels, plane_attend_back(): pl.pallas_call(functools.partial(attend_back_kernel, groups, heads, rows)...  39.5 us
    pallas_call x6, Pallas kernels, hidden_units(): pl.pallas_call(functools.partial(units_kernel, len(pieces)), grid=(weight...  39.3 us
  transfers between devices with their start and end apart: 194, of which 100 were waited for; matrix products, arithmetic and copies ran while one was open for 10% of the time, Pallas kernels for 23%

profile of v3, /device:TPU:8, one launch (start us, length us, event | category | flops | bytes accessed | tf_op | source)
XLA Modules:
  0.0 1388.3 jit_solution(653425988184768367)
XLA Ops:
  90.4 33.7 %collective-permute-done.4.refs_1_ = bf16[64,4096]{1,0:T(8,128)(2,1)S(1)} collective-permute-done((bf16[64,4096]{1,0:T(8,128)(2,1)S(1)}, bf16[64,4096]{1,0:T(8,128)(2,1)S(1)}, u32[]{:S(2)}, u32[]{:S(2)}) %collective-permute-start.4) | collective-permute-done | bytes 524320 | tf_op jit(solution)/shard_map/ppermute | solution.py:573
  163.1 23.1 %collective-permute-done.12.refs_0_.refs_5_ = bf16[256,2048]{1,0:T(8,128)(2,1)S(1)} collective-permute-done((bf16[256,2048]{1,0:T(8,128)(2,1)S(1)}, bf16[256,2048]{1,0:T(8,128)(2,1)S(1)}, u32[]{:S(2)}, u32[]{:S(2)}) %collective-permute-start.12) | collective-permute-done | bytes 1048608 | tf_op jit(solution)/shard_map/ppermute | solution.py:427
  191.0 23.3 %collective-permute-done.16.refs_0_.refs_9_ = bf16[128,2048]{1,0:T(8,128)(2,1)S(1)} collective-permute-done((bf16[128,2048]{1,0:T(8,128)(2,1)S(1)}, bf16[128,2048]{1,0:T(8,128)(2,1)S(1)}, u32[]{:S(2)}, u32[]{:S(2)}) %collective-permute-start.16) | collective-permute-done | bytes 524320 | tf_op jit(solution)/shard_map/ppermute | solution.py:427
  215.0 16.7 %collective-permute-done.10.refs_3_ = bf16[2,1,768,256]{3,2,1,0:T(8,128)(2,1)S(1)} collective-permute-done((bf16[2,1,768,256]{3,2,1,0:T(8,128)(2,1)S(1)}, bf16[2,1,768,256]{3,2,1,0:T(8,128)(2,1)S(1)}, u32[]{:S(2)}, u32[]{:S(2)}) %collective-permute-start.10) | collective-permute-done | bytes 786464 | tf_op jit(solution)/shard_map/ppermute | solution.py:427
  244.9 11.7 attend.2
  285.1 17.9 %collective-permute-done.30 = bf16[256,2048]{1,0:T(8,128)(2,1)} collective-permute-done((bf16[256,2048]{1,0:T(8,128)(2,1)S(1)}, bf16[256,2048]{1,0:T(8,128)(2,1)}, u32[]{:S(2)}, u32[]{:S(2)}) %collective-permute-start.30) | collective-permute-done | bytes 1048608 | tf_op jit(solution)/shard_map/ppermute | solution.py:427
  310.5 20.9 %collective-permute-done.31.refs_0_.refs_5_ = bf16[256,2048]{1,0:T(8,128)(2,1)S(1)} collective-permute-done((bf16[256,2048]{1,0:T(8,128)(2,1)S(1)}, bf16[256,2048]{1,0:T(8,128)(2,1)S(1)}, u32[]{:S(2)}, u32[]{:S(2)}) %collective-permute-start.31) | collective-permute-done | bytes 1048608 | tf_op jit(solution)/shard_map/ppermute | solution.py:427
  363.6 10.4 hidden_units.6
  407.8 19.7 %collective-permute-done.51 = bf16[256,2048]{1,0:T(8,128)(2,1)S(1)} collective-permute-done((bf16[256,2048]{1,0:T(8,128)(2,1)S(1)}, bf16[256,2048]{1,0:T(8,128)(2,1)S(1)}, u32[]{:S(2)}, u32[]{:S(2)}) %collective-permute-start.51) | collective-permute-done | bytes 1048608 | tf_op jit(solution)/shard_map/ppermute | solution.py:427
  433.8 22.8 %collective-permute-done.57.refs_0_.refs_5_ = bf16[256,2048]{1,0:T(8,128)(2,1)S(1)} collective-permute-done((bf16[256,2048]{1,0:T(8,128)(2,1)S(1)}, bf16[256,2048]{1,0:T(8,128)(2,1)S(1)}, u32[]{:S(2)}, u32[]{:S(2)}) %collective-permute-start.57) | collective-permute-done | bytes 1048608 | tf_op jit(solution)/shard_map/ppermute | solution.py:427
  461.7 11.8 collective-permute-done.54.refs_2_
  473.5 11.2 collective-permute-done.61.refs_0_.refs_9_
  485.2 14.0 %collective-permute-done.55.refs_3_ = bf16[2,1,768,256]{3,2,1,0:T(8,128)(2,1)S(1)} collective-permute-done((bf16[2,1,768,256]{3,2,1,0:T(8,128)(2,1)S(1)}, bf16[2,1,768,256]{3,2,1,0:T(8,128)(2,1)S(1)}, u32[]{:S(2)}, u32[]{:S(2)}) %collective-permute-start.55) | collective-permute-done | bytes 786464 | tf_op jit(solution)/shard_map/ppermute | solution.py:427
  507.5 12.1 attend.3
  543.2 21.9 %collective-permute-done.72 = bf16[256,2048]{1,0:T(8,128)(2,1)S(1)} collective-permute-done((bf16[256,2048]{1,0:T(8,128)(2,1)S(1)}, bf16[256,2048]{1,0:T(8,128)(2,1)S(1)}, u32[]{:S(2)}, u32[]{:S(2)}) %collective-permute-start.72) | collective-permute-done | bytes 1048608 | tf_op jit(solution)/shard_map/ppermute | solution.py:427
  569.1 21.1 %collective-permute-done.73.refs_0_.refs_5_ = bf16[256,2048]{1,0:T(8,128)(2,1)} collective-permute-done((bf16[256,2048]{1,0:T(8,128)(2,1)S(1)}, bf16[256,2048]{1,0:T(8,128)(2,1)}, u32[]{:S(2)}, u32[]{:S(2)}) %collective-permute-start.73) | collective-permute-done | bytes 1048608 | tf_op jit(solution)/shard_map/ppermute | solution.py:427
  700.9 27.4 %outer.4 = bf16[3,768,2048]{2,1,0:T(8,128)(2,1)} custom-call(bf16[512,768]{1,0:T(8,128)(2,1)} %copy-done.60, bf16[1024,768]{1,0:T(8,128)(2,1)} %copy-done.13, bf16[512,768]{1,0:T(8,128)(2,1)} %copy-done.54, bf16[256,2048]{1,0:T(8,128)(2,1)} %copy-done.45, bf16[256,2048]{1,0:T(8,128)(2,1)} %copy-done.106, ...), custom_call_target="tpu_custom_call" | custom-call | flops 9663676416 | bytes 1024 | tf_op jit(solution)/shard_map/outer/pallas_call | solution.py:1057
  748.1 23.2 %collective-permute-done.107.refs_0_.refs_18_ = bf16[256,2048]{1,0:T(8,128)(2,1)} collective-permute-done((bf16[256,2048]{1,0:T(8,128)(2,1)}, bf16[256,2048]{1,0:T(8,128)(2,1)}, u32[]{:S(2)}, u32[]{:S(2)}) %collective-permute-start.107) | collective-permute-done | bytes 1048608 | tf_op jit(solution)/shard_map/ppermute | solution.py:427
  813.6 19.8 %attend_back.2 = (bf16[2,2,4,32,512]{4,3,2,1,0:T(8,128)(2,1)S(1)}, bf16[4,2,4,32,512]{4,3,2,1,0:T(8,128)(2,1)S(1)}, bf16[2,2,4,32,512]{4,3,2,1,0:T(8,128)(2,1)S(1)}, f32[2,2,128]{2,1,0:T(2,128)S(1)}) custom-call(s32[1]{0:T(128)} %bitcast.29.refs_0_, f32[2,2,4,32,512]{4,3,2,1,0:T(8,128)S(1)} %bitcast.370, f32[4,2,4,32,512]{4,3,2,1,0:T(8,128)S(1)} %bitcast.364, ...), custom_call_target="tpu_custom_call" | custom-call | flops 4294967296 | bytes 1024 | tf_op jit(solution)/shard_map/attend_back/pallas_call | solution.py:832
  861.7 12.6 outer.5
  874.3 10.2 collective-permute-done.123
  897.8 19.9 %collective-permute-done.124.refs_0_.refs_21_ = bf16[256,2048]{1,0:T(8,128)(2,1)S(1)} collective-permute-done((bf16[256,2048]{1,0:T(8,128)(2,1)S(1)}, bf16[256,2048]{1,0:T(8,128)(2,1)S(1)}, u32[]{:S(2)}, u32[]{:S(2)}) %collective-permute-start.124) | collective-permute-done | bytes 1048608 | tf_op jit(solution)/shard_map/ppermute | solution.py:427
  989.1 14.3 %collective-permute-done.140.refs_2_ = bf16[2,1,768,256]{3,2,1,0:T(8,128)(2,1)S(1)} collective-permute-done((bf16[2,1,768,256]{3,2,1,0:T(8,128)(2,1)S(1)}, bf16[2,1,768,256]{3,2,1,0:T(8,128)(2,1)S(1)}, u32[]{:S(2)}, u32[]{:S(2)}) %collective-permute-start.140) | collective-permute-done | bytes 786464 | tf_op jit(solution)/shard_map/ppermute | solution.py:427
  1003.4 16.3 %collective-permute-done.141.refs_3_ = bf16[2,1,768,256]{3,2,1,0:T(8,128)(2,1)S(1)} collective-permute-done((bf16[2,1,768,256]{3,2,1,0:T(8,128)(2,1)S(1)}, bf16[2,1,768,256]{3,2,1,0:T(8,128)(2,1)S(1)}, u32[]{:S(2)}, u32[]{:S(2)}) %collective-permute-start.141) | collective-permute-done | bytes 786464 | tf_op jit(solution)/shard_map/ppermute | solution.py:427
  1024.2 27.5 %outer.6 = bf16[3,768,2048]{2,1,0:T(8,128)(2,1)} custom-call(bf16[512,768]{1,0:T(8,128)(2,1)} %copy-done.56, bf16[1024,768]{1,0:T(8,128)(2,1)} %copy-done.10, bf16[512,768]{1,0:T(8,128)(2,1)} %copy-done.51, bf16[256,2048]{1,0:T(8,128)(2,1)} %copy-done.44, bf16[256,2048]{1,0:T(8,128)(2,1)} %copy-done.101, bf16[256,2048]{1,0:T(8,128)(2,1)} %copy-done.74, ...), custom_call_target="tpu_custom_call" | custom-call | flops 9663676416 | bytes 1024 | tf_op jit(solution)/shard_map/outer/pallas_call | solution.py:1057
  1064.9 21.9 %collective-permute-done.145.refs_0_.refs_18_ = bf16[256,2048]{1,0:T(8,128)(2,1)S(1)} collective-permute-done((bf16[256,2048]{1,0:T(8,128)(2,1)S(1)}, bf16[256,2048]{1,0:T(8,128)(2,1)S(1)}, u32[]{:S(2)}, u32[]{:S(2)}) %collective-permute-start.145) | collective-permute-done | bytes 1048608 | tf_op jit(solution)/shard_map/ppermute | solution.py:427
  1113.8 19.8 %attend_back.3 = (bf16[2,2,4,32,512]{4,3,2,1,0:T(8,128)(2,1)S(1)}, bf16[4,2,4,32,512]{4,3,2,1,0:T(8,128)(2,1)S(1)}, bf16[2,2,4,32,512]{4,3,2,1,0:T(8,128)(2,1)S(1)}, f32[2,2,128]{2,1,0:T(2,128)S(1)}) custom-call(s32[1]{0:T(128)} %bitcast.29.refs_0_, f32[2,2,4,32,512]{4,3,2,1,0:T(8,128)S(1)} %bitcast.366, f32[4,2,4,32,512]{4,3,2,1,0:T(8,128)S(1)} %bitcast.362, ...), custom_call_target="tpu_custom_call" | custom-call | flops 4294967296 | bytes 1024 | tf_op jit(solution)/shard_map/attend_back/pallas_call | solution.py:832
  1166.1 12.4 outer.7
  1178.5 10.4 collective-permute-done.165
  1222.4 15.7 %collective-permute-done.168.refs_3_ = bf16[2,1,768,256]{3,2,1,0:T(8,128)(2,1)S(1)} collective-permute-done((bf16[2,1,768,256]{3,2,1,0:T(8,128)(2,1)S(1)}, bf16[2,1,768,256]{3,2,1,0:T(8,128)(2,1)S(1)}, u32[]{:S(2)}, u32[]{:S(2)}) %collective-permute-start.168) | collective-permute-done | bytes 786464 | tf_op jit(solution)/shard_map/ppermute | solution.py:427
  1247.7 32.6 %collective-permute-done.172.refs_1_ = bf16[64,4096]{1,0:T(8,128)(2,1)S(1)} collective-permute-done((bf16[64,4096]{1,0:T(8,128)(2,1)S(1)}, bf16[64,4096]{1,0:T(8,128)(2,1)S(1)}, u32[]{:S(2)}, u32[]{:S(2)}) %collective-permute-start.172) | collective-permute-done | bytes 524320 | tf_op jit(solution)/shard_map/ppermute | solution.py:573
  1349.7 13.5 collective-permute-done.184.refs_3_
  (1165 shorter events, 749.6 us)
Async XLA Ops:
  7.2 130.2 %all-gather.5.cloned.1.call-start = ((), (), s32[]{:S(2)}) async-start(), calls=%async_computation.4 | async-start | bytes 3932160 | tf_op jit(solution)/shard_map/all_gather | solution.py:510
  25.5 320.9 %all-gather.7.cloned.1.call-start = ((), (), s32[]{:S(2)}) async-start(), calls=%async_computation.5 | async-start | bytes 11796480 | tf_op jit(solution)/shard_map/all_gather | solution.py:510
  81.6 55.8 %collective-permute-start.36 = (bf16[2,6,192,256]{3,2,1,0:T(8,128)(2,1)}, bf16[2,6,192,256]{3,2,1,0:T(8,128)(2,1)S(1)}, u32[]{:S(2)}, u32[]{:S(2)}) collective-permute-start(bf16[2,6,192,256]{3,2,1,0:T(8,128)(2,1)} %pad_maximum_fusion.7), channel_id=1, source_target_pairs={{0,24},{4,28},{8,16},{12,20},{16,8},{20,12},{24,0},{28,4},{1,25},{... | collective-permute-start | bytes 3538952 | tf_op jit(solution)/shard_map/ppermute | solution.py:427
  84.1 53.4 %collective-permute-start.37 = (bf16[2,6,192,256]{3,2,1,0:T(8,128)(2,1)}, bf16[2,6,192,256]{3,2,1,0:T(8,128)(2,1)S(1)}, u32[]{:S(2)}, u32[]{:S(2)}) collective-permute-start(bf16[2,6,192,256]{3,2,1,0:T(8,128)(2,1)} %pad_maximum_fusion.8), channel_id=1, source_target_pairs={{0,16},{4,20},{8,24},{12,28},{16,0},{20,4},{24,8},{28,12},{1,17},{... | collective-permute-start | bytes 3538952 | tf_op jit(solution)/shard_map/ppermute | solution.py:427
  85.9 51.5 %collective-permute-start.38 = (bf16[2,6,192,256]{3,2,1,0:T(8,128)(2,1)}, bf16[2,6,192,256]{3,2,1,0:T(8,128)(2,1)}, u32[]{:S(2)}, u32[]{:S(2)}) collective-permute-start(bf16[2,6,192,256]{3,2,1,0:T(8,128)(2,1)} %pad_maximum_fusion.9), channel_id=1, source_target_pairs={{0,8},{4,12},{8,0},{12,4},{16,24},{20,28},{24,16},{28,20},{1,9},{5... | collective-permute-start | bytes 3538952 | tf_op jit(solution)/shard_map/ppermute | solution.py:427
  87.5 36.5 %collective-permute-start.4 = (bf16[64,4096]{1,0:T(8,128)(2,1)S(1)}, bf16[64,4096]{1,0:T(8,128)(2,1)S(1)}, u32[]{:S(2)}, u32[]{:S(2)}) collective-permute-start(bf16[64,4096]{1,0:T(8,128)(2,1)S(1)} %get-tuple-element.621), channel_id=1, source_target_pairs={{0,1},{1,2},{2,3},{3,0},{4,5},{5,6},{6,7},{7,4},{8,9},{9,10},{10,1... | collective-permute-start | bytes 1572872 | tf_op jit(solution)/shard_map/ppermute | solution.py:573
  89.2 44.3 %collective-permute-start.5 = (bf16[64,4096]{1,0:T(8,128)(2,1)S(1)}, bf16[64,4096]{1,0:T(8,128)(2,1)S(1)}, u32[]{:S(2)}, u32[]{:S(2)}) collective-permute-start(bf16[64,4096]{1,0:T(8,128)(2,1)S(1)} %get-tuple-element.620), channel_id=1, source_target_pairs={{0,2},{1,3},{2,0},{3,1},{4,6},{5,7},{6,4},{7,5},{8,10},{9,11},{10,... | collective-permute-start | bytes 1572872 | tf_op jit(solution)/shard_map/ppermute | solution.py:573
  142.0 263.4 %all-gather.9.cloned.1.call-start = ((), (), s32[]{:S(2)}) async-start(), calls=%async_computation.6 | async-start | bytes 3932160 | tf_op jit(solution)/shard_map/all_gather | solution.py:510
  162.3 52.5 %collective-permute-start.9 = (bf16[2,1,768,256]{3,2,1,0:T(8,128)(2,1)S(1)}, bf16[2,1,768,256]{3,2,1,0:T(8,128)(2,1)S(1)}, u32[]{:S(2)}, u32[]{:S(2)}) collective-permute-start(bf16[2,1,768,256]{3,2,1,0:T(8,128)(2,1)S(1)} %pad_maximum_fusion.32), channel_id=1, source_target_pairs={{0,8},{4,12},{8,0},{12,4},{16,24},{20,28},{24,16},{28,20},{1,9},{5... | collective-permute-start | bytes 2359304 | tf_op jit(solution)/shard_map/ppermute | solution.py:427
  188.6 43.2 %collective-permute-start.10 = (bf16[2,1,768,256]{3,2,1,0:T(8,128)(2,1)S(1)}, bf16[2,1,768,256]{3,2,1,0:T(8,128)(2,1)S(1)}, u32[]{:S(2)}, u32[]{:S(2)}) collective-permute-start(bf16[2,1,768,256]{3,2,1,0:T(8,128)(2,1)S(1)} %pad_maximum_fusion.33), channel_id=1, source_target_pairs={{0,16},{4,20},{8,24},{12,28},{16,0},{20,4},{24,8},{28,12},{1,17},{... | collective-permute-start | bytes 2359304 | tf_op jit(solution)/shard_map/ppermute | solution.py:427
  189.4 42.4 %collective-permute-start.11 = (bf16[2,1,768,256]{3,2,1,0:T(8,128)(2,1)S(1)}, bf16[2,1,768,256]{3,2,1,0:T(8,128)(2,1)S(1)}, u32[]{:S(2)}, u32[]{:S(2)}) collective-permute-start(bf16[2,1,768,256]{3,2,1,0:T(8,128)(2,1)S(1)} %pad_maximum_fusion.34), channel_id=1, source_target_pairs={{0,24},{4,28},{8,16},{12,20},{16,8},{20,12},{24,0},{28,4},{1,25},{... | collective-permute-start | bytes 2359304 | tf_op jit(solution)/shard_map/ppermute | solution.py:427
  284.9 327.8 %all-gather.11.cloned.1.call-start = ((), (), s32[]{:S(2)}) async-start(), calls=%async_computation.7 | async-start | bytes 11796480 | tf_op jit(solution)/shard_map/all_gather | solution.py:510
  310.5 34.9 %collective-permute-start.39 = (bf16[256,2048]{1,0:T(8,128)(2,1)S(1)}, bf16[256,2048]{1,0:T(8,128)(2,1)S(1)}, u32[]{:S(2)}, u32[]{:S(2)}) collective-permute-start(bf16[256,2048]{1,0:T(8,128)(2,1)S(1)} %multiply_convert_fusion.2.refs_0_.refs_3_), channel_id=1, source_target_pairs={{0,4},{4,0},{8,12},{12,8},{16,20},{20,16},{24,28},{28,24},{1,5},{5... | collective-permute-start | bytes 3145736 | tf_op jit(solution)/shard_map/ppermute | solution.py:427
  387.8 634.2 %reduce-scatter.5.cloned.1.call-start = ((), (), s32[]{:S(2)}) async-start(), calls=%async_computation.8 | async-start | bytes 11796480 | tf_op jit(solution)/shard_map/reduce_scatter | solution.py:514
  432.8 40.7 %collective-permute-start.54 = (bf16[2,1,768,256]{3,2,1,0:T(8,128)(2,1)S(1)}, bf16[2,1,768,256]{3,2,1,0:T(8,128)(2,1)S(1)}, u32[]{:S(2)}, u32[]{:S(2)}) collective-permute-start(bf16[2,1,768,256]{3,2,1,0:T(8,128)(2,1)S(1)} %pad_maximum_fusion.36), channel_id=1, source_target_pairs={{0,8},{4,12},{8,0},{12,4},{16,24},{20,28},{24,16},{28,20},{1,9},{5... | collective-permute-start | bytes 2359304 | tf_op jit(solution)/shard_map/ppermute | solution.py:427
  459.0 40.2 %collective-permute-start.55 = (bf16[2,1,768,256]{3,2,1,0:T(8,128)(2,1)S(1)}, bf16[2,1,768,256]{3,2,1,0:T(8,128)(2,1)S(1)}, u32[]{:S(2)}, u32[]{:S(2)}) collective-permute-start(bf16[2,1,768,256]{3,2,1,0:T(8,128)(2,1)S(1)} %pad_maximum_fusion.37), channel_id=1, source_target_pairs={{0,16},{4,20},{8,24},{12,28},{16,0},{20,4},{24,8},{28,12},{1,17},{... | collective-permute-start | bytes 2359304 | tf_op jit(solution)/shard_map/ppermute | solution.py:427
  460.1 39.1 %collective-permute-start.56 = (bf16[2,1,768,256]{3,2,1,0:T(8,128)(2,1)S(1)}, bf16[2,1,768,256]{3,2,1,0:T(8,128)(2,1)S(1)}, u32[]{:S(2)}, u32[]{:S(2)}) collective-permute-start(bf16[2,1,768,256]{3,2,1,0:T(8,128)(2,1)S(1)} %pad_maximum_fusion.38), channel_id=1, source_target_pairs={{0,24},{4,28},{8,16},{12,20},{16,8},{20,12},{24,0},{28,4},{1,25},{... | collective-permute-start | bytes 2359304 | tf_op jit(solution)/shard_map/ppermute | solution.py:427
  746.6 557.8 %reduce-scatter.9.cloned.1.call-start = ((), (), s32[]{:S(2)}) async-start(), calls=%async_computation.10 | async-start | bytes 3932160 | tf_op jit(solution)/shard_map/reduce_scatter | solution.py:514
  747.6 38.2 %collective-permute-start.99 = (bf16[256,2048]{1,0:T(8,128)(2,1)}, bf16[256,2048]{1,0:T(8,128)(2,1)S(1)}, u32[]{:S(2)}, u32[]{:S(2)}) collective-permute-start(bf16[256,2048]{1,0:T(8,128)(2,1)} %copy-done.173), channel_id=1, source_target_pairs={{0,4},{4,0},{8,12},{12,8},{16,20},{20,16},{24,28},{28,24},{1,5},{5... | collective-permute-start | bytes 3145736 | tf_op jit(solution)/shard_map/ppermute | solution.py:427
  748.1 37.8 %collective-permute-start.100 = (bf16[256,2048]{1,0:T(8,128)(2,1)}, bf16[256,2048]{1,0:T(8,128)(2,1)S(1)}, u32[]{:S(2)}, u32[]{:S(2)}) collective-permute-start(bf16[256,2048]{1,0:T(8,128)(2,1)} %copy-done.172), channel_id=1, source_target_pairs={{0,4},{4,0},{8,12},{12,8},{16,20},{20,16},{24,28},{28,24},{1,5},{5... | collective-permute-start | bytes 3145736 | tf_op jit(solution)/shard_map/ppermute | solution.py:427
  796.4 37.1 %collective-permute-start.106 = (bf16[256,2048]{1,0:T(8,128)(2,1)S(1)}, bf16[256,2048]{1,0:T(8,128)(2,1)S(1)}, u32[]{:S(2)}, u32[]{:S(2)}) collective-permute-start(bf16[256,2048]{1,0:T(8,128)(2,1)S(1)} %pad_maximum_fusion.23), channel_id=1, source_target_pairs={{0,16},{4,20},{8,24},{12,28},{16,0},{20,4},{24,8},{28,12},{1,17},{... | collective-permute-start | bytes 3145736 | tf_op jit(solution)/shard_map/ppermute | solution.py:427
  797.8 35.6 %collective-permute-start.105 = (bf16[256,2048]{1,0:T(8,128)(2,1)S(1)}, bf16[256,2048]{1,0:T(8,128)(2,1)S(1)}, u32[]{:S(2)}, u32[]{:S(2)}) collective-permute-start(bf16[256,2048]{1,0:T(8,128)(2,1)S(1)} %pad_maximum_fusion.22), channel_id=1, source_target_pairs={{0,8},{4,12},{8,0},{12,4},{16,24},{20,28},{24,16},{28,20},{1,9},{5... | collective-permute-start | bytes 3145736 | tf_op jit(solution)/shard_map/ppermute | solution.py:427
  984.4 35.3 %collective-permute-start.141 = (bf16[2,1,768,256]{3,2,1,0:T(8,128)(2,1)S(1)}, bf16[2,1,768,256]{3,2,1,0:T(8,128)(2,1)S(1)}, u32[]{:S(2)}, u32[]{:S(2)}) collective-permute-start(bf16[2,1,768,256]{3,2,1,0:T(8,128)(2,1)S(1)} %pad_maximum_fusion.40), channel_id=1, source_target_pairs={{0,16},{4,20},{8,24},{12,28},{16,0},{20,4},{24,8},{28,12},{1,17},{... | collective-permute-start | bytes 2359304 | tf_op jit(solution)/shard_map/ppermute | solution.py:427
  1022.1 282.4 %reduce-scatter.7.cloned.1.call-start = ((), (), s32[]{:S(2)}) async-start(), calls=%async_computation.9 | async-start | bytes 11796480 | tf_op jit(solution)/shard_map/reduce_scatter | solution.py:514
  1054.8 320.1 %reduce-scatter.11.cloned.1.call-start = ((), (), s32[]{:S(2)}) async-start(), calls=%async_computation.11 | async-start | bytes 3932160 | tf_op jit(solution)/shard_map/reduce_scatter | solution.py:514
  1203.0 35.1 %collective-permute-start.168 = (bf16[2,1,768,256]{3,2,1,0:T(8,128)(2,1)S(1)}, bf16[2,1,768,256]{3,2,1,0:T(8,128)(2,1)S(1)}, u32[]{:S(2)}, u32[]{:S(2)}) collective-permute-start(bf16[2,1,768,256]{3,2,1,0:T(8,128)(2,1)S(1)} %pad_maximum_fusion.43), channel_id=1, source_target_pairs={{0,16},{4,20},{8,24},{12,28},{16,0},{20,4},{24,8},{28,12},{1,17},{... | collective-permute-start | bytes 2359304 | tf_op jit(solution)/shard_map/ppermute | solution.py:427
  1204.5 34.7 %collective-permute-start.169 = (bf16[2,1,768,256]{3,2,1,0:T(8,128)(2,1)S(1)}, bf16[2,1,768,256]{3,2,1,0:T(8,128)(2,1)S(1)}, u32[]{:S(2)}, u32[]{:S(2)}) collective-permute-start(bf16[2,1,768,256]{3,2,1,0:T(8,128)(2,1)S(1)} %pad_maximum_fusion.44), channel_id=1, source_target_pairs={{0,24},{4,28},{8,16},{12,20},{16,8},{20,12},{24,0},{28,4},{1,25},{... | collective-permute-start | bytes 2359304 | tf_op jit(solution)/shard_map/ppermute | solution.py:427
  1243.2 37.1 %collective-permute-start.172 = (bf16[64,4096]{1,0:T(8,128)(2,1)S(1)}, bf16[64,4096]{1,0:T(8,128)(2,1)S(1)}, u32[]{:S(2)}, u32[]{:S(2)}) collective-permute-start(bf16[64,4096]{1,0:T(8,128)(2,1)S(1)} %get-tuple-element.617), channel_id=1, source_target_pairs={{0,1},{1,2},{2,3},{3,0},{4,5},{5,6},{6,7},{7,4},{8,9},{9,10},{10,1... | collective-permute-start | bytes 1572872 | tf_op jit(solution)/shard_map/ppermute | solution.py:573
  1245.5 44.6 %collective-permute-start.173 = (bf16[64,4096]{1,0:T(8,128)(2,1)S(1)}, bf16[64,4096]{1,0:T(8,128)(2,1)S(1)}, u32[]{:S(2)}, u32[]{:S(2)}) collective-permute-start(bf16[64,4096]{1,0:T(8,128)(2,1)S(1)} %get-tuple-element.616), channel_id=1, source_target_pairs={{0,2},{1,3},{2,0},{3,1},{4,6},{5,7},{6,4},{7,5},{8,10},{9,11},{10,... | collective-permute-start | bytes 1572872 | tf_op jit(solution)/shard_map/ppermute | solution.py:573
  1247.0 44.3 %collective-permute-start.174 = (bf16[64,4096]{1,0:T(8,128)(2,1)S(1)}, bf16[64,4096]{1,0:T(8,128)(2,1)S(1)}, u32[]{:S(2)}, u32[]{:S(2)}) collective-permute-start(bf16[64,4096]{1,0:T(8,128)(2,1)S(1)} %get-tuple-element.615), channel_id=1, source_target_pairs={{0,3},{1,0},{2,1},{3,2},{4,7},{5,4},{6,5},{7,6},{8,11},{9,8},{10,9... | collective-permute-start | bytes 1572872 | tf_op jit(solution)/shard_map/ppermute | solution.py:573
  1319.2 44.0 %collective-permute-start.184 = (bf16[2,3,192,256]{3,2,1,0:T(8,128)(2,1)}, bf16[2,3,192,256]{3,2,1,0:T(8,128)(2,1)}, u32[]{:S(2)}, u32[]{:S(2)}) collective-permute-start(bf16[2,3,192,256]{3,2,1,0:T(8,128)(2,1)} %pad_maximum_fusion.49), channel_id=1, source_target_pairs={{0,16},{4,20},{8,24},{12,28},{16,0},{20,4},{24,8},{28,12},{1,17},{... | collective-permute-start | bytes 1769480 | tf_op jit(solution)/shard_map/ppermute | solution.py:427
  1326.5 36.8 %collective-permute-start.185 = (bf16[2,3,192,256]{3,2,1,0:T(8,128)(2,1)}, bf16[2,3,192,256]{3,2,1,0:T(8,128)(2,1)}, u32[]{:S(2)}, u32[]{:S(2)}) collective-permute-start(bf16[2,3,192,256]{3,2,1,0:T(8,128)(2,1)} %pad_maximum_fusion.50), channel_id=1, source_target_pairs={{0,24},{4,28},{8,16},{12,20},{16,8},{20,12},{24,0},{28,4},{1,25},{... | collective-permute-start | bytes 1769480 | tf_op jit(solution)/shard_map/ppermute | solution.py:427
  (406 other events, 5124.0 us)
Sparse Core Ops, SparseCore 0:
  25.6 62.3 all-gather.4
  142.1 162.8 all-gather.6
  306.6 62.3 all-gather.8
  387.9 163.8 all-gather.10
  746.7 160.9 reduce-scatter.4
  1022.2 59.7 reduce-scatter.8
  1084.4 163.1 reduce-scatter.6
  1304.6 60.6 reduce-scatter.10

commit v4 on v3

--- a/solution.py
+++ b/solution.py
@@ -1249,6 +1249,7 @@
     both = line_rows_back(both, below)
     gain_stack = sum_plane(gain_stack)
     hidden_grads[0] = swap(hidden_sums[0], 2, 1, below)
+    both, hidden_grads[0] = lax.optimization_barrier((both, hidden_grads[0]))
     both = swap(both, 0, 0)
     result, token_grad = both[:, : tokens.shape[1]], wide(both[:, tokens.shape[1] :])
     kinds = wide(jnp.stack(hidden_grads, 1))

time: 1400 us -> 1450 us (1.036)
  waiting for transfers between devices: 665 us -> 700 us
    ppermute x6, waiting for transfers between devices: 88.4 us -> 123 us  [line_swap(): moved.append(lax.ppermute(piece, 'tp', pairs))]
    unnamed x492 -> x504, local copies, waits for them, and re-layouts: 60.7 us -> 69.9 us
  transfers between devices with their start and end apart: 194 -> 194, of which waited for: 100 -> 92; matrix products, arithmetic and copies ran while one was open for 10% -> 10% of each run, Pallas kernels for 23% -> 22%
where the time goes in v4:
time: 1450 us; the launch traced here: 1440 us
  waiting for transfers between devices  700 us (48%)
  Pallas kernels  329 us (23%)
  local copies, waits for them, and re-layouts  134 us (9%)
  starting transfers between devices  132 us (9%)
  other arithmetic  92.4 us (6%)
  between operations  49.1 us (3%)
    ppermute x178, waiting for transfers between devices, plane_send(): lax.ppermute(values, 'fsdp', [(i, i ^ distance) for i in range(size)])  572 us
    ppermute x6, waiting for transfers between devices, line_swap(): moved.append(lax.ppermute(piece, 'tp', pairs))  123 us
    ppermute x178, starting transfers between devices, plane_send(): lax.ppermute(values, 'fsdp', [(i, i ^ distance) for i in range(size)])  120 us
    pallas_call x24, Pallas kernels, parts_of(): pl.pallas_call(functools.partial(parts_kernel, len(ds), len(terms), adds...  87.8 us
    pallas_call x4, Pallas kernels, outer(): pl.pallas_call(functools.partial(outer_kernel, plan), grid=(shape[-1] //...  79.6 us
    unnamed x504, local copies, waits for them, and re-layouts  69.9 us
    pallas_call x6, Pallas kernels, hidden_units(): pl.pallas_call(functools.partial(units_kernel, len(pieces)), grid=(weight...  39.3 us
    pallas_call x2, Pallas kernels, plane_attend_back(): pl.pallas_call(functools.partial(attend_back_kernel, groups, heads, rows)...  39.1 us
  transfers between devices with their start and end apart: 194, of which 92 were waited for; matrix products, arithmetic and copies ran while one was open for 10% of the time, Pallas kernels for 22%

profile of v4, /device:TPU:8, one launch (start us, length us, event | category | flops | bytes accessed | tf_op | source)
XLA Modules:
  0.0 1436.2 jit_solution(3420760349571155232)
XLA Ops:
  90.4 33.7 %collective-permute-done.4.refs_1_ = bf16[64,4096]{1,0:T(8,128)(2,1)S(1)} collective-permute-done((bf16[64,4096]{1,0:T(8,128)(2,1)S(1)}, bf16[64,4096]{1,0:T(8,128)(2,1)S(1)}, u32[]{:S(2)}, u32[]{:S(2)}) %collective-permute-start.4) | collective-permute-done | bytes 524320 | tf_op jit(solution)/shard_map/ppermute | solution.py:573
  163.1 23.1 %collective-permute-done.12.refs_0_.refs_5_ = bf16[256,2048]{1,0:T(8,128)(2,1)S(1)} collective-permute-done((bf16[256,2048]{1,0:T(8,128)(2,1)S(1)}, bf16[256,2048]{1,0:T(8,128)(2,1)S(1)}, u32[]{:S(2)}, u32[]{:S(2)}) %collective-permute-start.12) | collective-permute-done | bytes 1048608 | tf_op jit(solution)/shard_map/ppermute | solution.py:427
  191.0 23.3 %collective-permute-done.16.refs_0_.refs_9_ = bf16[128,2048]{1,0:T(8,128)(2,1)S(1)} collective-permute-done((bf16[128,2048]{1,0:T(8,128)(2,1)S(1)}, bf16[128,2048]{1,0:T(8,128)(2,1)S(1)}, u32[]{:S(2)}, u32[]{:S(2)}) %collective-permute-start.16) | collective-permute-done | bytes 524320 | tf_op jit(solution)/shard_map/ppermute | solution.py:427
  215.0 16.7 %collective-permute-done.10.refs_3_ = bf16[2,1,768,256]{3,2,1,0:T(8,128)(2,1)S(1)} collective-permute-done((bf16[2,1,768,256]{3,2,1,0:T(8,128)(2,1)S(1)}, bf16[2,1,768,256]{3,2,1,0:T(8,128)(2,1)S(1)}, u32[]{:S(2)}, u32[]{:S(2)}) %collective-permute-start.10) | collective-permute-done | bytes 786464 | tf_op jit(solution)/shard_map/ppermute | solution.py:427
  244.9 11.7 attend.2
  285.1 17.9 %collective-permute-done.30 = bf16[256,2048]{1,0:T(8,128)(2,1)} collective-permute-done((bf16[256,2048]{1,0:T(8,128)(2,1)S(1)}, bf16[256,2048]{1,0:T(8,128)(2,1)}, u32[]{:S(2)}, u32[]{:S(2)}) %collective-permute-start.30) | collective-permute-done | bytes 1048608 | tf_op jit(solution)/shard_map/ppermute | solution.py:427
  310.6 20.9 %collective-permute-done.31.refs_0_.refs_5_ = bf16[256,2048]{1,0:T(8,128)(2,1)S(1)} collective-permute-done((bf16[256,2048]{1,0:T(8,128)(2,1)S(1)}, bf16[256,2048]{1,0:T(8,128)(2,1)S(1)}, u32[]{:S(2)}, u32[]{:S(2)}) %collective-permute-start.31) | collective-permute-done | bytes 1048608 | tf_op jit(solution)/shard_map/ppermute | solution.py:427
  407.8 19.7 %collective-permute-done.51 = bf16[256,2048]{1,0:T(8,128)(2,1)S(1)} collective-permute-done((bf16[256,2048]{1,0:T(8,128)(2,1)S(1)}, bf16[256,2048]{1,0:T(8,128)(2,1)S(1)}, u32[]{:S(2)}, u32[]{:S(2)}) %collective-permute-start.51) | collective-permute-done | bytes 1048608 | tf_op jit(solution)/shard_map/ppermute | solution.py:427
  433.9 22.8 %collective-permute-done.57.refs_0_.refs_5_ = bf16[256,2048]{1,0:T(8,128)(2,1)S(1)} collective-permute-done((bf16[256,2048]{1,0:T(8,128)(2,1)S(1)}, bf16[256,2048]{1,0:T(8,128)(2,1)S(1)}, u32[]{:S(2)}, u32[]{:S(2)}) %collective-permute-start.57) | collective-permute-done | bytes 1048608 | tf_op jit(solution)/shard_map/ppermute | solution.py:427
  461.7 11.8 collective-permute-done.54.refs_2_
  473.5 11.2 collective-permute-done.61.refs_0_.refs_9_
  485.3 14.0 collective-permute-done.55.refs_3_
  507.5 12.1 attend.3
  543.3 21.9 %collective-permute-done.72 = bf16[256,2048]{1,0:T(8,128)(2,1)S(1)} collective-permute-done((bf16[256,2048]{1,0:T(8,128)(2,1)S(1)}, bf16[256,2048]{1,0:T(8,128)(2,1)S(1)}, u32[]{:S(2)}, u32[]{:S(2)}) %collective-permute-start.72) | collective-permute-done | bytes 1048608 | tf_op jit(solution)/shard_map/ppermute | solution.py:427
  569.2 21.0 %collective-permute-done.73.refs_0_.refs_5_ = bf16[256,2048]{1,0:T(8,128)(2,1)} collective-permute-done((bf16[256,2048]{1,0:T(8,128)(2,1)S(1)}, bf16[256,2048]{1,0:T(8,128)(2,1)}, u32[]{:S(2)}, u32[]{:S(2)}) %collective-permute-start.73) | collective-permute-done | bytes 1048608 | tf_op jit(solution)/shard_map/ppermute | solution.py:427
  700.9 27.4 %outer.4 = bf16[3,768,2048]{2,1,0:T(8,128)(2,1)} custom-call(bf16[512,768]{1,0:T(8,128)(2,1)} %copy-done.69, bf16[1024,768]{1,0:T(8,128)(2,1)} %copy-done.13, bf16[512,768]{1,0:T(8,128)(2,1)} %copy-done.63, bf16[256,2048]{1,0:T(8,128)(2,1)} %copy-done.53, bf16[256,2048]{1,0:T(8,128)(2,1)} %copy-done.114, ...), custom_call_target="tpu_custom_call" | custom-call | flops 9663676416 | bytes 1024 | tf_op jit(solution)/shard_map/outer/pallas_call | solution.py:1057
  746.2 23.0 %collective-permute-done.107.refs_0_.refs_18_ = bf16[256,2048]{1,0:T(8,128)(2,1)S(1)} collective-permute-done((bf16[256,2048]{1,0:T(8,128)(2,1)S(1)}, bf16[256,2048]{1,0:T(8,128)(2,1)S(1)}, u32[]{:S(2)}, u32[]{:S(2)}) %collective-permute-start.107) | collective-permute-done | bytes 1048608 | tf_op jit(solution)/shard_map/ppermute | solution.py:427
  810.0 19.4 %attend_back.2 = (bf16[2,2,4,32,512]{4,3,2,1,0:T(8,128)(2,1)S(1)}, bf16[4,2,4,32,512]{4,3,2,1,0:T(8,128)(2,1)S(1)}, bf16[2,2,4,32,512]{4,3,2,1,0:T(8,128)(2,1)S(1)}, f32[2,2,128]{2,1,0:T(2,128)S(1)}) custom-call(s32[1]{0:T(128)} %bitcast.29.refs_0_, f32[2,2,4,32,512]{4,3,2,1,0:T(8,128)S(1)} %bitcast.370, f32[4,2,4,32,512]{4,3,2,1,0:T(8,128)S(1)} %bitcast.364, ...), custom_call_target="tpu_custom_call" | custom-call | flops 4294967296 | bytes 1024 | tf_op jit(solution)/shard_map/attend_back/pallas_call | solution.py:832
  858.3 12.7 outer.5
  894.1 19.9 %collective-permute-done.124.refs_0_.refs_21_ = bf16[256,2048]{1,0:T(8,128)(2,1)S(1)} collective-permute-done((bf16[256,2048]{1,0:T(8,128)(2,1)S(1)}, bf16[256,2048]{1,0:T(8,128)(2,1)S(1)}, u32[]{:S(2)}, u32[]{:S(2)}) %collective-permute-start.124) | collective-permute-done | bytes 1048608 | tf_op jit(solution)/shard_map/ppermute | solution.py:427
  985.8 14.3 collective-permute-done.140.refs_2_
  1000.1 16.0 %collective-permute-done.141.refs_3_ = bf16[2,1,768,256]{3,2,1,0:T(8,128)(2,1)S(1)} collective-permute-done((bf16[2,1,768,256]{3,2,1,0:T(8,128)(2,1)S(1)}, bf16[2,1,768,256]{3,2,1,0:T(8,128)(2,1)S(1)}, u32[]{:S(2)}, u32[]{:S(2)}) %collective-permute-start.141) | collective-permute-done | bytes 786464 | tf_op jit(solution)/shard_map/ppermute | solution.py:427
  1020.3 26.9 %outer.6 = bf16[3,768,2048]{2,1,0:T(8,128)(2,1)} custom-call(bf16[512,768]{1,0:T(8,128)(2,1)} %copy-done.65, bf16[1024,768]{1,0:T(8,128)(2,1)} %copy-done.10, bf16[512,768]{1,0:T(8,128)(2,1)} %copy-done.60, bf16[256,2048]{1,0:T(8,128)(2,1)} %copy-done.52, bf16[256,2048]{1,0:T(8,128)(2,1)} %copy-done.109, bf16[256,2048]{1,0:T(8,128)(2,1)} %copy-done.82, ...), custom_call_target="tpu_custom_call" | custom-call | flops 9663676416 | bytes 1024 | tf_op jit(solution)/shard_map/outer/pallas_call | solution.py:1057
  1062.3 21.9 %collective-permute-done.145.refs_0_.refs_18_ = bf16[256,2048]{1,0:T(8,128)(2,1)S(1)} collective-permute-done((bf16[256,2048]{1,0:T(8,128)(2,1)S(1)}, bf16[256,2048]{1,0:T(8,128)(2,1)S(1)}, u32[]{:S(2)}, u32[]{:S(2)}) %collective-permute-start.145) | collective-permute-done | bytes 1048608 | tf_op jit(solution)/shard_map/ppermute | solution.py:427
  1116.6 19.8 %attend_back.3 = (bf16[2,2,4,32,512]{4,3,2,1,0:T(8,128)(2,1)S(1)}, bf16[4,2,4,32,512]{4,3,2,1,0:T(8,128)(2,1)S(1)}, bf16[2,2,4,32,512]{4,3,2,1,0:T(8,128)(2,1)S(1)}, f32[2,2,128]{2,1,0:T(2,128)S(1)}) custom-call(s32[1]{0:T(128)} %bitcast.29.refs_0_, f32[2,2,4,32,512]{4,3,2,1,0:T(8,128)S(1)} %bitcast.366, f32[4,2,4,32,512]{4,3,2,1,0:T(8,128)S(1)} %bitcast.362, ...), custom_call_target="tpu_custom_call" | custom-call | flops 4294967296 | bytes 1024 | tf_op jit(solution)/shard_map/attend_back/pallas_call | solution.py:832
  1169.6 12.6 outer.7
  1211.6 13.1 collective-permute-done.167.refs_2_
  1224.7 18.0 %collective-permute-done.168.refs_3_ = bf16[2,1,768,256]{3,2,1,0:T(8,128)(2,1)S(1)} collective-permute-done((bf16[2,1,768,256]{3,2,1,0:T(8,128)(2,1)}, bf16[2,1,768,256]{3,2,1,0:T(8,128)(2,1)S(1)}, u32[]{:S(2)}, u32[]{:S(2)}) %collective-permute-start.168) | collective-permute-done | bytes 786464 | tf_op jit(solution)/shard_map/ppermute | solution.py:427
  1268.4 23.9 %collective-permute-done.185 = f32[68,128]{1,0:T(8,128)S(1)} collective-permute-done((f32[68,128]{1,0:T(8,128)S(1)}, f32[68,128]{1,0:T(8,128)S(1)}, u32[]{:S(2)}, u32[]{:S(2)}) %collective-permute-start.185) | collective-permute-done | bytes 34848 | tf_op jit(solution)/shard_map/ppermute | solution.py:427
  1298.2 60.6 %collective-permute-done.173.refs_2_ = bf16[64,4096]{1,0:T(8,128)(2,1)} collective-permute-done((bf16[64,4096]{1,0:T(8,128)(2,1)}, bf16[64,4096]{1,0:T(8,128)(2,1)}, u32[]{:S(2)}, u32[]{:S(2)}) %collective-permute-start.173) | collective-permute-done | bytes 524320 | tf_op jit(solution)/shard_map/ppermute | solution.py:573
  1358.8 17.9 %collective-permute-done.174.refs_3_ = bf16[64,4096]{1,0:T(8,128)(2,1)} collective-permute-done((bf16[64,4096]{1,0:T(8,128)(2,1)}, bf16[64,4096]{1,0:T(8,128)(2,1)}, u32[]{:S(2)}, u32[]{:S(2)}) %collective-permute-start.174) | collective-permute-done | bytes 524320 | tf_op jit(solution)/shard_map/ppermute | solution.py:573
  1408.3 11.9 collective-permute-done.181.refs_3_
  (1177 shorter events, 745.9 us)
Async XLA Ops:
  7.2 130.2 %all-gather.5.cloned.1.call-start = ((), (), s32[]{:S(2)}) async-start(), calls=%async_computation.4 | async-start | bytes 3932160 | tf_op jit(solution)/shard_map/all_gather | solution.py:510
  25.5 321.0 %all-gather.7.cloned.1.call-start = ((), (), s32[]{:S(2)}) async-start(), calls=%async_computation.5 | async-start | bytes 11796480 | tf_op jit(solution)/shard_map/all_gather | solution.py:510
  81.6 55.8 %collective-permute-start.36 = (bf16[2,6,192,256]{3,2,1,0:T(8,128)(2,1)}, bf16[2,6,192,256]{3,2,1,0:T(8,128)(2,1)S(1)}, u32[]{:S(2)}, u32[]{:S(2)}) collective-permute-start(bf16[2,6,192,256]{3,2,1,0:T(8,128)(2,1)} %pad_maximum_fusion.7), channel_id=1, source_target_pairs={{0,24},{4,28},{8,16},{12,20},{16,8},{20,12},{24,0},{28,4},{1,25},{... | collective-permute-start | bytes 3538952 | tf_op jit(solution)/shard_map/ppermute | solution.py:427
  84.0 53.4 %collective-permute-start.37 = (bf16[2,6,192,256]{3,2,1,0:T(8,128)(2,1)}, bf16[2,6,192,256]{3,2,1,0:T(8,128)(2,1)S(1)}, u32[]{:S(2)}, u32[]{:S(2)}) collective-permute-start(bf16[2,6,192,256]{3,2,1,0:T(8,128)(2,1)} %pad_maximum_fusion.8), channel_id=1, source_target_pairs={{0,16},{4,20},{8,24},{12,28},{16,0},{20,4},{24,8},{28,12},{1,17},{... | collective-permute-start | bytes 3538952 | tf_op jit(solution)/shard_map/ppermute | solution.py:427
  85.9 51.5 %collective-permute-start.38 = (bf16[2,6,192,256]{3,2,1,0:T(8,128)(2,1)}, bf16[2,6,192,256]{3,2,1,0:T(8,128)(2,1)}, u32[]{:S(2)}, u32[]{:S(2)}) collective-permute-start(bf16[2,6,192,256]{3,2,1,0:T(8,128)(2,1)} %pad_maximum_fusion.9), channel_id=1, source_target_pairs={{0,8},{4,12},{8,0},{12,4},{16,24},{20,28},{24,16},{28,20},{1,9},{5... | collective-permute-start | bytes 3538952 | tf_op jit(solution)/shard_map/ppermute | solution.py:427
  87.5 36.5 %collective-permute-start.4 = (bf16[64,4096]{1,0:T(8,128)(2,1)S(1)}, bf16[64,4096]{1,0:T(8,128)(2,1)S(1)}, u32[]{:S(2)}, u32[]{:S(2)}) collective-permute-start(bf16[64,4096]{1,0:T(8,128)(2,1)S(1)} %get-tuple-element.625), channel_id=1, source_target_pairs={{0,1},{1,2},{2,3},{3,0},{4,5},{5,6},{6,7},{7,4},{8,9},{9,10},{10,1... | collective-permute-start | bytes 1572872 | tf_op jit(solution)/shard_map/ppermute | solution.py:573
  89.2 44.3 %collective-permute-start.5 = (bf16[64,4096]{1,0:T(8,128)(2,1)S(1)}, bf16[64,4096]{1,0:T(8,128)(2,1)S(1)}, u32[]{:S(2)}, u32[]{:S(2)}) collective-permute-start(bf16[64,4096]{1,0:T(8,128)(2,1)S(1)} %get-tuple-element.624), channel_id=1, source_target_pairs={{0,2},{1,3},{2,0},{3,1},{4,6},{5,7},{6,4},{7,5},{8,10},{9,11},{10,... | collective-permute-start | bytes 1572872 | tf_op jit(solution)/shard_map/ppermute | solution.py:573
  142.0 263.5 %all-gather.9.cloned.1.call-start = ((), (), s32[]{:S(2)}) async-start(), calls=%async_computation.6 | async-start | bytes 3932160 | tf_op jit(solution)/shard_map/all_gather | solution.py:510
  162.3 52.5 %collective-permute-start.9 = (bf16[2,1,768,256]{3,2,1,0:T(8,128)(2,1)S(1)}, bf16[2,1,768,256]{3,2,1,0:T(8,128)(2,1)S(1)}, u32[]{:S(2)}, u32[]{:S(2)}) collective-permute-start(bf16[2,1,768,256]{3,2,1,0:T(8,128)(2,1)S(1)} %pad_maximum_fusion.32), channel_id=1, source_target_pairs={{0,8},{4,12},{8,0},{12,4},{16,24},{20,28},{24,16},{28,20},{1,9},{5... | collective-permute-start | bytes 2359304 | tf_op jit(solution)/shard_map/ppermute | solution.py:427
  188.6 43.2 %collective-permute-start.10 = (bf16[2,1,768,256]{3,2,1,0:T(8,128)(2,1)S(1)}, bf16[2,1,768,256]{3,2,1,0:T(8,128)(2,1)S(1)}, u32[]{:S(2)}, u32[]{:S(2)}) collective-permute-start(bf16[2,1,768,256]{3,2,1,0:T(8,128)(2,1)S(1)} %pad_maximum_fusion.33), channel_id=1, source_target_pairs={{0,16},{4,20},{8,24},{12,28},{16,0},{20,4},{24,8},{28,12},{1,17},{... | collective-permute-start | bytes 2359304 | tf_op jit(solution)/shard_map/ppermute | solution.py:427
  189.4 42.4 %collective-permute-start.11 = (bf16[2,1,768,256]{3,2,1,0:T(8,128)(2,1)S(1)}, bf16[2,1,768,256]{3,2,1,0:T(8,128)(2,1)S(1)}, u32[]{:S(2)}, u32[]{:S(2)}) collective-permute-start(bf16[2,1,768,256]{3,2,1,0:T(8,128)(2,1)S(1)} %pad_maximum_fusion.34), channel_id=1, source_target_pairs={{0,24},{4,28},{8,16},{12,20},{16,8},{20,12},{24,0},{28,4},{1,25},{... | collective-permute-start | bytes 2359304 | tf_op jit(solution)/shard_map/ppermute | solution.py:427
  284.9 327.9 %all-gather.11.cloned.1.call-start = ((), (), s32[]{:S(2)}) async-start(), calls=%async_computation.7 | async-start | bytes 11796480 | tf_op jit(solution)/shard_map/all_gather | solution.py:510
  310.6 34.9 %collective-permute-start.39 = (bf16[256,2048]{1,0:T(8,128)(2,1)S(1)}, bf16[256,2048]{1,0:T(8,128)(2,1)S(1)}, u32[]{:S(2)}, u32[]{:S(2)}) collective-permute-start(bf16[256,2048]{1,0:T(8,128)(2,1)S(1)} %multiply_convert_fusion.2.refs_0_.refs_3_), channel_id=1, source_target_pairs={{0,4},{4,0},{8,12},{12,8},{16,20},{20,16},{24,28},{28,24},{1,5},{5... | collective-permute-start | bytes 3145736 | tf_op jit(solution)/shard_map/ppermute | solution.py:427
  387.9 719.6 %reduce-scatter.5.cloned.1.call-start = ((), (), s32[]{:S(2)}) async-start(), calls=%async_computation.8 | async-start | bytes 11796480 | tf_op jit(solution)/shard_map/reduce_scatter | solution.py:514
  432.8 40.7 %collective-permute-start.54 = (bf16[2,1,768,256]{3,2,1,0:T(8,128)(2,1)S(1)}, bf16[2,1,768,256]{3,2,1,0:T(8,128)(2,1)S(1)}, u32[]{:S(2)}, u32[]{:S(2)}) collective-permute-start(bf16[2,1,768,256]{3,2,1,0:T(8,128)(2,1)S(1)} %pad_maximum_fusion.36), channel_id=1, source_target_pairs={{0,8},{4,12},{8,0},{12,4},{16,24},{20,28},{24,16},{28,20},{1,9},{5... | collective-permute-start | bytes 2359304 | tf_op jit(solution)/shard_map/ppermute | solution.py:427
  459.0 40.3 %collective-permute-start.55 = (bf16[2,1,768,256]{3,2,1,0:T(8,128)(2,1)S(1)}, bf16[2,1,768,256]{3,2,1,0:T(8,128)(2,1)S(1)}, u32[]{:S(2)}, u32[]{:S(2)}) collective-permute-start(bf16[2,1,768,256]{3,2,1,0:T(8,128)(2,1)S(1)} %pad_maximum_fusion.37), channel_id=1, source_target_pairs={{0,16},{4,20},{8,24},{12,28},{16,0},{20,4},{24,8},{28,12},{1,17},{... | collective-permute-start | bytes 2359304 | tf_op jit(solution)/shard_map/ppermute | solution.py:427
  460.2 39.1 %collective-permute-start.56 = (bf16[2,1,768,256]{3,2,1,0:T(8,128)(2,1)S(1)}, bf16[2,1,768,256]{3,2,1,0:T(8,128)(2,1)S(1)}, u32[]{:S(2)}, u32[]{:S(2)}) collective-permute-start(bf16[2,1,768,256]{3,2,1,0:T(8,128)(2,1)S(1)} %pad_maximum_fusion.38), channel_id=1, source_target_pairs={{0,24},{4,28},{8,16},{12,20},{16,8},{20,12},{24,0},{28,4},{1,25},{... | collective-permute-start | bytes 2359304 | tf_op jit(solution)/shard_map/ppermute | solution.py:427
  775.3 469.8 %reduce-scatter.7.cloned.1.call-start = ((), (), s32[]{:S(2)}) async-start(), calls=%async_computation.9 | async-start | bytes 11796480 | tf_op jit(solution)/shard_map/reduce_scatter | solution.py:514
  795.3 34.1 %collective-permute-start.106 = (bf16[256,2048]{1,0:T(8,128)(2,1)S(1)}, bf16[256,2048]{1,0:T(8,128)(2,1)S(1)}, u32[]{:S(2)}, u32[]{:S(2)}) collective-permute-start(bf16[256,2048]{1,0:T(8,128)(2,1)S(1)} %pad_maximum_fusion.23), channel_id=1, source_target_pairs={{0,16},{4,20},{8,24},{12,28},{16,0},{20,4},{24,8},{28,12},{1,17},{... | collective-permute-start | bytes 3145736 | tf_op jit(solution)/shard_map/ppermute | solution.py:427
  980.8 35.3 %collective-permute-start.141 = (bf16[2,1,768,256]{3,2,1,0:T(8,128)(2,1)S(1)}, bf16[2,1,768,256]{3,2,1,0:T(8,128)(2,1)S(1)}, u32[]{:S(2)}, u32[]{:S(2)}) collective-permute-start(bf16[2,1,768,256]{3,2,1,0:T(8,128)(2,1)S(1)} %pad_maximum_fusion.40), channel_id=1, source_target_pairs={{0,16},{4,20},{8,24},{12,28},{16,0},{20,4},{24,8},{28,12},{1,17},{... | collective-permute-start | bytes 2359304 | tf_op jit(solution)/shard_map/ppermute | solution.py:427
  981.9 34.2 %collective-permute-start.142 = (bf16[2,1,768,256]{3,2,1,0:T(8,128)(2,1)S(1)}, bf16[2,1,768,256]{3,2,1,0:T(8,128)(2,1)S(1)}, u32[]{:S(2)}, u32[]{:S(2)}) collective-permute-start(bf16[2,1,768,256]{3,2,1,0:T(8,128)(2,1)S(1)} %pad_maximum_fusion.41), channel_id=1, source_target_pairs={{0,24},{4,28},{8,16},{12,20},{16,8},{20,12},{24,0},{28,4},{1,25},{... | collective-permute-start | bytes 2359304 | tf_op jit(solution)/shard_map/ppermute | solution.py:427
  1050.4 247.2 %reduce-scatter.9.cloned.1.call-start = ((), (), s32[]{:S(2)}) async-start(), calls=%async_computation.10 | async-start | bytes 3932160 | tf_op jit(solution)/shard_map/reduce_scatter | solution.py:514
  1169.5 253.3 %reduce-scatter.11.cloned.1.call-start = ((), (), s32[]{:S(2)}) async-start(), calls=%async_computation.11 | async-start | bytes 3932160 | tf_op jit(solution)/shard_map/reduce_scatter | solution.py:514
  1206.2 36.6 %collective-permute-start.168 = (bf16[2,1,768,256]{3,2,1,0:T(8,128)(2,1)}, bf16[2,1,768,256]{3,2,1,0:T(8,128)(2,1)S(1)}, u32[]{:S(2)}, u32[]{:S(2)}) collective-permute-start(bf16[2,1,768,256]{3,2,1,0:T(8,128)(2,1)} %pad_maximum_fusion.43), channel_id=1, source_target_pairs={{0,16},{4,20},{8,24},{12,28},{16,0},{20,4},{24,8},{28,12},{1,17},{... | collective-permute-start | bytes 2359304 | tf_op jit(solution)/shard_map/ppermute | solution.py:427
  1208.1 34.6 %collective-permute-start.169 = (bf16[2,1,768,256]{3,2,1,0:T(8,128)(2,1)}, bf16[2,1,768,256]{3,2,1,0:T(8,128)(2,1)S(1)}, u32[]{:S(2)}, u32[]{:S(2)}) collective-permute-start(bf16[2,1,768,256]{3,2,1,0:T(8,128)(2,1)} %pad_maximum_fusion.44), channel_id=1, source_target_pairs={{0,24},{4,28},{8,16},{12,20},{16,8},{20,12},{24,0},{28,4},{1,25},{... | collective-permute-start | bytes 2359304 | tf_op jit(solution)/shard_map/ppermute | solution.py:427
  1210.3 39.4 %collective-permute-start.170 = (f32[68,128]{1,0:T(8,128)}, f32[68,128]{1,0:T(8,128)}, u32[]{:S(2)}, u32[]{:S(2)}) collective-permute-start(f32[68,128]{1,0:T(8,128)} %reshape.380), channel_id=1, source_target_pairs={{0,1},{1,0},{2,3},{3,2},{4,5},{5,4},{6,7},{7,6},{8,9},{9,8},{10,11... | collective-permute-start | bytes 104456 | tf_op jit(solution)/shard_map/ppermute | solution.py:492
  1260.5 35.9 %collective-permute-start.172 = (bf16[64,4096]{1,0:T(8,128)(2,1)S(1)}, bf16[64,4096]{1,0:T(8,128)(2,1)S(1)}, u32[]{:S(2)}, u32[]{:S(2)}) collective-permute-start(bf16[64,4096]{1,0:T(8,128)(2,1)S(1)} %get-tuple-element.621), channel_id=1, source_target_pairs={{0,1},{1,2},{2,3},{3,0},{4,5},{5,6},{6,7},{7,4},{8,9},{9,10},{10,1... | collective-permute-start | bytes 1572872 | tf_op jit(solution)/shard_map/ppermute | solution.py:573
  1262.1 116.0 %collective-permute-start.176 = (bf16[2,3,192,256]{3,2,1,0:T(8,128)(2,1)}, bf16[2,3,192,256]{3,2,1,0:T(8,128)(2,1)S(1)}, u32[]{:S(2)}, u32[]{:S(2)}) collective-permute-start(bf16[2,3,192,256]{3,2,1,0:T(8,128)(2,1)} %pad_maximum_fusion.48), channel_id=1, source_target_pairs={{0,8},{4,12},{8,0},{12,4},{16,24},{20,28},{24,16},{28,20},{1,9},{5... | collective-permute-start | bytes 1769480 | tf_op jit(solution)/shard_map/ppermute | solution.py:427
  1264.1 114.0 %collective-permute-start.177 = (bf16[2,3,192,256]{3,2,1,0:T(8,128)(2,1)}, bf16[2,3,192,256]{3,2,1,0:T(8,128)(2,1)S(1)}, u32[]{:S(2)}, u32[]{:S(2)}) collective-permute-start(bf16[2,3,192,256]{3,2,1,0:T(8,128)(2,1)} %pad_maximum_fusion.49), channel_id=1, source_target_pairs={{0,16},{4,20},{8,24},{12,28},{16,0},{20,4},{24,8},{28,12},{1,17},{... | collective-permute-start | bytes 1769480 | tf_op jit(solution)/shard_map/ppermute | solution.py:427
  1265.7 112.4 %collective-permute-start.178 = (bf16[2,3,192,256]{3,2,1,0:T(8,128)(2,1)}, bf16[2,3,192,256]{3,2,1,0:T(8,128)(2,1)S(1)}, u32[]{:S(2)}, u32[]{:S(2)}) collective-permute-start(bf16[2,3,192,256]{3,2,1,0:T(8,128)(2,1)} %pad_maximum_fusion.50), channel_id=1, source_target_pairs={{0,24},{4,28},{8,16},{12,20},{16,8},{20,12},{24,0},{28,4},{1,25},{... | collective-permute-start | bytes 1769480 | tf_op jit(solution)/shard_map/ppermute | solution.py:427
  1292.4 66.4 %collective-permute-start.173 = (bf16[64,4096]{1,0:T(8,128)(2,1)}, bf16[64,4096]{1,0:T(8,128)(2,1)}, u32[]{:S(2)}, u32[]{:S(2)}) collective-permute-start(bf16[64,4096]{1,0:T(8,128)(2,1)} %get-tuple-element.620), channel_id=1, source_target_pairs={{0,2},{1,3},{2,0},{3,1},{4,6},{5,7},{6,4},{7,5},{8,10},{9,11},{10,... | collective-permute-start | bytes 1572872 | tf_op jit(solution)/shard_map/ppermute | solution.py:573
  1296.4 80.3 %collective-permute-start.174 = (bf16[64,4096]{1,0:T(8,128)(2,1)}, bf16[64,4096]{1,0:T(8,128)(2,1)}, u32[]{:S(2)}, u32[]{:S(2)}) collective-permute-start(bf16[64,4096]{1,0:T(8,128)(2,1)} %get-tuple-element.619), channel_id=1, source_target_pairs={{0,3},{1,0},{2,1},{3,2},{4,7},{5,4},{6,5},{7,6},{8,11},{9,8},{10,9... | collective-permute-start | bytes 1572872 | tf_op jit(solution)/shard_map/ppermute | solution.py:573
  (412 other events, 5297.8 us)
Sparse Core Ops, SparseCore 0:
  25.6 62.3 all-gather.4
  142.1 162.8 all-gather.6
  306.6 62.3 all-gather.8
  388.0 163.8 all-gather.10
  775.5 161.1 reduce-scatter.4
  1050.5 161.2 reduce-scatter.6
  1214.7 72.1 reduce-scatter.8
  1297.7 83.2 reduce-scatter.10
